TPU v7x, 32 devices: a whole 2x2x4 slice. The times are simulated.
32 devices in a mesh: groups: 2 (over y), node: 4 (over z), local: 2 (over x), sub: 2 (over core).
Axes of the slice: x: 2, y: 2, z: 4, core: 2. Of those that a mesh axis runs over, the one named last changes fastest.
Arguments:
- tokens: bfloat16 [256, 3584], P(('groups', 'node', 'local', 'sub')), parts along dimension 0, may hold values from -6 to 6
- ids: int32 [256, 8], P(('groups', 'node', 'local', 'sub')), parts along dimension 0, may hold values from 0 to 7, as said below
- scores: float32 [256, 8], P(('groups', 'node', 'local', 'sub')), parts along dimension 0, may hold values from -6 to 6
- gate_w: bfloat16 [8, 3584, 2048], P('node', None, ('local', 'sub')), may hold values from -0.09375 to 0.09375
- up_w: bfloat16 [8, 3584, 2048], P('node', None, ('local', 'sub')), may hold values from -0.09375 to 0.09375
- down_w: bfloat16 [8, 2048, 3584], P('node', None, ('local', 'sub')), may hold values from -0.125 to 0.125
Outputs:
- combined: bfloat16 [256, 3584], P(('groups', 'node', 'local', 'sub')), parts along dimension 0
There are 2 independent parts, one for each index of `groups`. A program takes and returns all parts, laid end to end along the dimension named above; an argument that names none is the same for every part. Nothing has to cross between parts.
Inputs may be any that keep to these rules, and one draw needn't show every extreme that they name: `ids`: each token names 8 different experts. Of the 8 tokens of one device (an aligned block of rows), at most 8 name any one expert, and in every draw one expert is named by exactly 8 tokens of every device.
All inputs are finite; a program needn't handle non-finite values.
Results may differ from a plain program's by a relative error of at most 0.0058.
Values may be sent and summed in bfloat16 or wider, within the bound.
No kernel may reach another device: no remote copies, remote signals or barrier semaphores. Data moves between devices by JAX's collectives and lax.ppermute only.
A program may use at most 192 MiB of HBM per device.

v0:
```python
import jax
import jax.numpy as jnp
from jax import lax
from jax.sharding import PartitionSpec as P

route_scale = 2.827


def per_device(tokens, ids, scores, gate_w, up_w, down_w):
    tok_rows, features = tokens.shape
    top_count = ids.shape[1]
    local_experts = gate_w.shape[0]
    node_count = lax.axis_size("node")
    experts = local_experts * node_count
    capacity = max(2, min(tok_rows, 2 * tok_rows * top_count // experts))
    flat_experts = ids.reshape(-1)
    one_hot = (flat_experts[:, None] == jnp.arange(experts, dtype=jnp.int32)[None, :]).astype(
        jnp.int32
    )
    before = jnp.cumsum(one_hot, axis=0) - one_hot
    slot_rank = jnp.sum(before * one_hot, axis=1)
    where_to = flat_experts * capacity + slot_rank
    matches = (
        jnp.arange(experts * capacity, dtype=jnp.int32)[:, None] == where_to[None, :]
    ).astype(jnp.int32)
    source = (
        jnp.sum(matches * (jnp.arange(flat_experts.shape[0], dtype=jnp.int32)[None, :] + 1), axis=1)
        - 1
    )
    filled = jnp.take(tokens, jnp.maximum(source, 0) // top_count, axis=0)
    packed = jnp.where((source >= 0)[:, None], filled, jnp.zeros_like(filled))
    packed = packed.reshape(node_count, local_experts, capacity, features)
    arrived = lax.all_to_all(packed, "node", split_axis=0, concat_axis=0, tiled=True)
    block_part = lax.all_gather(arrived[None], ("local", "sub"), axis=0, tiled=True)
    gate_part = jnp.einsum(
        "anecd,edf->anecf", block_part, gate_w, preferred_element_type=jnp.float32
    )
    up_part = jnp.einsum("anecd,edf->anecf", block_part, up_w, preferred_element_type=jnp.float32)
    hidden = (jax.nn.silu(gate_part) * up_part).astype(jnp.bfloat16)
    outcome = jnp.einsum(
        "anecf,efd->anecd",
        lax.all_gather(hidden, ("local", "sub"), axis=4, tiled=True),
        down_w,
        preferred_element_type=jnp.float32,
    ).astype(jnp.bfloat16)
    returned_rows = lax.all_to_all(
        outcome, ("local", "sub"), split_axis=0, concat_axis=4, tiled=True
    )[0]
    returned = lax.all_to_all(returned_rows, "node", split_axis=0, concat_axis=0, tiled=True)
    flat_back = returned.reshape(experts * capacity, features)
    picked = (
        jnp.take(flat_back, where_to, axis=0)
        .astype(jnp.float32)
        .reshape(tok_rows, top_count, features)
    )
    sigmoid_vals = jax.nn.sigmoid(scores)
    share = route_scale * sigmoid_vals / jnp.sum(sigmoid_vals, axis=1, keepdims=True)
    return jnp.sum(share[:, :, None] * picked, axis=1).astype(jnp.bfloat16)


def solution(mesh):
    placed = (
        P(("groups", "node", "local", "sub"), None),
        P(("groups", "node", "local", "sub"), None),
        P(("groups", "node", "local", "sub"), None),
        P("node", None, ("local", "sub")),
        P("node", None, ("local", "sub")),
        P("node", None, ("local", "sub")),
    )
    return jax.shard_map(
        per_device,
        mesh=mesh,
        in_specs=placed,
        out_specs=P(("groups", "node", "local", "sub"), None),
        check_vma=False,
    )
```

profile of v0, /device:TPU:0, one launch (start us, length us, event | category | flops | bytes accessed | tf_op | source)
XLA Modules:
  0.0 118.3 jit_solution(7804761677815629796)
XLA Ops:
  6.5 0.0 copy-start
  6.5 0.0 all-gather.6.cloned.1.call-start
  6.5 0.8 reshape.157
  7.3 0.1 fusion.24
  7.4 0.1 reduce_window_sum.11
  7.5 0.2 select_reduce_fusion.1
  7.7 0.1 select_reduce_fusion
  7.9 0.1 reshape.159
  7.9 0.1 div.32
  8.0 0.1 ge.32
  8.1 0.0 copy-done
  8.2 0.8 gather_fusion
  9.0 0.1 select_select_fusion
  9.1 19.3 %all_to_all.25 = bf16[4,2,8,3584]{3,2,1,0:T(8,128)(2,1)} all-to-all(bf16[4,2,8,3584]{3,2,1,0:T(8,128)(2,1)S(1)} %select_select_fusion), channel_id=1, replica_groups=mesh['groups'=2,'node'=4,'local'=2,'sub'=2] {'node'}, dimensions={0} | all-to-all | bytes 917504 | tf_op jit(solution)/shard_map/all_to_all | solution.py:33
  28.4 0.0 all-gather.6.cloned.1.call-update
  28.5 0.0 all-gather.4.cloned.1.call-start
  28.5 20.3 %all-gather.6.cloned.1.call-done = bf16[16,2,8,3584]{3,2,1,0:T(8,128)(2,1)} async-done(((bf16[4,2,8,3584]{3,2,1,0:T(8,128)(2,1)}), bf16[16,2,8,3584]{3,2,1,0:T(8,128)(2,1)}) %all-gather.6.cloned.1.call-update) | async-done | bytes 1835024 | tf_op jit(solution)/shard_map/all_gather | solution.py:34
  48.8 0.0 slice-start
  48.8 1.8 %copy.20 = bf16[16,2,8,3584]{3,2,0,1:T(8,128)(2,1)S(1)} copy(bf16[16,2,8,3584]{3,2,1,0:T(8,128)(2,1)} %all-gather.6.cloned.1.call-done) | data formatting | bytes 3670016 | tf_op jit(solution)/shard_map/all_gather | solution.py:34
  50.6 0.0 slice-start.1
  50.6 4.4 %fusion.9 = f32[4,4,2,8,512]{4,3,1,0,2:T(8,128)S(1)} fusion(bf16[4,4,2,8,3584]{4,3,1,0,2:T(8,128)(2,1)S(1)} %bitcast.68, bf16[2,3584,512]{2,1,0:T(8,128)(2,1)} %param.9), kind=kOutput, calls=%fused_computation.9 | convolution fusion | flops 939524096 | bytes 9699328 | tf_op jit(solution)/shard_map/anecd,edf->anecf/dot_general | solution.py:35
  55.0 0.0 slice-done
  55.0 0.0 slice-done.1
  55.0 1.9 %fusion.21 = bf16[4,4,2,8,512]{4,3,1,0,2:T(8,128)(2,1)} fusion(bf16[4,4,2,8,3584]{4,3,1,0,2:T(8,128)(2,1)S(1)} %bitcast.69, bf16[2,3584,512]{2,1,0:T(8,128)(2,1)S(1)} %bitcast.74, f32[4,4,2,8,512]{4,3,1,0,2:T(8,128)S(1)} %fusion.9), kind=kOutput, calls=%fused_computation.13 | convolution fusion | flops 940310528 | bytes 9961472 | tf_op jit(solution)/shard_map/anecd,edf->anecf/dot_general | solution.py:38
  56.9 0.0 all-gather.4.cloned.1.call-update
  56.9 0.0 copy-start.1
  56.9 0.0 copy-start.2
  56.9 16.9 %all-gather.4.cloned.1.call-done = bf16[4,4,2,8,2048]{4,3,1,0,2:T(8,128)(2,1)} async-done(((bf16[4,4,2,8,512]{4,3,1,0,2:T(8,128)(2,1)}), bf16[4,4,2,8,2048]{4,3,1,0,2:T(8,128)(2,1)}) %all-gather.4.cloned.1.call-update) | async-done | bytes 1048592 | tf_op jit(solution)/shard_map/all_gather | solution.py:42
  73.8 4.7 %fusion.18 = bf16[4,4,2,8,896]{4,3,1,0,2:T(8,128)(2,1)S(1)} fusion(bf16[4,4,2,8,2048]{4,3,1,0,2:T(8,128)(2,1)} %all-gather.4.cloned.1.call-done, bf16[2,2048,896]{2,1,0:T(8,128)(2,1)} %param.11), kind=kOutput, calls=%fused_computation.12 | convolution fusion | flops 939753472 | bytes 8847360 | tf_op jit(solution)/shard_map/anecf,efd->anecd/dot_general | solution.py:40
  78.5 0.8 copy.21
  79.3 3.5 %all-to-all-start.1 = ((bf16[4,4,2,8,896]{4,3,1,2,0:T(8,128)(2,1)}), bf16[4,4,2,8,896]{4,3,1,2,0:T(8,128)(2,1)S(1)}, u32[]{:S(2)}, u32[]{:S(2)}) async-start(bf16[4,4,2,8,896]{4,3,1,2,0:T(8,128)(2,1)} %copy.21), calls=%async_computation.1 | async-start | bytes 917504 | tf_op jit(solution)/shard_map/all_to_all | solution.py:46
  82.7 0.0 copy-done.1
  82.8 0.1 mul.77
  82.8 8.0 %all-to-all-done.1 = bf16[4,4,2,8,896]{4,3,1,2,0:T(8,128)(2,1)S(1)} async-done(((bf16[4,4,2,8,896]{4,3,1,2,0:T(8,128)(2,1)}), bf16[4,4,2,8,896]{4,3,1,2,0:T(8,128)(2,1)S(1)}, u32[]{:S(2)}, u32[]{:S(2)}) %all-to-all-start.1) | async-done | bytes 458784 | tf_op jit(solution)/shard_map/all_to_all | solution.py:46
  90.9 0.4 copy.22
  91.2 0.9 squeeze.3
  92.2 4.6 %all-to-all-start.2 = ((bf16[4,2,8,3584]{3,2,1,0:T(8,128)(2,1)}), bf16[4,2,8,3584]{3,2,1,0:T(8,128)(2,1)S(1)}, u32[]{:S(2)}, u32[]{:S(2)}) async-start(bf16[4,2,8,3584]{3,2,1,0:T(8,128)(2,1)} %squeeze.3), calls=%async_computation.2 | async-start | bytes 917504 | tf_op jit(solution)/shard_map/all_to_all | solution.py:49
  96.8 0.1 reduce_sum.42
  96.8 0.0 copy-done.2
  96.9 0.1 fusion.25
  97.0 0.1 multiply_divide_fusion
  97.1 12.6 %all-to-all-done.2 = bf16[4,2,8,3584]{3,2,1,0:T(8,128)(2,1)S(1)} async-done(((bf16[4,2,8,3584]{3,2,1,0:T(8,128)(2,1)}), bf16[4,2,8,3584]{3,2,1,0:T(8,128)(2,1)S(1)}, u32[]{:S(2)}, u32[]{:S(2)}) %all-to-all-start.2) | async-done | bytes 458784 | tf_op jit(solution)/shard_map/all_to_all | solution.py:49
  109.6 0.8 gather_fusion.1
  110.5 1.0 multiply_reduce_fusion
  (11 shorter events, 0.1 us)
Async XLA Ops:
  6.5 1.6 %copy-start = (bf16[8,3584]{1,0:T(8,128)(2,1)S(1)}, bf16[8,3584]{1,0:T(8,128)(2,1)}, u32[]{:S(2)}) copy-start(bf16[8,3584]{1,0:T(8,128)(2,1)} %param.6) | copy-start | bytes 172036
  6.5 42.3 %all-gather.6.cloned.1.call-start = ((), (), s32[]{:S(2)}) async-start(), calls=%async_computation.4 | async-start | bytes 2293760 | tf_op jit(solution)/shard_map/all_gather | solution.py:34
  28.5 45.3 %all-gather.4.cloned.1.call-start = ((), (), s32[]{:S(2)}) async-start(), calls=%async_computation.3 | async-start | bytes 1310720 | tf_op jit(solution)/shard_map/all_gather | solution.py:42
  48.8 6.1 %slice-start = ((s8[7340032]{0:T(1024)(128)(4,1)}), s8[4194304]{0:T(1024)(128)(4,1)S(1)}, s32[]{:S(2)}) async-start(s8[7340032]{0:T(1024)(128)(4,1)} %bitcast.73), calls=%async_computation.5 | async-start | bytes 8388608
  50.6 4.4 %slice-start.1 = ((s8[7340032]{0:T(1024)(128)(4,1)}), s8[3145728]{0:T(1024)(128)(4,1)S(1)}, s32[]{:S(2)}) async-start(s8[7340032]{0:T(1024)(128)(4,1)} %bitcast.73), calls=%async_computation.6 | async-start | bytes 6291456
  56.9 25.8 %copy-start.1 = (s32[8,8]{1,0:T(8,128)S(1)}, s32[8,8]{1,0:T(8,128)}, u32[]{:S(2)}) copy-start(s32[8,8]{1,0:T(8,128)} %param.7) | copy-start | bytes 772
  56.9 39.9 %copy-start.2 = (f32[8,8]{1,0:T(8,128)S(1)}, f32[8,8]{1,0:T(8,128)}, u32[]{:S(2)}) copy-start(f32[8,8]{1,0:T(8,128)} %param.8) | copy-start | bytes 772
  79.3 11.6 %all-to-all-start.1 = ((bf16[4,4,2,8,896]{4,3,1,2,0:T(8,128)(2,1)}), bf16[4,4,2,8,896]{4,3,1,2,0:T(8,128)(2,1)S(1)}, u32[]{:S(2)}, u32[]{:S(2)}) async-start(bf16[4,4,2,8,896]{4,3,1,2,0:T(8,128)(2,1)} %copy.21), calls=%async_computation.1 | async-start | bytes 917504 | tf_op jit(solution)/shard_map/all_to_all | solution.py:46
  92.2 17.5 %all-to-all-start.2 = ((bf16[4,2,8,3584]{3,2,1,0:T(8,128)(2,1)}), bf16[4,2,8,3584]{3,2,1,0:T(8,128)(2,1)S(1)}, u32[]{:S(2)}, u32[]{:S(2)}) async-start(bf16[4,2,8,3584]{3,2,1,0:T(8,128)(2,1)} %squeeze.3), calls=%async_computation.2 | async-start | bytes 917504 | tf_op jit(solution)/shard_map/all_to_all | solution.py:49
Sparse Core Ops, SparseCore 0:
  28.6 20.2 all-gather.5
  57.0 16.7 all-gather.3
where the time goes:
time: 119 us; the launch traced here: 118 us
  waiting for transfers between devices  57.8 us (49%)
  blocking collectives  19.3 us (16%)
  between operations  13.6 us (11%)
  matrix products  10.9 us (9%)
  starting transfers between devices  8.11 us (7%)
  local copies, waits for them, and re-layouts  6.73 us (6%)
  other arithmetic  1.86 us (2%)
    all_gather x1, waiting for transfers between devices, per_device(): lax.all_gather(arrived[None], ('local', 'sub'), axis=0, tiled=True)  20.3 us
    all_to_all x1, blocking collectives, per_device(): lax.all_to_all(packed, 'node', split_axis=0, concat_axis=0, tiled=True)  19.3 us
    all_gather x1, waiting for transfers between devices, per_device(): lax.all_gather(hidden, ('local', 'sub'), axis=4, tiled=True)  16.9 us
    all_to_all x1, waiting for transfers between devices, per_device(): lax.all_to_all(returned_rows, 'node', split_axis=0, concat_axis=0, tiled=...  12.6 us
    all_to_all x1, waiting for transfers between devices, per_device(): lax.all_to_all(outcome, ('local', 'sub'), split_axis=0, concat_axis=4, ti...  8.01 us
    dot_general x1, matrix products, per_device(): jnp.einsum('anecf,efd->anecd', lax.all_gather(hidden, ('local', 'sub'), a...  4.68 us
    all_to_all x1, starting transfers between devices, per_device(): lax.all_to_all(returned_rows, 'node', split_axis=0, concat_axis=0, tiled=...  4.6 us
    dot_general x1, matrix products, per_device(): jnp.einsum('anecd,edf->anecf', block_part, gate_w, preferred_element_type...  4.35 us
  transfers between devices with their start and end apart: 4, of which 4 were waited for; matrix products, arithmetic and copies ran while one was open for 0% of the time, Pallas kernels for 0%

commit v1 on v0

v1 whole, which is shorter than its diff:
```python
import functools

import jax
import jax.numpy as jnp
from jax import lax
from jax.experimental import pallas as pl
from jax.experimental.pallas import tpu as pltpu
from jax.sharding import PartitionSpec as P

route_scale = 2.827
LANES = 128
f32, bf16 = jnp.float32, jnp.bfloat16
VMEM = pl.BlockSpec(memory_space=pltpu.VMEM)


def swap(x, axis, k):
    return lax.ppermute(x, axis, [(i, i ^ k) for i in range(lax.axis_size(axis))])


def call(kernel, out_shape, n_in, flops=0, size=0, vmem=16):
    return pl.pallas_call(
        kernel,
        out_shape=out_shape,
        in_specs=[VMEM] * n_in,
        out_specs=jax.tree.map(lambda _: VMEM, out_shape),
        compiler_params=pltpu.CompilerParams(vmem_limit_bytes=vmem << 20),
        cost_estimate=pl.CostEstimate(flops=flops, bytes_accessed=size, transcendentals=0),
    )


def pack_kernel(experts, tok_ref, ids_ref, scores_ref, out_ref):
    rows, features = tok_ref.shape
    extra = out_ref.shape[1] - features
    out_ref[:, :features] = tok_ref[...]
    gate = 1.0 / (1.0 + jnp.exp(-scores_ref[...]))
    share = route_scale * gate / jnp.sum(gate, axis=1, keepdims=True)
    column = lax.broadcasted_iota(jnp.int32, (rows, extra), 1)
    expert, term = column % experts, column // experts
    weight = jnp.zeros((rows, extra), f32)
    for k in range(ids_ref.shape[1]):
        weight += jnp.where(ids_ref[:, k : k + 1] == expert, share[:, k : k + 1], 0.0)
    first = weight.astype(bf16).astype(f32)
    second = (weight - first).astype(bf16).astype(f32)
    third = weight - first - second
    terms = jnp.where(term == 0, first, jnp.where(term == 1, second, jnp.where(term == 2, third, 0.0)))
    out_ref[:, features:] = terms.astype(bf16)


def hidden_kernel(e, experts, features, *refs):
    *blocks, gate_ref, up_ref, out_ref = refs
    local_experts = gate_ref.shape[0]
    x = jnp.concatenate([b[:, :features] for b in blocks], axis=0)
    tail = jnp.concatenate([b[:, features:] for b in blocks], axis=0).astype(f32)
    column = lax.broadcasted_iota(jnp.int32, tail.shape, 1)
    mine = lax.axis_index("node") * local_experts + e
    keep = (column % experts == mine) & (column < 3 * experts)
    weight = jnp.sum(jnp.where(keep, tail, 0.0), axis=1, keepdims=True)
    gate = jnp.dot(x, gate_ref[e], preferred_element_type=f32)
    up = jnp.dot(x, up_ref[e], preferred_element_type=f32)
    out_ref[...] = (gate / (1.0 + jnp.exp(-gate)) * up * weight).astype(bf16)


def down_kernel(local, sub, nodes, local_experts, *refs):
    n_slices = local * sub
    hidden, (down_ref, *outs) = refs[: local_experts * n_slices], refs[local_experts * n_slices :]
    tokens, depth = hidden[0].shape
    block = tokens // n_slices
    me = lax.axis_index("local") * sub + lax.axis_index("sub")
    total = jnp.zeros((tokens, down_ref.shape[2]), f32)
    for r in range(n_slices):
        s, x = divmod(r, local)
        rows = pl.ds(pl.multiple_of((me ^ (x * sub + s)) * depth, depth), depth)
        for e in range(local_experts):
            ref = hidden[e * n_slices + r]
            h = jnp.concatenate(
                [ref[pl.ds((b ^ r) * block, block), :] for b in range(n_slices)], axis=0
            )
            total += jnp.dot(h, down_ref[e, rows, :], preferred_element_type=f32)
    rows = block // nodes
    for z in range(nodes):
        outs[z][...] = jnp.concatenate(
            [total[b * block + z * rows : b * block + (z + 1) * rows] for b in range(n_slices)],
            axis=0,
        ).astype(bf16)


def add_kernel(*refs):
    *parts, out_ref = refs
    total = parts[0][...].astype(f32)
    for part in parts[1:]:
        total += part[...].astype(f32)
    out_ref[...] = total.astype(bf16)


def place_kernel(local, sub, *refs):
    *pieces, out_ref = refs
    me = lax.axis_index("local") * sub + lax.axis_index("sub")
    width = pieces[0].shape[1]
    for r, piece in enumerate(pieces):
        s, x = divmod(r, local)
        at = pl.multiple_of((me ^ (x * sub + s)) * width, LANES)
        out_ref[:, pl.ds(at, width)] = piece[...]


def per_device(tokens, ids, scores, gate_w, up_w, down_w):
    nodes, local, sub = (lax.axis_size(a) for a in ("node", "local", "sub"))
    rows, features = tokens.shape
    local_experts, _, depth = gate_w.shape
    width = down_w.shape[2]
    experts = local_experts * nodes
    n_slices = local * sub
    extra = -(-3 * experts // LANES) * LANES
    block = nodes * rows
    count = n_slices * block

    packed = call(
        functools.partial(pack_kernel, experts),
        jax.ShapeDtypeStruct((rows, features + extra), bf16),
        3,
    )(tokens, ids, scores)
    own = jnp.concatenate([packed] + [swap(packed, "node", z) for z in range(1, nodes)], axis=0)
    blocks = [own] + [swap(own, "local", x) for x in range(1, local)]
    for s in range(1, sub):
        blocks += [swap(b, "sub", s) for b in blocks[:local]]

    hidden = []
    for e in range(local_experts):
        h = call(
            functools.partial(hidden_kernel, e, experts, features),
            jax.ShapeDtypeStruct((count, depth), bf16),
            n_slices + 2,
            flops=4 * count * features * depth,
            size=4 * features * depth,
            vmem=32 if count > 256 else 16,
        )(*blocks, gate_w, up_w)
        parts = [h] + [swap(h, "local", x) for x in range(1, local)]
        for s in range(1, sub):
            parts += [swap(p, "sub", s) for p in parts[:local]]
        hidden += parts

    outs = call(
        functools.partial(down_kernel, local, sub, nodes, local_experts),
        [jax.ShapeDtypeStruct((n_slices * rows, width), bf16)] * nodes,
        len(hidden) + 1,
        flops=2 * count * local_experts * n_slices * depth * width,
        size=2 * local_experts * n_slices * depth * width,
        vmem=32 if count > 256 else 16,
    )(*hidden, down_w)
    arrived = [outs[0]] + [swap(outs[z], "node", z) for z in range(1, nodes)]
    mine = call(
        add_kernel, jax.ShapeDtypeStruct((n_slices * rows, width), bf16), nodes
    )(*arrived)
    pieces = []
    for r in range(n_slices):
        s, x = divmod(r, local)
        piece = mine[r * rows : (r + 1) * rows]
        if r:
            pair = x * sub + s
            piece = lax.ppermute(
                piece, ("local", "sub"), [(i, i ^ pair) for i in range(n_slices)]
            )
        pieces.append(piece)
    if width % LANES == 0:
        return call(
            functools.partial(place_kernel, local, sub),
            jax.ShapeDtypeStruct((rows, features), bf16),
            n_slices,
        )(*pieces)
    me = lax.axis_index("local") * sub + lax.axis_index("sub")
    out = jnp.zeros((rows, features), bf16)
    for r, piece in enumerate(pieces):
        s, x = divmod(r, local)
        out = lax.dynamic_update_slice(out, piece, (0, (me ^ (x * sub + s)) * width))
    return out


def solution(mesh):
    everything = P(("groups", "node", "local", "sub"), None)
    weights = P("node", None, ("local", "sub"))
    return jax.shard_map(
        per_device,
        mesh=mesh,
        in_specs=(everything,) * 3 + (weights,) * 3,
        out_specs=everything,
        check_vma=False,
    )
```

time: 119 us -> 54.8 us (0.46)
  waiting for transfers between devices: 57.8 us -> 24.9 us
  blocking collectives: 19.3 us -> 0 us
  between operations: 13.6 us -> 0.1 us
  matrix products: 10.9 us -> 0 us
  starting transfers between devices: 8.11 us -> 16.7 us
  Pallas kernels: 0 us -> 4.36 us
  other arithmetic: 1.86 us -> 0.03 us
  local copies, waits for them, and re-layouts: 6.73 us -> 8.38 us
    all_gather x2 -> x0, waiting for transfers between devices: 37.2 us -> none  [the longest x1 20.3 us: per_device(): lax.all_gather(arrived[None], ('local', 'sub'), axis=0, tiled=True)]
    ppermute x0 -> x18, waiting for transfers between devices: none -> 24.9 us  [the longest x15 21.7 us: swap(): lax.ppermute(x, axis, [(i, i ^ k) for i in range(lax.axis_size(axis))])]
    all_to_all x2 -> x0, waiting for transfers between devices: 20.6 us -> none  [the longest x1 12.6 us: per_device(): lax.all_to_all(returned_rows, 'node', split_axis=0, concat_axis=0, tiled=...]
    all_to_all x1 -> x0, blocking collectives: 19.3 us -> none  [per_device(): lax.all_to_all(packed, 'node', split_axis=0, concat_axis=0, tiled=True)]
    ppermute x0 -> x18, starting transfers between devices: none -> 16.7 us  [the longest x15 14.5 us: swap(): lax.ppermute(x, axis, [(i, i ^ k) for i in range(lax.axis_size(axis))])]
    dot_general x3 -> x0, matrix products: 10.9 us -> none  [the longest x1 4.68 us: per_device(): jnp.einsum('anecf,efd->anecd', lax.all_gather(hidden, ('local', 'sub'), a...]
    unnamed x10 -> x14, local copies, waits for them, and re-layouts: 0.03 us -> 8.37 us
    all_to_all x2 -> x0, starting transfers between devices: 8.06 us -> none  [the longest x1 4.6 us: per_device(): lax.all_to_all(returned_rows, 'node', split_axis=0, concat_axis=0, tiled=...]
  transfers between devices with their start and end apart: 4 -> 18, of which waited for: 4 -> 12; matrix products, arithmetic and copies ran while one was open for 0% -> 0% of each run, Pallas kernels for 0% -> 2%
where the time goes in v1:
time: 54.8 us; the launch traced here: 54.5 us
  waiting for transfers between devices  24.9 us (45%)
  starting transfers between devices  16.7 us (30%)
  local copies, waits for them, and re-layouts  8.38 us (15%)
  Pallas kernels  4.36 us (8%)
    ppermute x15, waiting for transfers between devices, swap(): lax.ppermute(x, axis, [(i, i ^ k) for i in range(lax.axis_size(axis))])  21.7 us
    ppermute x15, starting transfers between devices, swap(): lax.ppermute(x, axis, [(i, i ^ k) for i in range(lax.axis_size(axis))])  14.5 us
    unnamed x14, local copies, waits for them, and re-layouts  8.37 us
    ppermute x3, waiting for transfers between devices, per_device(): lax.ppermute(piece, ('local', 'sub'), [(i, i ^ pair) for i in range(n_sli...  3.18 us
    pallas_call x2, Pallas kernels, per_device(): call(functools.partial(hidden_kernel, e, experts, features), jax.ShapeDty...  2.24 us
    ppermute x3, starting transfers between devices, per_device(): lax.ppermute(piece, ('local', 'sub'), [(i, i ^ pair) for i in range(n_sli...  2.2 us
    pallas_call x1, Pallas kernels, per_device(): call(functools.partial(down_kernel, local, sub, nodes, local_experts), [j...  1.27 us
  transfers between devices with their start and end apart: 18, of which 12 were waited for; matrix products, arithmetic and copies ran while one was open for 0% of the time, Pallas kernels for 2%

profile of v1, /device:TPU:0, one launch (start us, length us, event | category | flops | bytes accessed | tf_op | source)
XLA Modules:
  0.0 54.5 jit_solution(8222233160648137226)
XLA Ops:
  0.0 0.0 copy-start.2
  0.0 0.8 %copy-done.2 = bf16[8,3584]{1,0:T(8,128)(2,1)S(1)} copy-done((bf16[8,3584]{1,0:T(8,128)(2,1)S(1)}, bf16[8,3584]{1,0:T(8,128)(2,1)}, u32[]{:S(2)}) %copy-start.2) | copy-done | bytes 57368
  0.8 0.0 copy-start.3
  0.8 0.7 %copy-done.3 = s32[8,8]{1,0:T(8,128)S(1)} copy-done((s32[8,8]{1,0:T(8,128)S(1)}, s32[8,8]{1,0:T(8,128)}, u32[]{:S(2)}) %copy-start.3) | copy-done | bytes 280
  1.5 0.0 copy-start.4
  1.5 0.7 %copy-done.4 = f32[8,8]{1,0:T(8,128)S(1)} copy-done((f32[8,8]{1,0:T(8,128)S(1)}, f32[8,8]{1,0:T(8,128)}, u32[]{:S(2)}) %copy-start.4) | copy-done | bytes 280
  2.2 0.2 shard_map.64
  2.4 5.1 %collective-permute-start.2 = (bf16[8,3712]{1,0:T(8,128)(2,1)S(1)}, bf16[8,3712]{1,0:T(8,128)(2,1)S(1)}, u32[]{:S(2)}, u32[]{:S(2)}) collective-permute-start(bf16[8,3712]{1,0:T(8,128)(2,1)S(1)} %shard_map.64), channel_id=1, source_target_pairs={{0,12},{4,8},{8,4},{12,0},{1,13},{5,9},{9,5},{13,1},{2,14},{6,10},... | collective-permute-start | bytes 178184 | tf_op jit(solution)/shard_map/ppermute | solution.py:17
  7.5 0.0 collective-permute-start.1
  7.5 0.6 %collective-permute-start = (bf16[8,3712]{1,0:T(8,128)(2,1)S(1)}, bf16[8,3712]{1,0:T(8,128)(2,1)S(1)}, u32[]{:S(2)}, u32[]{:S(2)}) collective-permute-start(bf16[8,3712]{1,0:T(8,128)(2,1)S(1)} %shard_map.64), channel_id=1, source_target_pairs={{0,4},{4,0},{8,12},{12,8},{1,5},{5,1},{9,13},{13,9},{2,6},{6,2},{1... | collective-permute-start | bytes 178184 | tf_op jit(solution)/shard_map/ppermute | solution.py:17
  8.1 1.8 %collective-permute-done.2 = bf16[8,3712]{1,0:T(8,128)(2,1)S(1)} collective-permute-done((bf16[8,3712]{1,0:T(8,128)(2,1)S(1)}, bf16[8,3712]{1,0:T(8,128)(2,1)S(1)}, u32[]{:S(2)}, u32[]{:S(2)}) %collective-permute-start.2) | collective-permute-done | bytes 59424 | tf_op jit(solution)/shard_map/ppermute | solution.py:17
  10.0 2.7 %collective-permute-done.1 = bf16[8,3712]{1,0:T(8,128)(2,1)S(1)} collective-permute-done((bf16[8,3712]{1,0:T(8,128)(2,1)S(1)}, bf16[8,3712]{1,0:T(8,128)(2,1)S(1)}, u32[]{:S(2)}, u32[]{:S(2)}) %collective-permute-start.1) | collective-permute-done | bytes 59424 | tf_op jit(solution)/shard_map/ppermute | solution.py:17
  12.7 0.0 collective-permute-done
  12.7 1.6 %collective-permute-start.3 = (bf16[32,3712]{1,0:T(8,128)(2,1)S(1)}, bf16[32,3712]{1,0:T(8,128)(2,1)S(1)}, u32[]{:S(2)}, u32[]{:S(2)}) collective-permute-start(bf16[32,3712]{1,0:T(8,128)(2,1)S(1)} %pad_maximum_fusion.refs_0_), channel_id=1, source_target_pairs={{0,2},{2,0},{1,3},{3,1},{4,6},{6,4},{5,7},{7,5},{8,10},{10,8},{9,1... | collective-permute-start | bytes 712712 | tf_op jit(solution)/shard_map/ppermute | solution.py:17
  14.3 0.0 collective-permute-start.4
  14.3 5.3 %collective-permute-done.3.refs_1_ = bf16[32,3712]{1,0:T(8,128)(2,1)S(1)} collective-permute-done((bf16[32,3712]{1,0:T(8,128)(2,1)S(1)}, bf16[32,3712]{1,0:T(8,128)(2,1)S(1)}, u32[]{:S(2)}, u32[]{:S(2)}) %collective-permute-start.3) | collective-permute-done | bytes 237600 | tf_op jit(solution)/shard_map/ppermute | solution.py:17
  19.6 0.0 collective-permute-start.5
  19.6 0.0 collective-permute-done.4.refs_2_
  19.6 1.5 %collective-permute-done.5.refs_3_ = bf16[32,3712]{1,0:T(8,128)(2,1)S(1)} collective-permute-done((bf16[32,3712]{1,0:T(8,128)(2,1)S(1)}, bf16[32,3712]{1,0:T(8,128)(2,1)S(1)}, u32[]{:S(2)}, u32[]{:S(2)}) %collective-permute-start.5) | collective-permute-done | bytes 237600 | tf_op jit(solution)/shard_map/ppermute | solution.py:17
  21.1 0.0 copy-start
  21.1 3.1 %copy-done = bf16[2,3584,512]{2,1,0:T(8,128)(2,1)S(1)} copy-done((bf16[2,3584,512]{2,1,0:T(8,128)(2,1)S(1)}, bf16[2,3584,512]{2,1,0:T(8,128)(2,1)}, u32[]{:S(2)}) %copy-start) | copy-done | bytes 7340056
  24.2 0.0 copy-start.1
  24.2 3.1 %copy-done.1 = bf16[2,3584,512]{2,1,0:T(8,128)(2,1)S(1)} copy-done((bf16[2,3584,512]{2,1,0:T(8,128)(2,1)S(1)}, bf16[2,3584,512]{2,1,0:T(8,128)(2,1)}, u32[]{:S(2)}) %copy-start.1) | copy-done | bytes 7340056
  27.3 0.0 slice-start
  27.3 1.1 %shard_map.65.refs_0_ = bf16[128,512]{1,0:T(8,128)(2,1)S(1)} custom-call(bf16[32,3712]{1,0:T(8,128)(2,1)S(1)} %pad_maximum_fusion.refs_0_, bf16[32,3712]{1,0:T(8,128)(2,1)S(1)} %collective-permute-done.3.refs_1_, bf16[32,3712]{1,0:T(8,128)(2,1)S(1)} %collective-permute-done.4.refs_2_, bf16[32,3712]{1,0:T(8,128)(2,1)S(1)} %collective-permute-done.5.refs_3_, ...), custom_call_target="tpu_custom_call" | custom-call | flops 939524096 | bytes 7340032 | tf_op jit(solution)/shard_map/pallas_call | solution.py:128
  28.4 0.0 slice-start.1
  28.4 1.6 %collective-permute-start.6 = (bf16[128,512]{1,0:T(8,128)(2,1)S(1)}, bf16[128,512]{1,0:T(8,128)(2,1)S(1)}, u32[]{:S(2)}, u32[]{:S(2)}) collective-permute-start(bf16[128,512]{1,0:T(8,128)(2,1)S(1)} %shard_map.65.refs_0_), channel_id=1, source_target_pairs={{0,2},{2,0},{1,3},{3,1},{4,6},{6,4},{5,7},{7,5},{8,10},{10,8},{9,1... | collective-permute-start | bytes 393224 | tf_op jit(solution)/shard_map/ppermute | solution.py:17
  30.1 1.1 %shard_map.66.refs_4_ = bf16[128,512]{1,0:T(8,128)(2,1)S(1)} custom-call(bf16[32,3712]{1,0:T(8,128)(2,1)S(1)} %pad_maximum_fusion.refs_0_, bf16[32,3712]{1,0:T(8,128)(2,1)S(1)} %collective-permute-done.3.refs_1_, bf16[32,3712]{1,0:T(8,128)(2,1)S(1)} %collective-permute-done.4.refs_2_, bf16[32,3712]{1,0:T(8,128)(2,1)S(1)} %collective-permute-done.5.refs_3_, ...), custom_call_target="tpu_custom_call" | custom-call | flops 939524096 | bytes 7340032 | tf_op jit(solution)/shard_map/pallas_call | solution.py:128
  31.2 0.5 collective-permute-start.9
  31.7 0.0 collective-permute-start.7
  31.7 0.5 collective-permute-start.10
  32.2 2.1 %collective-permute-done.6.refs_1_ = bf16[128,512]{1,0:T(8,128)(2,1)S(1)} collective-permute-done((bf16[128,512]{1,0:T(8,128)(2,1)S(1)}, bf16[128,512]{1,0:T(8,128)(2,1)S(1)}, u32[]{:S(2)}, u32[]{:S(2)}) %collective-permute-start.6) | collective-permute-done | bytes 131104 | tf_op jit(solution)/shard_map/ppermute | solution.py:17
  34.3 0.0 collective-permute-start.8
  34.3 2.6 %collective-permute-done.9.refs_5_ = bf16[128,512]{1,0:T(8,128)(2,1)S(1)} collective-permute-done((bf16[128,512]{1,0:T(8,128)(2,1)S(1)}, bf16[128,512]{1,0:T(8,128)(2,1)S(1)}, u32[]{:S(2)}, u32[]{:S(2)}) %collective-permute-start.9) | collective-permute-done | bytes 131104 | tf_op jit(solution)/shard_map/ppermute | solution.py:17
  36.8 0.0 collective-permute-start.11
  36.8 0.0 collective-permute-done.7.refs_2_
  36.9 0.0 collective-permute-done.10.refs_6_
  36.9 0.0 collective-permute-done.8.refs_3_
  36.9 1.3 %collective-permute-done.11.refs_7_ = bf16[128,512]{1,0:T(8,128)(2,1)S(1)} collective-permute-done((bf16[128,512]{1,0:T(8,128)(2,1)S(1)}, bf16[128,512]{1,0:T(8,128)(2,1)S(1)}, u32[]{:S(2)}, u32[]{:S(2)}) %collective-permute-start.11) | collective-permute-done | bytes 131104 | tf_op jit(solution)/shard_map/ppermute | solution.py:17
  38.2 0.0 slice-done
  38.2 0.0 slice-done.1
  38.2 1.3 %shard_map.67 = (bf16[32,896]{1,0:T(8,128)(2,1)S(1)}, bf16[32,896]{1,0:T(8,128)(2,1)S(1)}, bf16[32,896]{1,0:T(8,128)(2,1)S(1)}, bf16[32,896]{1,0:T(8,128)(2,1)S(1)}) custom-call(bf16[128,512]{1,0:T(8,128)(2,1)S(1)} %shard_map.65.refs_0_, bf16[128,512]{1,0:T(8,128)(2,1)S(1)} %collective-permute-done.6.refs_1_, ...), custom_call_target="tpu_custom_call" | custom-call | flops 939524096 | bytes 7340032 | tf_op jit(solution)/shard_map/pallas_call | solution.py:141
  39.5 0.7 %collective-permute-start.12 = (bf16[32,896]{1,0:T(8,128)(2,1)S(1)}, bf16[32,896]{1,0:T(8,128)(2,1)S(1)}, u32[]{:S(2)}, u32[]{:S(2)}) collective-permute-start(bf16[32,896]{1,0:T(8,128)(2,1)S(1)} %get-tuple-element.10), channel_id=1, source_target_pairs={{0,4},{4,0},{8,12},{12,8},{1,5},{5,1},{9,13},{13,9},{2,6},{6,2},{1... | collective-permute-start | bytes 172040 | tf_op jit(solution)/shard_map/ppermute | solution.py:17
  40.2 2.1 %collective-permute-start.13 = (bf16[32,896]{1,0:T(8,128)(2,1)S(1)}, bf16[32,896]{1,0:T(8,128)(2,1)S(1)}, u32[]{:S(2)}, u32[]{:S(2)}) collective-permute-start(bf16[32,896]{1,0:T(8,128)(2,1)S(1)} %get-tuple-element.11), channel_id=1, source_target_pairs={{0,8},{4,12},{8,0},{12,4},{1,9},{5,13},{9,1},{13,5},{2,10},{6,14},... | collective-permute-start | bytes 172040 | tf_op jit(solution)/shard_map/ppermute | solution.py:17
  42.3 1.6 %collective-permute-start.14 = (bf16[32,896]{1,0:T(8,128)(2,1)S(1)}, bf16[32,896]{1,0:T(8,128)(2,1)S(1)}, u32[]{:S(2)}, u32[]{:S(2)}) collective-permute-start(bf16[32,896]{1,0:T(8,128)(2,1)S(1)} %get-tuple-element.12), channel_id=1, source_target_pairs={{0,12},{4,8},{8,4},{12,0},{1,13},{5,9},{9,5},{13,1},{2,14},{6,10},... | collective-permute-start | bytes 172040 | tf_op jit(solution)/shard_map/ppermute | solution.py:17
  43.9 0.4 collective-permute-done.12.refs_1_
  44.3 3.1 %collective-permute-done.13.refs_2_ = bf16[32,896]{1,0:T(8,128)(2,1)S(1)} collective-permute-done((bf16[32,896]{1,0:T(8,128)(2,1)S(1)}, bf16[32,896]{1,0:T(8,128)(2,1)S(1)}, u32[]{:S(2)}, u32[]{:S(2)}) %collective-permute-start.13) | collective-permute-done | bytes 57376 | tf_op jit(solution)/shard_map/ppermute | solution.py:17
  47.4 1.0 %collective-permute-done.14.refs_3_ = bf16[32,896]{1,0:T(8,128)(2,1)S(1)} collective-permute-done((bf16[32,896]{1,0:T(8,128)(2,1)S(1)}, bf16[32,896]{1,0:T(8,128)(2,1)S(1)}, u32[]{:S(2)}, u32[]{:S(2)}) %collective-permute-start.14) | collective-permute-done | bytes 57376 | tf_op jit(solution)/shard_map/ppermute | solution.py:17
  48.5 0.1 collective-permute-start.17
  48.5 1.6 %collective-permute-start.16 = (bf16[8,896]{1,0:T(8,128)(2,1)S(1)}, bf16[8,896]{1,0:T(8,128)(2,1)S(1)}, u32[]{:S(2)}, u32[]{:S(2)}) collective-permute-start(bf16[8,896]{1,0:T(8,128)(2,1)S(1)} %get-tuple-element.14), channel_id=1, source_target_pairs={{0,1},{1,0},{2,3},{3,2},{4,5},{5,4},{6,7},{7,6},{8,9},{9,8},{10,11... | collective-permute-start | bytes 43016 | tf_op jit(solution)/shard_map/ppermute | solution.py:159
  50.1 0.5 collective-permute-start.15
  50.7 1.1 %collective-permute-done.17.refs_3_ = bf16[8,896]{1,0:T(8,128)(2,1)S(1)} collective-permute-done((bf16[8,896]{1,0:T(8,128)(2,1)S(1)}, bf16[8,896]{1,0:T(8,128)(2,1)S(1)}, u32[]{:S(2)}, u32[]{:S(2)}) %collective-permute-start.17) | collective-permute-done | bytes 14368 | tf_op jit(solution)/shard_map/ppermute | solution.py:159
  51.8 0.0 collective-permute-done.16.refs_2_
  51.8 2.1 %collective-permute-done.15.refs_1_ = bf16[8,896]{1,0:T(8,128)(2,1)S(1)} collective-permute-done((bf16[8,896]{1,0:T(8,128)(2,1)S(1)}, bf16[8,896]{1,0:T(8,128)(2,1)S(1)}, u32[]{:S(2)}, u32[]{:S(2)}) %collective-permute-start.15) | collective-permute-done | bytes 14368 | tf_op jit(solution)/shard_map/ppermute | solution.py:159
  53.8 0.6 %shard_map.69 = bf16[8,3584]{1,0:T(8,128)(2,1)} custom-call(bf16[8,896]{1,0:T(8,128)(2,1)S(1)} %get-tuple-element.16.refs_0_, bf16[8,896]{1,0:T(8,128)(2,1)S(1)} %collective-permute-done.15.refs_1_, bf16[8,896]{1,0:T(8,128)(2,1)S(1)} %collective-permute-done.16.refs_2_, bf16[8,896]{1,0:T(8,128)(2,1)S(1)} %collective-permute-done.17.refs_3_), custom_call_target="tpu_custom_call" | custom-call | tf_op jit(solution)/shard_map/pallas_call | solution.py:164
  (4 shorter events, 0.1 us)
Async XLA Ops:
  0.0 0.8 %copy-start.2 = (bf16[8,3584]{1,0:T(8,128)(2,1)S(1)}, bf16[8,3584]{1,0:T(8,128)(2,1)}, u32[]{:S(2)}) copy-start(bf16[8,3584]{1,0:T(8,128)(2,1)} %tok_ref.1) | copy-start | bytes 172036
  0.8 0.7 %copy-start.3 = (s32[8,8]{1,0:T(8,128)S(1)}, s32[8,8]{1,0:T(8,128)}, u32[]{:S(2)}) copy-start(s32[8,8]{1,0:T(8,128)} %ids_ref.1) | copy-start | bytes 772
  1.5 0.7 %copy-start.4 = (f32[8,8]{1,0:T(8,128)S(1)}, f32[8,8]{1,0:T(8,128)}, u32[]{:S(2)}) copy-start(f32[8,8]{1,0:T(8,128)} %scores_ref.1) | copy-start | bytes 772
  2.4 7.6 %collective-permute-start.2 = (bf16[8,3712]{1,0:T(8,128)(2,1)S(1)}, bf16[8,3712]{1,0:T(8,128)(2,1)S(1)}, u32[]{:S(2)}, u32[]{:S(2)}) collective-permute-start(bf16[8,3712]{1,0:T(8,128)(2,1)S(1)} %shard_map.64), channel_id=1, source_target_pairs={{0,12},{4,8},{8,4},{12,0},{1,13},{5,9},{9,5},{13,1},{2,14},{6,10},... | collective-permute-start | bytes 178184 | tf_op jit(solution)/shard_map/ppermute | solution.py:17
  7.5 5.2 %collective-permute-start.1 = (bf16[8,3712]{1,0:T(8,128)(2,1)S(1)}, bf16[8,3712]{1,0:T(8,128)(2,1)S(1)}, u32[]{:S(2)}, u32[]{:S(2)}) collective-permute-start(bf16[8,3712]{1,0:T(8,128)(2,1)S(1)} %shard_map.64), channel_id=1, source_target_pairs={{0,8},{4,12},{8,0},{12,4},{1,9},{5,13},{9,1},{13,5},{2,10},{6,14},... | collective-permute-start | bytes 178184 | tf_op jit(solution)/shard_map/ppermute | solution.py:17
  7.5 5.2 %collective-permute-start = (bf16[8,3712]{1,0:T(8,128)(2,1)S(1)}, bf16[8,3712]{1,0:T(8,128)(2,1)S(1)}, u32[]{:S(2)}, u32[]{:S(2)}) collective-permute-start(bf16[8,3712]{1,0:T(8,128)(2,1)S(1)} %shard_map.64), channel_id=1, source_target_pairs={{0,4},{4,0},{8,12},{12,8},{1,5},{5,1},{9,13},{13,9},{2,6},{6,2},{1... | collective-permute-start | bytes 178184 | tf_op jit(solution)/shard_map/ppermute | solution.py:17
  12.7 6.9 %collective-permute-start.3 = (bf16[32,3712]{1,0:T(8,128)(2,1)S(1)}, bf16[32,3712]{1,0:T(8,128)(2,1)S(1)}, u32[]{:S(2)}, u32[]{:S(2)}) collective-permute-start(bf16[32,3712]{1,0:T(8,128)(2,1)S(1)} %pad_maximum_fusion.refs_0_), channel_id=1, source_target_pairs={{0,2},{2,0},{1,3},{3,1},{4,6},{6,4},{5,7},{7,5},{8,10},{10,8},{9,1... | collective-permute-start | bytes 712712 | tf_op jit(solution)/shard_map/ppermute | solution.py:17
  14.3 5.3 %collective-permute-start.4 = (bf16[32,3712]{1,0:T(8,128)(2,1)S(1)}, bf16[32,3712]{1,0:T(8,128)(2,1)S(1)}, u32[]{:S(2)}, u32[]{:S(2)}) collective-permute-start(bf16[32,3712]{1,0:T(8,128)(2,1)S(1)} %pad_maximum_fusion.refs_0_), channel_id=1, source_target_pairs={{0,1},{1,0},{2,3},{3,2},{4,5},{5,4},{6,7},{7,6},{8,9},{9,8},{10,11... | collective-permute-start | bytes 712712 | tf_op jit(solution)/shard_map/ppermute | solution.py:17
  19.6 1.5 %collective-permute-start.5 = (bf16[32,3712]{1,0:T(8,128)(2,1)S(1)}, bf16[32,3712]{1,0:T(8,128)(2,1)S(1)}, u32[]{:S(2)}, u32[]{:S(2)}) collective-permute-start(bf16[32,3712]{1,0:T(8,128)(2,1)S(1)} %collective-permute-done.3.refs_1_), channel_id=1, source_target_pairs={{0,1},{1,0},{2,3},{3,2},{4,5},{5,4},{6,7},{7,6},{8,9},{9,8},{10,11... | collective-permute-start | bytes 712712 | tf_op jit(solution)/shard_map/ppermute | solution.py:17
  21.1 3.1 %copy-start = (bf16[2,3584,512]{2,1,0:T(8,128)(2,1)S(1)}, bf16[2,3584,512]{2,1,0:T(8,128)(2,1)}, u32[]{:S(2)}) copy-start(bf16[2,3584,512]{2,1,0:T(8,128)(2,1)} %refs_4_.3) | copy-start | bytes 22020100
  24.2 3.1 %copy-start.1 = (bf16[2,3584,512]{2,1,0:T(8,128)(2,1)S(1)}, bf16[2,3584,512]{2,1,0:T(8,128)(2,1)}, u32[]{:S(2)}) copy-start(bf16[2,3584,512]{2,1,0:T(8,128)(2,1)} %refs_5_.3) | copy-start | bytes 22020100
  27.3 10.9 %slice-start = ((s8[7340032]{0:T(1024)(128)(4,1)}), s8[4194304]{0:T(1024)(128)(4,1)S(1)}, s32[]{:S(2)}) async-start(s8[7340032]{0:T(1024)(128)(4,1)} %bitcast), calls=%async_computation | async-start | bytes 8388608
  28.4 9.8 %slice-start.1 = ((s8[7340032]{0:T(1024)(128)(4,1)}), s8[3145728]{0:T(1024)(128)(4,1)S(1)}, s32[]{:S(2)}) async-start(s8[7340032]{0:T(1024)(128)(4,1)} %bitcast), calls=%async_computation.1 | async-start | bytes 6291456
  28.4 5.9 %collective-permute-start.6 = (bf16[128,512]{1,0:T(8,128)(2,1)S(1)}, bf16[128,512]{1,0:T(8,128)(2,1)S(1)}, u32[]{:S(2)}, u32[]{:S(2)}) collective-permute-start(bf16[128,512]{1,0:T(8,128)(2,1)S(1)} %shard_map.65.refs_0_), channel_id=1, source_target_pairs={{0,2},{2,0},{1,3},{3,1},{4,6},{6,4},{5,7},{7,5},{8,10},{10,8},{9,1... | collective-permute-start | bytes 393224 | tf_op jit(solution)/shard_map/ppermute | solution.py:17
  31.2 5.6 %collective-permute-start.9 = (bf16[128,512]{1,0:T(8,128)(2,1)S(1)}, bf16[128,512]{1,0:T(8,128)(2,1)S(1)}, u32[]{:S(2)}, u32[]{:S(2)}) collective-permute-start(bf16[128,512]{1,0:T(8,128)(2,1)S(1)} %shard_map.66.refs_4_), channel_id=1, source_target_pairs={{0,2},{2,0},{1,3},{3,1},{4,6},{6,4},{5,7},{7,5},{8,10},{10,8},{9,1... | collective-permute-start | bytes 393224 | tf_op jit(solution)/shard_map/ppermute | solution.py:17
  31.7 5.1 %collective-permute-start.7 = (bf16[128,512]{1,0:T(8,128)(2,1)S(1)}, bf16[128,512]{1,0:T(8,128)(2,1)S(1)}, u32[]{:S(2)}, u32[]{:S(2)}) collective-permute-start(bf16[128,512]{1,0:T(8,128)(2,1)S(1)} %shard_map.65.refs_0_), channel_id=1, source_target_pairs={{0,1},{1,0},{2,3},{3,2},{4,5},{5,4},{6,7},{7,6},{8,9},{9,8},{10,11... | collective-permute-start | bytes 393224 | tf_op jit(solution)/shard_map/ppermute | solution.py:17
  31.7 5.1 %collective-permute-start.10 = (bf16[128,512]{1,0:T(8,128)(2,1)S(1)}, bf16[128,512]{1,0:T(8,128)(2,1)S(1)}, u32[]{:S(2)}, u32[]{:S(2)}) collective-permute-start(bf16[128,512]{1,0:T(8,128)(2,1)S(1)} %shard_map.66.refs_4_), channel_id=1, source_target_pairs={{0,1},{1,0},{2,3},{3,2},{4,5},{5,4},{6,7},{7,6},{8,9},{9,8},{10,11... | collective-permute-start | bytes 393224 | tf_op jit(solution)/shard_map/ppermute | solution.py:17
  34.3 2.6 %collective-permute-start.8 = (bf16[128,512]{1,0:T(8,128)(2,1)S(1)}, bf16[128,512]{1,0:T(8,128)(2,1)S(1)}, u32[]{:S(2)}, u32[]{:S(2)}) collective-permute-start(bf16[128,512]{1,0:T(8,128)(2,1)S(1)} %collective-permute-done.6.refs_1_), channel_id=1, source_target_pairs={{0,1},{1,0},{2,3},{3,2},{4,5},{5,4},{6,7},{7,6},{8,9},{9,8},{10,11... | collective-permute-start | bytes 393224 | tf_op jit(solution)/shard_map/ppermute | solution.py:17
  36.8 1.3 %collective-permute-start.11 = (bf16[128,512]{1,0:T(8,128)(2,1)S(1)}, bf16[128,512]{1,0:T(8,128)(2,1)S(1)}, u32[]{:S(2)}, u32[]{:S(2)}) collective-permute-start(bf16[128,512]{1,0:T(8,128)(2,1)S(1)} %collective-permute-done.9.refs_5_), channel_id=1, source_target_pairs={{0,1},{1,0},{2,3},{3,2},{4,5},{5,4},{6,7},{7,6},{8,9},{9,8},{10,11... | collective-permute-start | bytes 393224 | tf_op jit(solution)/shard_map/ppermute | solution.py:17
  39.5 4.9 %collective-permute-start.12 = (bf16[32,896]{1,0:T(8,128)(2,1)S(1)}, bf16[32,896]{1,0:T(8,128)(2,1)S(1)}, u32[]{:S(2)}, u32[]{:S(2)}) collective-permute-start(bf16[32,896]{1,0:T(8,128)(2,1)S(1)} %get-tuple-element.10), channel_id=1, source_target_pairs={{0,4},{4,0},{8,12},{12,8},{1,5},{5,1},{9,13},{13,9},{2,6},{6,2},{1... | collective-permute-start | bytes 172040 | tf_op jit(solution)/shard_map/ppermute | solution.py:17
  40.2 7.2 %collective-permute-start.13 = (bf16[32,896]{1,0:T(8,128)(2,1)S(1)}, bf16[32,896]{1,0:T(8,128)(2,1)S(1)}, u32[]{:S(2)}, u32[]{:S(2)}) collective-permute-start(bf16[32,896]{1,0:T(8,128)(2,1)S(1)} %get-tuple-element.11), channel_id=1, source_target_pairs={{0,8},{4,12},{8,0},{12,4},{1,9},{5,13},{9,1},{13,5},{2,10},{6,14},... | collective-permute-start | bytes 172040 | tf_op jit(solution)/shard_map/ppermute | solution.py:17
  42.3 6.1 %collective-permute-start.14 = (bf16[32,896]{1,0:T(8,128)(2,1)S(1)}, bf16[32,896]{1,0:T(8,128)(2,1)S(1)}, u32[]{:S(2)}, u32[]{:S(2)}) collective-permute-start(bf16[32,896]{1,0:T(8,128)(2,1)S(1)} %get-tuple-element.12), channel_id=1, source_target_pairs={{0,12},{4,8},{8,4},{12,0},{1,13},{5,9},{9,5},{13,1},{2,14},{6,10},... | collective-permute-start | bytes 172040 | tf_op jit(solution)/shard_map/ppermute | solution.py:17
  48.5 3.3 %collective-permute-start.17 = (bf16[8,896]{1,0:T(8,128)(2,1)S(1)}, bf16[8,896]{1,0:T(8,128)(2,1)S(1)}, u32[]{:S(2)}, u32[]{:S(2)}) collective-permute-start(bf16[8,896]{1,0:T(8,128)(2,1)S(1)} %get-tuple-element.13), channel_id=1, source_target_pairs={{0,3},{1,2},{2,1},{3,0},{4,7},{5,6},{6,5},{7,4},{8,11},{9,10},{10,... | collective-permute-start | bytes 43016 | tf_op jit(solution)/shard_map/ppermute | solution.py:159
  48.5 3.2 %collective-permute-start.16 = (bf16[8,896]{1,0:T(8,128)(2,1)S(1)}, bf16[8,896]{1,0:T(8,128)(2,1)S(1)}, u32[]{:S(2)}, u32[]{:S(2)}) collective-permute-start(bf16[8,896]{1,0:T(8,128)(2,1)S(1)} %get-tuple-element.14), channel_id=1, source_target_pairs={{0,1},{1,0},{2,3},{3,2},{4,5},{5,4},{6,7},{7,6},{8,9},{9,8},{10,11... | collective-permute-start | bytes 43016 | tf_op jit(solution)/shard_map/ppermute | solution.py:159
  50.1 3.7 %collective-permute-start.15 = (bf16[8,896]{1,0:T(8,128)(2,1)S(1)}, bf16[8,896]{1,0:T(8,128)(2,1)S(1)}, u32[]{:S(2)}, u32[]{:S(2)}) collective-permute-start(bf16[8,896]{1,0:T(8,128)(2,1)S(1)} %get-tuple-element.15), channel_id=1, source_target_pairs={{0,2},{1,3},{2,0},{3,1},{4,6},{5,7},{6,4},{7,5},{8,10},{9,11},{10,... | collective-permute-start | bytes 43016 | tf_op jit(solution)/shard_map/ppermute | solution.py:159

commit v2 on v1

v2 whole, which is shorter than its diff:
```python
import functools

import jax
import jax.numpy as jnp
from jax import lax
from jax.experimental import pallas as pl
from jax.experimental.pallas import tpu as pltpu
from jax.sharding import PartitionSpec as P

route_scale = 2.827
LANES = 128
f32, bf16 = jnp.float32, jnp.bfloat16
VMEM = pl.BlockSpec(memory_space=pltpu.VMEM)
HBM = pl.BlockSpec(memory_space=pltpu.HBM)


def swap(x, axis, k):
    return lax.ppermute(x, axis, [(i, i ^ k) for i in range(lax.axis_size(axis))])


def in_hbm(x):
    return pltpu.with_memory_space_constraint(x, pltpu.HBM)


def call(kernel, out_shape, n_in, flops=0, size=0, vmem=4, scratch=(), spec=VMEM):
    return pl.pallas_call(
        kernel,
        out_shape=out_shape,
        in_specs=[spec] * n_in,
        out_specs=jax.tree.map(lambda _: VMEM, out_shape),
        scratch_shapes=scratch,
        compiler_params=pltpu.CompilerParams(vmem_limit_bytes=vmem << 20),
        cost_estimate=pl.CostEstimate(flops=flops, bytes_accessed=size, transcendentals=0),
    )


def pack_kernel(experts, tok_hbm, ids_hbm, scores_hbm, out_ref, ids_ref, scores_ref, sems):
    rows, features = tok_hbm.shape
    extra = out_ref.shape[1] - features
    pairs = ((ids_hbm, ids_ref), (scores_hbm, scores_ref), (tok_hbm, out_ref.at[:, :features]))
    copies = [pltpu.make_async_copy(a, b, sems.at[i]) for i, (a, b) in enumerate(pairs)]
    for copy in copies:
        copy.start()
    copies[0].wait()
    copies[1].wait()
    gate = 1.0 / (1.0 + jnp.exp(-scores_ref[...]))
    share = route_scale * gate / jnp.sum(gate, axis=1, keepdims=True)
    column = lax.broadcasted_iota(jnp.int32, (rows, extra), 1)
    expert, term = column % experts, column // experts
    weight = jnp.zeros((rows, extra), f32)
    for k in range(ids_ref.shape[1]):
        weight += jnp.where(ids_ref[:, k : k + 1] == expert, share[:, k : k + 1], 0.0)
    first = weight.astype(bf16).astype(f32)
    second = (weight - first).astype(bf16).astype(f32)
    third = weight - first - second
    terms = jnp.where(term == 0, first, jnp.where(term == 1, second, jnp.where(term == 2, third, 0.0)))
    out_ref[:, features:] = terms.astype(bf16)
    copies[2].wait()


def fetch(parts, after, pieces=4):
    arrays = [p[0] for p in parts]

    def body(*refs):
        n = len(arrays)
        srcs, outs, mark, sems = refs[:n], refs[n + 1 : 2 * n + 1], refs[2 * n + 1], refs[2 * n + 2]
        mark[...] = jnp.zeros_like(mark)
        copies = []
        for (_, first, count), src, out in zip(parts, srcs, outs):
            step = src.shape[1] // pieces
            for e in range(count):
                for p in range(pieces):
                    rows = pl.ds(p * step, step)
                    copies.append(
                        pltpu.make_async_copy(
                            src.at[first + e, rows], out.at[e, rows], sems.at[len(copies)]
                        )
                    )
        for copy in copies:
            copy.start()
        for copy in copies:
            copy.wait()

    shapes = [(count,) + a.shape[1:] for a, _, count in parts]
    return pl.pallas_call(
        body,
        out_shape=[pltpu.VMEM(s, bf16) for s in shapes] + [pltpu.VMEM((8, LANES), f32)],
        in_specs=[HBM] * len(arrays) + [VMEM],
        out_specs=[VMEM] * (len(arrays) + 1),
        scratch_shapes=[pltpu.SemaphoreType.DMA((pieces * sum(s[0] for s in shapes),))],
        compiler_params=pltpu.CompilerParams(vmem_limit_bytes=1 << 20),
        cost_estimate=pl.CostEstimate(
            flops=0, bytes_accessed=sum(2 * s[0] * s[1] * s[2] for s in shapes), transcendentals=0
        ),
    )(*[in_hbm(a) for a in arrays], after)


def stack(parts, after):
    def body(*refs):
        at, out = 0, refs[-1]
        for ref in refs[: len(parts)]:
            rows = ref.shape[0]
            out[at : at + rows, :] = ref[...]
            at += rows

    rows, width = sum(p.shape[0] for p in parts), parts[0].shape[1]
    shape = jax.ShapeDtypeStruct((rows, width), parts[0].dtype)
    return call(body, shape, len(parts) + len(after))(*parts, *after)


def stack_one(part, after):
    def body(ref, _, out):
        out[...] = ref[...]

    return call(body, jax.ShapeDtypeStruct(part.shape, part.dtype), 2)(part, after)


def hidden(blocks, gates, ups, which, experts, features):
    n = len(blocks)
    local_experts, _, depth = ups.shape
    count = sum(b.shape[0] for b in blocks)

    def body(*refs):
        ins, (gate_ref, up_ref, out_ref) = refs[:n], refs[n:]
        x = jnp.concatenate([b[:, :features] for b in ins], axis=0)
        tail = jnp.concatenate([b[:, features:] for b in ins], axis=0).astype(f32)
        column = lax.broadcasted_iota(jnp.int32, tail.shape, 1)
        for i, e in enumerate(which):
            mine = lax.axis_index("node") * local_experts + e
            keep = (column % experts == mine) & (column < 3 * experts)
            weight = jnp.sum(jnp.where(keep, tail, 0.0), axis=1, keepdims=True)
            gate = jnp.dot(x, gate_ref[e], preferred_element_type=f32)
            up = jnp.dot(x, up_ref[e], preferred_element_type=f32)
            out_ref[i] = (gate / (1.0 + jnp.exp(-gate)) * up * weight).astype(bf16)

    shape = jax.ShapeDtypeStruct((len(which), count, depth), bf16)
    work = len(which) * features * depth
    return call(
        body, shape, n + 2, 4 * count * work, 4 * work, 32 if count > 128 else 4
    )(*blocks, gates, ups)


def down(terms, total, weights, local, sub, nodes, last):
    n_slices = local * sub
    arrays = []
    for term in terms:
        if not any(term[0] is a for a in arrays):
            arrays.append(term[0])
    index = [next(i for i, a in enumerate(arrays) if a is term[0]) for term in terms]
    tokens, width = total
    block = tokens // n_slices
    depth = terms[0][0].shape[2]
    rows = block // nodes
    before = [] if last is None else [last]

    def place(r):
        s, x = divmod(r, local)
        return (lax.axis_index("local") * sub + lax.axis_index("sub")) ^ (x * sub + s)

    def body(*refs):
        ins = refs[: len(arrays)]
        down_ref, out_ref = refs[len(arrays)], refs[-1]
        acc = [None] * n_slices
        if before:
            for b in range(n_slices):
                acc[b] = refs[len(arrays) + 1][b * block : (b + 1) * block, :]
        groups = {}
        for i, (_, entry, e, r, blocks) in zip(index, terms):
            groups.setdefault((e, r), []).append((i, entry, blocks))
        for (e, r), members in groups.items():
            w = down_ref[e, pl.ds(pl.multiple_of(place(r) * depth, depth), depth), :]
            h = jnp.concatenate([ins[i][entry] for i, entry, _ in members], axis=0)
            product = jnp.dot(h, w, preferred_element_type=f32)
            for j, b in enumerate(b for m in members for b in m[2]):
                part = product[j * block : (j + 1) * block]
                acc[b] = part if acc[b] is None else acc[b] + part
        if not before:
            for b in range(n_slices):
                out_ref[b * block : (b + 1) * block, :] = acc[b]
            return
        node = lax.axis_index("node")
        for b in range(n_slices):
            for z in range(nodes):
                out_ref[(node ^ z) * n_slices + place(b)] = acc[b][z * rows : (z + 1) * rows].astype(
                    bf16
                )

    shape = (
        jax.ShapeDtypeStruct((nodes * n_slices, rows, width), bf16)
        if before
        else jax.ShapeDtypeStruct((tokens, width), f32)
    )
    pairs = {(t[2], t[3]) for t in terms}
    return call(
        body,
        shape,
        len(arrays) + 1 + len(before),
        2 * tokens * len(pairs) * depth * width,
        2 * len(pairs) * depth * width,
        32 if tokens > 256 else 4,
    )(*arrays, weights, *before)


def sum_kernel(nodes, in_ref, out_ref):
    n_slices, width = in_ref.shape[0] // nodes, in_ref.shape[2]
    for i in range(n_slices):
        total = in_ref[i].astype(f32)
        for n in range(1, nodes):
            total += in_ref[n * n_slices + i].astype(f32)
        out_ref[:, i * width : (i + 1) * width] = total.astype(bf16)


def per_device(tokens, ids, scores, gate_w, up_w, down_w):
    nodes, local, sub = (lax.axis_size(a) for a in ("node", "local", "sub"))
    rows, features = tokens.shape
    local_experts, _, depth = gate_w.shape
    width = down_w.shape[2]
    experts = local_experts * nodes
    n_slices = local * sub
    extra = -(-3 * experts // LANES) * LANES
    count = n_slices * nodes * rows

    packed = call(
        functools.partial(pack_kernel, experts),
        jax.ShapeDtypeStruct((rows, features + extra), bf16),
        3,
        scratch=[
            pltpu.VMEM(ids.shape, ids.dtype),
            pltpu.VMEM(scores.shape, f32),
            pltpu.SemaphoreType.DMA((3,)),
        ],
        spec=HBM,
    )(in_hbm(tokens), in_hbm(ids), in_hbm(scores))
    early = [swap(packed, "local", x) for x in range(1, local)]
    others = [swap(packed, "node", z) for z in range(1, nodes)]
    gates, mark = fetch([(gate_w, 0, local_experts)], packed)
    rest = stack(others, [mark] + early)
    far = [swap(rest, "local", x) for x in range(1, local)]
    ups, mark = fetch([(up_w, 0, local_experts)], rest)

    blocks = [stack([packed, rest], [])]
    blocks += [stack(pair, [mark]) for pair in zip(early, far)]
    for s in range(1, sub):
        blocks += [swap(b, "sub", s) for b in blocks[:local]]

    def spread(parts, e, over):
        terms = []
        for x, part in enumerate(parts):
            for s in over:
                r = s * local + x
                piece = swap(part, "sub", s) if s else part
                terms.append((piece, 0, e, r, [b ^ r for b in range(n_slices)]))
        return terms

    soon, late = [], []
    for e in range(local_experts):
        h = hidden(blocks, gates, ups, [e], experts, features)
        parts = [h] + [swap(h, "local", x) for x in range(1, local)]
        if e < local_experts - 1:
            terms = spread(parts, e, range(sub))
            soon += [t for t in terms if t[3] <= local]
            late += [t for t in terms if t[3] > local]
    soon += spread(parts[:1], e, range(sub))
    shape = (count, width)
    total = down(soon, shape, down_w, local, sub, nodes, None)
    parts[1:] = [stack_one(p, total) for p in parts[1:]]
    late += [t for t in spread(parts, e, range(sub)) if t[3] % local]
    part = down(late, shape, down_w, local, sub, nodes, total)
    part = lax.all_to_all(part, ("node", "local", "sub"), 0, 0, tiled=True)
    return call(
        functools.partial(sum_kernel, nodes), jax.ShapeDtypeStruct((rows, features), bf16), 1
    )(part)


def solution(mesh):
    everything = P(("groups", "node", "local", "sub"), None)
    weights = P("node", None, ("local", "sub"))
    return jax.shard_map(
        per_device,
        mesh=mesh,
        in_specs=(everything,) * 3 + (weights,) * 3,
        out_specs=everything,
        check_vma=False,
    )
```

time: 54.8 us -> 45.8 us (0.84)
  waiting for transfers between devices: 24.9 us -> 9.93 us
  blocking collectives: 0 us -> 13.2 us
  local copies, waits for them, and re-layouts: 8.38 us -> 0.01 us
  Pallas kernels: 4.36 us -> 11.7 us
  starting transfers between devices: 16.7 us -> 10.6 us
    all_to_all x0 -> x1, blocking collectives: none -> 13.2 us  [per_device(): part = lax.all_to_all(part, ('node', 'local', 'sub'), 0, 0, tiled=True)]
    ppermute x15 -> x13, waiting for transfers between devices: 21.7 us -> 9.93 us  [swap(): lax.ppermute(x, axis, [(i, i ^ k) for i in range(lax.axis_size(axis))])]
    unnamed x14 -> x4, local copies, waits for them, and re-layouts: 8.37 us -> 0.01 us
    pallas_call x5 -> x11, Pallas kernels: 4.17 us -> 10.8 us  [the longest x2 6.34 us: fetch(): pl.pallas_call(body, out_shape=[pltpu.VMEM(s, bf16) for s in shapes] + [p...]
    ppermute x15 -> x13, starting transfers between devices: 14.5 us -> 10.6 us  [swap(): lax.ppermute(x, axis, [(i, i ^ k) for i in range(lax.axis_size(axis))])]
    ppermute x3 -> x0, waiting for transfers between devices: 3.18 us -> none  [per_device(): lax.ppermute(piece, ('local', 'sub'), [(i, i ^ pair) for i in range(n_sli...]
    ppermute x3 -> x0, starting transfers between devices: 2.2 us -> none  [per_device(): lax.ppermute(piece, ('local', 'sub'), [(i, i ^ pair) for i in range(n_sli...]
    pallas_call x1, Pallas kernels: 0.19 us -> 0.92 us  [per_device(): call(functools.partial(pack_kernel, experts), jax.ShapeDtypeStruct((rows,...]
  transfers between devices with their start and end apart: 18 -> 13, of which waited for: 12 -> 6; matrix products, arithmetic and copies ran while one was open for 0% -> 0% of each run, Pallas kernels for 2% -> 18%
where the time goes in v2:
time: 45.8 us; the launch traced here: 45.6 us
  blocking collectives  13.2 us (29%)
  Pallas kernels  11.7 us (26%)
  starting transfers between devices  10.6 us (23%)
  waiting for transfers between devices  9.93 us (22%)
    all_to_all x1, blocking collectives, per_device(): part = lax.all_to_all(part, ('node', 'local', 'sub'), 0, 0, tiled=True)  13.2 us
    ppermute x13, starting transfers between devices, swap(): lax.ppermute(x, axis, [(i, i ^ k) for i in range(lax.axis_size(axis))])  10.6 us
    ppermute x13, waiting for transfers between devices, swap(): lax.ppermute(x, axis, [(i, i ^ k) for i in range(lax.axis_size(axis))])  9.93 us
    pallas_call x2, Pallas kernels, fetch(): pl.pallas_call(body, out_shape=[pltpu.VMEM(s, bf16) for s in shapes] + [p...  6.34 us
    pallas_call x2, Pallas kernels, hidden(): call(body, shape, n + 2, 4 * count * work, 4 * work, 32 if count > 128 el...  2.26 us
    pallas_call x2, Pallas kernels, down(): call(body, shape, len(arrays) + 1 + len(before), 2 * tokens * len(pairs)...  1.48 us
    pallas_call x1, Pallas kernels, per_device(): call(functools.partial(pack_kernel, experts), jax.ShapeDtypeStruct((rows,...  0.92 us
  transfers between devices with their start and end apart: 13, of which 6 were waited for; matrix products, arithmetic and copies ran while one was open for 0% of the time, Pallas kernels for 18%

profile of v2, /device:TPU:0, one launch (start us, length us, event | category | flops | bytes accessed | tf_op | source)
XLA Modules:
  0.0 45.6 jit_solution(9135664290700265904)
XLA Ops:
  0.0 0.9 %shard_map.64.refs_1_.refs_0_ = bf16[8,3712]{1,0:T(8,128)(2,1)S(1)} custom-call(bf16[8,3584]{1,0:T(8,128)(2,1)} %tok_hbm.1, s32[8,8]{1,0:T(8,128)} %ids_hbm.1, f32[8,8]{1,0:T(8,128)} %scores_hbm.1), custom_call_target="tpu_custom_call" | custom-call | tf_op jit(solution)/shard_map/pallas_call | solution.py:223
  0.9 3.0 %collective-permute-start.3 = (bf16[8,3712]{1,0:T(8,128)(2,1)S(1)}, bf16[8,3712]{1,0:T(8,128)(2,1)S(1)}, u32[]{:S(2)}, u32[]{:S(2)}) collective-permute-start(bf16[8,3712]{1,0:T(8,128)(2,1)S(1)} %shard_map.64.refs_1_.refs_0_), channel_id=1, source_target_pairs={{0,2},{2,0},{1,3},{3,1},{4,6},{6,4},{5,7},{7,5},{8,10},{10,8},{9,1... | collective-permute-start | bytes 178184 | tf_op jit(solution)/shard_map/ppermute | solution.py:18
  3.9 3.6 %collective-permute-start.2 = (bf16[8,3712]{1,0:T(8,128)(2,1)S(1)}, bf16[8,3712]{1,0:T(8,128)(2,1)S(1)}, u32[]{:S(2)}, u32[]{:S(2)}) collective-permute-start(bf16[8,3712]{1,0:T(8,128)(2,1)S(1)} %shard_map.64.refs_1_.refs_0_), channel_id=1, source_target_pairs={{0,12},{4,8},{8,4},{12,0},{1,13},{5,9},{9,5},{13,1},{2,14},{6,10},... | collective-permute-start | bytes 178184 | tf_op jit(solution)/shard_map/ppermute | solution.py:18
  7.5 0.0 collective-permute-start.1
  7.5 0.8 %collective-permute-start = (bf16[8,3712]{1,0:T(8,128)(2,1)S(1)}, bf16[8,3712]{1,0:T(8,128)(2,1)S(1)}, u32[]{:S(2)}, u32[]{:S(2)}) collective-permute-start(bf16[8,3712]{1,0:T(8,128)(2,1)S(1)} %shard_map.64.refs_1_.refs_0_), channel_id=1, source_target_pairs={{0,4},{4,0},{8,12},{12,8},{1,5},{5,1},{9,13},{13,9},{2,6},{6,2},{1... | collective-permute-start | bytes 178184 | tf_op jit(solution)/shard_map/ppermute | solution.py:18
  8.3 3.2 %shard_map.65 = (bf16[2,3584,512]{2,1,0:T(8,128)(2,1)S(1)}, f32[8,128]{1,0:T(8,128)S(1)}) custom-call(bf16[2,3584,512]{2,1,0:T(8,128)(2,1)} %refs_0_.2, bf16[8,3712]{1,0:T(8,128)(2,1)S(1)} %shard_map.64.refs_1_.refs_0_), custom_call_target="tpu_custom_call" | custom-call | bytes 7340032 | tf_op jit(solution)/shard_map/pallas_call | solution.py:85
  11.5 0.0 collective-permute-done.3.refs_4_.refs_0_
  11.5 0.0 collective-permute-done.2.refs_2_
  11.5 1.1 %collective-permute-done.1.refs_1_ = bf16[8,3712]{1,0:T(8,128)(2,1)S(1)} collective-permute-done((bf16[8,3712]{1,0:T(8,128)(2,1)S(1)}, bf16[8,3712]{1,0:T(8,128)(2,1)S(1)}, u32[]{:S(2)}, u32[]{:S(2)}) %collective-permute-start.1) | collective-permute-done | bytes 59424 | tf_op jit(solution)/shard_map/ppermute | solution.py:18
  12.6 0.0 collective-permute-done.refs_0_
  12.7 0.6 %collective-permute-start.4 = (bf16[24,3712]{1,0:T(8,128)(2,1)S(1)}, bf16[24,3712]{1,0:T(8,128)(2,1)S(1)}, u32[]{:S(2)}, u32[]{:S(2)}) collective-permute-start(bf16[24,3712]{1,0:T(8,128)(2,1)S(1)} %shard_map.66.refs_1_), channel_id=1, source_target_pairs={{0,2},{2,0},{1,3},{3,1},{4,6},{6,4},{5,7},{7,5},{8,10},{10,8},{9,1... | collective-permute-start | bytes 534536 | tf_op jit(solution)/shard_map/ppermute | solution.py:18
  13.3 0.1 collective-permute-start.5
  13.4 3.2 %shard_map.68 = (bf16[2,3584,512]{2,1,0:T(8,128)(2,1)S(1)}, f32[8,128]{1,0:T(8,128)S(1)}) custom-call(bf16[2,3584,512]{2,1,0:T(8,128)(2,1)} %refs_0_.3, bf16[24,3712]{1,0:T(8,128)(2,1)S(1)} %shard_map.66.refs_1_), custom_call_target="tpu_custom_call" | custom-call | bytes 7340032 | tf_op jit(solution)/shard_map/pallas_call | solution.py:85
  16.5 1.7 %collective-permute-done.4.refs_1_ = bf16[24,3712]{1,0:T(8,128)(2,1)S(1)} collective-permute-done((bf16[24,3712]{1,0:T(8,128)(2,1)S(1)}, bf16[24,3712]{1,0:T(8,128)(2,1)S(1)}, u32[]{:S(2)}, u32[]{:S(2)}) %collective-permute-start.4) | collective-permute-done | bytes 178208 | tf_op jit(solution)/shard_map/ppermute | solution.py:18
  18.2 0.1 collective-permute-start.6
  18.3 0.0 collective-permute-done.5.refs_2_
  18.3 1.5 %collective-permute-done.6.refs_3_ = bf16[32,3712]{1,0:T(8,128)(2,1)S(1)} collective-permute-done((bf16[32,3712]{1,0:T(8,128)(2,1)S(1)}, bf16[32,3712]{1,0:T(8,128)(2,1)S(1)}, u32[]{:S(2)}, u32[]{:S(2)}) %collective-permute-start.6) | collective-permute-done | bytes 237600 | tf_op jit(solution)/shard_map/ppermute | solution.py:18
  19.8 0.0 slice-start
  19.8 1.1 %shard_map.70.refs_0_ = bf16[1,128,512]{2,1,0:T(8,128)(2,1)S(1)} custom-call(bf16[32,3712]{1,0:T(8,128)(2,1)S(1)} %shard_map.67.refs_0_, bf16[32,3712]{1,0:T(8,128)(2,1)S(1)} %shard_map.69.refs_1_, bf16[32,3712]{1,0:T(8,128)(2,1)S(1)} %collective-permute-done.5.refs_2_, bf16[32,3712]{1,0:T(8,128)(2,1)S(1)} %collective-permute-done.6.refs_3_, ...), custom_call_target="tpu_custom_call" | custom-call | flops 939524096 | bytes 7340032 | tf_op jit(solution)/shard_map/pallas_call | solution.py:138
  20.9 0.0 slice-start.1
  20.9 0.2 collective-permute-start.10
  21.1 0.6 %collective-permute-start.7 = (bf16[1,128,512]{2,1,0:T(8,128)(2,1)S(1)}, bf16[1,128,512]{2,1,0:T(8,128)(2,1)S(1)}, u32[]{:S(2)}, u32[]{:S(2)}) collective-permute-start(bf16[1,128,512]{2,1,0:T(8,128)(2,1)S(1)} %shard_map.70.refs_0_), channel_id=1, source_target_pairs={{0,2},{2,0},{1,3},{3,1},{4,6},{6,4},{5,7},{7,5},{8,10},{10,8},{9,1... | collective-permute-start | bytes 393224 | tf_op jit(solution)/shard_map/ppermute | solution.py:18
  21.7 1.1 %shard_map.71.refs_3_ = bf16[1,128,512]{2,1,0:T(8,128)(2,1)S(1)} custom-call(bf16[32,3712]{1,0:T(8,128)(2,1)S(1)} %shard_map.67.refs_0_, bf16[32,3712]{1,0:T(8,128)(2,1)S(1)} %shard_map.69.refs_1_, bf16[32,3712]{1,0:T(8,128)(2,1)S(1)} %collective-permute-done.5.refs_2_, bf16[32,3712]{1,0:T(8,128)(2,1)S(1)} %collective-permute-done.6.refs_3_, ...), custom_call_target="tpu_custom_call" | custom-call | flops 939524096 | bytes 7340032 | tf_op jit(solution)/shard_map/pallas_call | solution.py:138
  22.8 0.1 collective-permute-start.11
  23.0 1.5 %collective-permute-start.9 = (bf16[1,128,512]{2,1,0:T(8,128)(2,1)S(1)}, bf16[1,128,512]{2,1,0:T(8,128)(2,1)S(1)}, u32[]{:S(2)}, u32[]{:S(2)}) collective-permute-start(bf16[1,128,512]{2,1,0:T(8,128)(2,1)S(1)} %shard_map.71.refs_3_), channel_id=1, source_target_pairs={{0,2},{2,0},{1,3},{3,1},{4,6},{6,4},{5,7},{7,5},{8,10},{10,8},{9,1... | collective-permute-start | bytes 393224 | tf_op jit(solution)/shard_map/ppermute | solution.py:18
  24.5 3.0 %collective-permute-done.7.refs_2_ = bf16[1,128,512]{2,1,0:T(8,128)(2,1)S(1)} collective-permute-done((bf16[1,128,512]{2,1,0:T(8,128)(2,1)S(1)}, bf16[1,128,512]{2,1,0:T(8,128)(2,1)S(1)}, u32[]{:S(2)}, u32[]{:S(2)}) %collective-permute-start.7) | collective-permute-done | bytes 131104 | tf_op jit(solution)/shard_map/ppermute | solution.py:18
  27.5 0.0 collective-permute-start.8
  27.5 0.0 collective-permute-done.10.refs_1_
  27.5 0.0 collective-permute-done.11.refs_4_
  27.5 0.0 slice-done
  27.5 0.0 slice-done.1
  27.5 0.9 %shard_map.72._.refs_4_ = f32[128,896]{1,0:T(8,128)S(1)} custom-call(bf16[1,128,512]{2,1,0:T(8,128)(2,1)S(1)} %shard_map.70.refs_0_, bf16[1,128,512]{2,1,0:T(8,128)(2,1)S(1)} %collective-permute-done.10.refs_1_, bf16[1,128,512]{2,1,0:T(8,128)(2,1)S(1)} %collective-permute-done.7.refs_2_, bf16[1,128,512]{2,1,0:T(8,128)(2,1)S(1)} %shard_map.71.refs_3_, ...), custom_call_target="tpu_custom_call" | custom-call | flops 587202560 | bytes 4587520 | tf_op jit(solution)/shard_map/pallas_call | solution.py:194
  28.4 1.3 %collective-permute-done.9.ref = bf16[1,128,512]{2,1,0:T(8,128)(2,1)S(1)} collective-permute-done((bf16[1,128,512]{2,1,0:T(8,128)(2,1)S(1)}, bf16[1,128,512]{2,1,0:T(8,128)(2,1)S(1)}, u32[]{:S(2)}, u32[]{:S(2)}) %collective-permute-start.9) | collective-permute-done | bytes 131104 | tf_op jit(solution)/shard_map/ppermute | solution.py:18
  29.7 0.1 collective-permute-start.12
  29.8 0.0 collective-permute-done.8.refs_0_
  29.8 1.3 %collective-permute-done.12.refs_2_ = bf16[1,128,512]{2,1,0:T(8,128)(2,1)S(1)} collective-permute-done((bf16[1,128,512]{2,1,0:T(8,128)(2,1)S(1)}, bf16[1,128,512]{2,1,0:T(8,128)(2,1)S(1)}, u32[]{:S(2)}, u32[]{:S(2)}) %collective-permute-start.12) | collective-permute-done | bytes 131104 | tf_op jit(solution)/shard_map/ppermute | solution.py:18
  31.2 0.6 %shard_map.74 = bf16[16,8,896]{2,1,0:T(8,128)(2,1)S(1)} custom-call(bf16[1,128,512]{2,1,0:T(8,128)(2,1)S(1)} %collective-permute-done.8.refs_0_, bf16[1,128,512]{2,1,0:T(8,128)(2,1)S(1)} %shard_map.73.refs_1_, bf16[1,128,512]{2,1,0:T(8,128)(2,1)S(1)} %collective-permute-done.12.refs_2_, bf16[2,2048,896]{2,1,0:T(8,128)(2,1)S(1)} %bitcast.1, ...), custom_call_target="tpu_custom_call" | custom-call | flops 352321536 | bytes 2752512 | tf_op jit(solution)/shard_map/pallas_call | solution.py:194
  31.8 13.2 %all_to_all.5.in_ref = bf16[16,8,896]{2,1,0:T(8,128)(2,1)S(1)} all-to-all(bf16[16,8,896]{2,1,0:T(8,128)(2,1)S(1)} %shard_map.74), channel_id=1, replica_groups=mesh['groups'=2,'node'=4,'local'=2,'sub'=2] {'node','local','sub'}, dimensions={0} | all-to-all | bytes 458752 | tf_op jit(solution)/shard_map/all_to_all | solution.py:269
  45.0 0.7 %shard_map.75 = bf16[8,3584]{1,0:T(8,128)(2,1)} custom-call(bf16[16,8,896]{2,1,0:T(8,128)(2,1)S(1)} %all_to_all.5.in_ref), custom_call_target="tpu_custom_call" | custom-call | tf_op jit(solution)/shard_map/pallas_call | solution.py:270
  (5 shorter events, 0.1 us)
Async XLA Ops:
  0.9 10.6 %collective-permute-start.3 = (bf16[8,3712]{1,0:T(8,128)(2,1)S(1)}, bf16[8,3712]{1,0:T(8,128)(2,1)S(1)}, u32[]{:S(2)}, u32[]{:S(2)}) collective-permute-start(bf16[8,3712]{1,0:T(8,128)(2,1)S(1)} %shard_map.64.refs_1_.refs_0_), channel_id=1, source_target_pairs={{0,2},{2,0},{1,3},{3,1},{4,6},{6,4},{5,7},{7,5},{8,10},{10,8},{9,1... | collective-permute-start | bytes 178184 | tf_op jit(solution)/shard_map/ppermute | solution.py:18
  3.9 7.6 %collective-permute-start.2 = (bf16[8,3712]{1,0:T(8,128)(2,1)S(1)}, bf16[8,3712]{1,0:T(8,128)(2,1)S(1)}, u32[]{:S(2)}, u32[]{:S(2)}) collective-permute-start(bf16[8,3712]{1,0:T(8,128)(2,1)S(1)} %shard_map.64.refs_1_.refs_0_), channel_id=1, source_target_pairs={{0,12},{4,8},{8,4},{12,0},{1,13},{5,9},{9,5},{13,1},{2,14},{6,10},... | collective-permute-start | bytes 178184 | tf_op jit(solution)/shard_map/ppermute | solution.py:18
  7.5 5.1 %collective-permute-start.1 = (bf16[8,3712]{1,0:T(8,128)(2,1)S(1)}, bf16[8,3712]{1,0:T(8,128)(2,1)S(1)}, u32[]{:S(2)}, u32[]{:S(2)}) collective-permute-start(bf16[8,3712]{1,0:T(8,128)(2,1)S(1)} %shard_map.64.refs_1_.refs_0_), channel_id=1, source_target_pairs={{0,8},{4,12},{8,0},{12,4},{1,9},{5,13},{9,1},{13,5},{2,10},{6,14},... | collective-permute-start | bytes 178184 | tf_op jit(solution)/shard_map/ppermute | solution.py:18
  7.5 5.1 %collective-permute-start = (bf16[8,3712]{1,0:T(8,128)(2,1)S(1)}, bf16[8,3712]{1,0:T(8,128)(2,1)S(1)}, u32[]{:S(2)}, u32[]{:S(2)}) collective-permute-start(bf16[8,3712]{1,0:T(8,128)(2,1)S(1)} %shard_map.64.refs_1_.refs_0_), channel_id=1, source_target_pairs={{0,4},{4,0},{8,12},{12,8},{1,5},{5,1},{9,13},{13,9},{2,6},{6,2},{1... | collective-permute-start | bytes 178184 | tf_op jit(solution)/shard_map/ppermute | solution.py:18
  12.7 5.5 %collective-permute-start.4 = (bf16[24,3712]{1,0:T(8,128)(2,1)S(1)}, bf16[24,3712]{1,0:T(8,128)(2,1)S(1)}, u32[]{:S(2)}, u32[]{:S(2)}) collective-permute-start(bf16[24,3712]{1,0:T(8,128)(2,1)S(1)} %shard_map.66.refs_1_), channel_id=1, source_target_pairs={{0,2},{2,0},{1,3},{3,1},{4,6},{6,4},{5,7},{7,5},{8,10},{10,8},{9,1... | collective-permute-start | bytes 534536 | tf_op jit(solution)/shard_map/ppermute | solution.py:18
  13.3 5.0 %collective-permute-start.5 = (bf16[32,3712]{1,0:T(8,128)(2,1)S(1)}, bf16[32,3712]{1,0:T(8,128)(2,1)S(1)}, u32[]{:S(2)}, u32[]{:S(2)}) collective-permute-start(bf16[32,3712]{1,0:T(8,128)(2,1)S(1)} %shard_map.67.refs_0_), channel_id=1, source_target_pairs={{0,1},{1,0},{2,3},{3,2},{4,5},{5,4},{6,7},{7,6},{8,9},{9,8},{10,11... | collective-permute-start | bytes 712712 | tf_op jit(solution)/shard_map/ppermute | solution.py:18
  18.2 1.6 %collective-permute-start.6 = (bf16[32,3712]{1,0:T(8,128)(2,1)S(1)}, bf16[32,3712]{1,0:T(8,128)(2,1)S(1)}, u32[]{:S(2)}, u32[]{:S(2)}) collective-permute-start(bf16[32,3712]{1,0:T(8,128)(2,1)S(1)} %shard_map.69.refs_1_), channel_id=1, source_target_pairs={{0,1},{1,0},{2,3},{3,2},{4,5},{5,4},{6,7},{7,6},{8,9},{9,8},{10,11... | collective-permute-start | bytes 712712 | tf_op jit(solution)/shard_map/ppermute | solution.py:18
  19.8 7.7 %slice-start = ((s8[7340032]{0:T(1024)(128)(4,1)}), s8[4194304]{0:T(1024)(128)(4,1)S(1)}, s32[]{:S(2)}) async-start(s8[7340032]{0:T(1024)(128)(4,1)} %bitcast), calls=%async_computation.1 | async-start | bytes 8388608
  20.9 6.6 %slice-start.1 = ((s8[7340032]{0:T(1024)(128)(4,1)}), s8[3145728]{0:T(1024)(128)(4,1)S(1)}, s32[]{:S(2)}) async-start(s8[7340032]{0:T(1024)(128)(4,1)} %bitcast), calls=%async_computation.2 | async-start | bytes 6291456
  20.9 6.5 %collective-permute-start.10 = (bf16[1,128,512]{2,1,0:T(8,128)(2,1)S(1)}, bf16[1,128,512]{2,1,0:T(8,128)(2,1)S(1)}, u32[]{:S(2)}, u32[]{:S(2)}) collective-permute-start(bf16[1,128,512]{2,1,0:T(8,128)(2,1)S(1)} %shard_map.70.refs_0_), channel_id=1, source_target_pairs={{0,1},{1,0},{2,3},{3,2},{4,5},{5,4},{6,7},{7,6},{8,9},{9,8},{10,11... | collective-permute-start | bytes 393224 | tf_op jit(solution)/shard_map/ppermute | solution.py:18
  21.1 6.3 %collective-permute-start.7 = (bf16[1,128,512]{2,1,0:T(8,128)(2,1)S(1)}, bf16[1,128,512]{2,1,0:T(8,128)(2,1)S(1)}, u32[]{:S(2)}, u32[]{:S(2)}) collective-permute-start(bf16[1,128,512]{2,1,0:T(8,128)(2,1)S(1)} %shard_map.70.refs_0_), channel_id=1, source_target_pairs={{0,2},{2,0},{1,3},{3,1},{4,6},{6,4},{5,7},{7,5},{8,10},{10,8},{9,1... | collective-permute-start | bytes 393224 | tf_op jit(solution)/shard_map/ppermute | solution.py:18
  22.8 4.7 %collective-permute-start.11 = (bf16[1,128,512]{2,1,0:T(8,128)(2,1)S(1)}, bf16[1,128,512]{2,1,0:T(8,128)(2,1)S(1)}, u32[]{:S(2)}, u32[]{:S(2)}) collective-permute-start(bf16[1,128,512]{2,1,0:T(8,128)(2,1)S(1)} %shard_map.71.refs_3_), channel_id=1, source_target_pairs={{0,1},{1,0},{2,3},{3,2},{4,5},{5,4},{6,7},{7,6},{8,9},{9,8},{10,11... | collective-permute-start | bytes 393224 | tf_op jit(solution)/shard_map/ppermute | solution.py:18
  23.0 6.8 %collective-permute-start.9 = (bf16[1,128,512]{2,1,0:T(8,128)(2,1)S(1)}, bf16[1,128,512]{2,1,0:T(8,128)(2,1)S(1)}, u32[]{:S(2)}, u32[]{:S(2)}) collective-permute-start(bf16[1,128,512]{2,1,0:T(8,128)(2,1)S(1)} %shard_map.71.refs_3_), channel_id=1, source_target_pairs={{0,2},{2,0},{1,3},{3,1},{4,6},{6,4},{5,7},{7,5},{8,10},{10,8},{9,1... | collective-permute-start | bytes 393224 | tf_op jit(solution)/shard_map/ppermute | solution.py:18
  27.5 2.4 %collective-permute-start.8 = (bf16[1,128,512]{2,1,0:T(8,128)(2,1)S(1)}, bf16[1,128,512]{2,1,0:T(8,128)(2,1)S(1)}, u32[]{:S(2)}, u32[]{:S(2)}) collective-permute-start(bf16[1,128,512]{2,1,0:T(8,128)(2,1)S(1)} %collective-permute-done.7.refs_2_), channel_id=1, source_target_pairs={{0,1},{1,0},{2,3},{3,2},{4,5},{5,4},{6,7},{7,6},{8,9},{9,8},{10,11... | collective-permute-start | bytes 393224 | tf_op jit(solution)/shard_map/ppermute | solution.py:18
  29.7 1.4 %collective-permute-start.12 = (bf16[1,128,512]{2,1,0:T(8,128)(2,1)S(1)}, bf16[1,128,512]{2,1,0:T(8,128)(2,1)S(1)}, u32[]{:S(2)}, u32[]{:S(2)}) collective-permute-start(bf16[1,128,512]{2,1,0:T(8,128)(2,1)S(1)} %shard_map.73.refs_1_), channel_id=1, source_target_pairs={{0,1},{1,0},{2,3},{3,2},{4,5},{5,4},{6,7},{7,6},{8,9},{9,8},{10,11... | collective-permute-start | bytes 393224 | tf_op jit(solution)/shard_map/ppermute | solution.py:18

commit v3 on v1

v3 whole, which is shorter than its diff:
```python
import functools

import jax
import jax.numpy as jnp
from jax import lax
from jax.experimental import pallas as pl
from jax.experimental.pallas import tpu as pltpu
from jax.sharding import PartitionSpec as P

route_scale = 2.827
LANES = 128
f32, bf16 = jnp.float32, jnp.bfloat16
VMEM = pl.BlockSpec(memory_space=pltpu.VMEM)
HBM = pl.BlockSpec(memory_space=pltpu.HBM)


def swap(x, **by):
    axes = tuple(by)
    sizes = [lax.axis_size(a) for a in axes]
    pairs = []
    for i in range(functools.reduce(lambda a, b: a * b, sizes)):
        rest, at, to, stride = i, [], 0, 1
        for size, k in zip(sizes[::-1], list(by.values())[::-1]):
            to += ((rest % size) ^ k) * stride
            stride *= size
            rest //= size
        pairs.append((i, to))
    return lax.ppermute(x, axes if len(axes) > 1 else axes[0], pairs)


def in_hbm(x):
    return pltpu.with_memory_space_constraint(x, pltpu.HBM)


def call(kernel, out_shape, args, beside=(), scratch=(), spec=VMEM, flops=0, size=0, vmem=4):
    n = len(args)

    def body(*refs):
        kernel(*refs[:n], *refs[n + len(beside) :])

    return pl.pallas_call(
        body,
        out_shape=out_shape,
        in_specs=[spec] * n + [HBM] * len(beside),
        out_specs=jax.tree.map(lambda _: VMEM, out_shape),
        scratch_shapes=scratch,
        compiler_params=pltpu.CompilerParams(vmem_limit_bytes=vmem << 20),
        cost_estimate=pl.CostEstimate(flops=flops, bytes_accessed=size, transcendentals=0)
        if size
        else None,
    )(*args, *[in_hbm(b) for b in beside])


def pack_kernel(experts, tok_hbm, ids_hbm, scores_hbm, out_ref, ids_ref, scores_ref, sems):
    rows, features = tok_hbm.shape
    extra = out_ref.shape[1] - features
    pairs = ((ids_hbm, ids_ref), (scores_hbm, scores_ref), (tok_hbm, out_ref.at[:, :features]))
    copies = [pltpu.make_async_copy(a, b, sems.at[i]) for i, (a, b) in enumerate(pairs)]
    for copy in copies:
        copy.start()
    copies[0].wait()
    copies[1].wait()
    gate = 1.0 / (1.0 + jnp.exp(-scores_ref[...]))
    share = route_scale * gate / jnp.sum(gate, axis=1, keepdims=True)
    column = lax.broadcasted_iota(jnp.int32, (rows, extra), 1)
    expert, term = column % experts, column // experts
    weight = jnp.zeros((rows, extra), f32)
    for k in range(ids_ref.shape[1]):
        weight += jnp.where(ids_ref[:, k : k + 1] == expert, share[:, k : k + 1], 0.0)
    first = weight.astype(bf16).astype(f32)
    second = (weight - first).astype(bf16).astype(f32)
    third = weight - first - second
    terms = jnp.where(term == 0, first, jnp.where(term == 1, second, jnp.where(term == 2, third, 0.0)))
    out_ref[:, features:] = terms.astype(bf16)
    copies[2].wait()


def stack(parts, after=(), beside=(), order=None, cuts=((0, None),)):
    operands = [*parts, *after]
    order = list(range(len(operands))) if order is None else order
    spans = [parts[first:end] for first, end in cuts]

    def kernel(*refs):
        for (first, _), span, out in zip(cuts, spans, refs[len(operands) :]):
            at = 0
            for i in range(first, first + len(span)):
                ref = refs[order.index(i)]
                rows = ref.shape[0]
                out[at : at + rows, :] = ref[...]
                at += rows

    width, kind = parts[0].shape[1], parts[0].dtype
    shapes = [jax.ShapeDtypeStruct((sum(p.shape[0] for p in span), width), kind) for span in spans]
    out = call(kernel, shapes, [operands[i] for i in order], beside)
    return out if len(cuts) > 1 else out[0]


def hidden(blocks, gate_w, up_w, e, features):
    n = len(blocks)
    local_experts, _, depth = gate_w.shape
    count = sum(b.shape[0] for b in blocks)

    def kernel(*refs):
        *ins, gate_ref, up_ref, out_ref = refs
        experts = local_experts * lax.axis_size("node")
        x = jnp.concatenate([b[:, :features] for b in ins], axis=0)
        tail = jnp.concatenate([b[:, features:] for b in ins], axis=0).astype(f32)
        column = lax.broadcasted_iota(jnp.int32, tail.shape, 1)
        mine = lax.axis_index("node") * local_experts + e
        keep = (column % experts == mine) & (column < 3 * experts)
        weight = jnp.sum(jnp.where(keep, tail, 0.0), axis=1, keepdims=True)
        gate = jnp.dot(x, gate_ref[e], preferred_element_type=f32)
        up = jnp.dot(x, up_ref[e], preferred_element_type=f32)
        out_ref[...] = (gate / (1.0 + jnp.exp(-gate)) * up * weight).astype(bf16)

    return call(
        kernel,
        jax.ShapeDtypeStruct((count, depth), bf16),
        [*blocks, gate_w, up_w],
        flops=4 * count * features * depth,
        size=4 * features * depth,
        vmem=32 if count > 128 else 4,
    )


def down(terms, weights, last, local, sub, nodes, final):
    n_slices = local * sub
    arrays = []
    for term in terms:
        if not any(term[0] is a for a in arrays):
            arrays.append(term[0])
    index = [next(i for i, a in enumerate(arrays) if a is term[0]) for term in terms]
    depth = weights.shape[1] // n_slices
    width = weights.shape[2]
    tokens = terms[0][4]
    block = tokens // n_slices
    rows = block // nodes
    before = [] if last is None else [last]

    def kernel(*refs):
        ins, down_ref = refs[: len(arrays)], refs[len(arrays)]
        outs = refs[len(arrays) + 1 + len(before) :]
        me = lax.axis_index("local") * sub + lax.axis_index("sub")
        total = refs[len(arrays) + 1][...] if before else None
        for i, (_, at, e, r, _) in zip(index, terms):
            s, x = divmod(r, local)
            here = pl.ds(pl.multiple_of((me ^ (x * sub + s)) * depth, depth), depth)
            h = [ins[i][pl.ds(at + (b ^ r) * block, block), :] for b in range(n_slices)]
            product = jnp.dot(
                jnp.concatenate(h, axis=0), down_ref[e, here, :], preferred_element_type=f32
            )
            total = product if total is None else total + product
        if not final:
            outs[0][...] = total
            return
        for z in range(nodes):
            starts = [b * block + z * rows for b in range(n_slices)]
            outs[z][...] = jnp.concatenate([total[a : a + rows] for a in starts], axis=0).astype(bf16)

    shape = (
        [jax.ShapeDtypeStruct((n_slices * rows, width), bf16)] * nodes
        if final
        else jax.ShapeDtypeStruct((tokens, width), f32)
    )
    return call(
        kernel,
        shape,
        [*arrays, weights, *before],
        flops=2 * len(terms) * tokens * depth * width,
        size=2 * len(terms) * depth * width,
        vmem=32 if tokens > 256 else 4,
    )


def add_up(parts, rows, n_slices):
    def kernel(*refs):
        ins, outs = refs[: len(parts)], refs[len(parts) :]
        total = ins[0][...].astype(f32)
        for ref in ins[1:]:
            total += ref[...].astype(f32)
        for r, out in enumerate(outs):
            out[...] = total[r * rows : (r + 1) * rows].astype(bf16)

    shape = jax.ShapeDtypeStruct((rows, parts[0].shape[1]), bf16)
    return call(kernel, [shape] * n_slices, parts)


def place_kernel(local, sub, *refs):
    *pieces, out_ref = refs
    me = lax.axis_index("local") * sub + lax.axis_index("sub")
    width = pieces[0].shape[1]
    for r, piece in enumerate(pieces):
        s, x = divmod(r, local)
        at = pl.multiple_of((me ^ (x * sub + s)) * width, LANES)
        out_ref[:, pl.ds(at, width)] = piece[...]


def per_device(tokens, ids, scores, gate_w, up_w, down_w):
    nodes, local, sub = (lax.axis_size(a) for a in ("node", "local", "sub"))
    rows, features = tokens.shape
    local_experts, _, depth = gate_w.shape
    width = down_w.shape[2]
    experts = local_experts * nodes
    n_slices = local * sub
    extra = -(-3 * experts // LANES) * LANES
    count = n_slices * nodes * rows

    packed = call(
        functools.partial(pack_kernel, experts),
        jax.ShapeDtypeStruct((rows, features + extra), bf16),
        [in_hbm(tokens), in_hbm(ids), in_hbm(scores)],
        scratch=[
            pltpu.VMEM(ids.shape, ids.dtype),
            pltpu.VMEM(scores.shape, f32),
            pltpu.SemaphoreType.DMA((3,)),
        ],
        spec=HBM,
    )
    direct = min(1, nodes)
    over = [[packed] + [swap(packed, node=z) for z in range(1, nodes)]]
    for x in range(1, local):
        over.append([swap(packed, local=x)])
        over[x] += [swap(packed, node=z, local=x) for z in range(1, direct)]
    early = [b for x in range(1, local) for b in over[x]]
    own, rest = stack(over[0], early, (gate_w, up_w), [4, 1, 3, 2, 0] if nodes == 4 else None, ((0, None), (direct, None)))
    far = [swap(rest, local=x) for x in range(1, local)]

    blocks = [own]
    blocks += [stack(over[x] + [far[x - 1]], (), (gate_w,)) for x in range(1, local)]
    for s in range(1, sub):
        blocks += [swap(b, sub=s) for b in blocks[:local]]

    units, crossed = [], []
    for e in range(local_experts):
        h = hidden(blocks, gate_w, up_w, e, features)
        units.append(h)
        crossed.append([swap(h, local=x) for x in range(1, local)])
    e = local_experts - 1

    def terms_of(array, at, e, r):
        return [(array, at, e, r, count)]

    add = functools.partial(down, weights=down_w, local=local, sub=sub, nodes=nodes)
    parts = [(units[e], e, 0) for e in range(local_experts)]
    parts += [(c, e, x + 1) for e in range(local_experts - 1) for x, c in enumerate(crossed[e])]
    terms = [(array, 0, e, x, count) for array, e, x in parts]
    total = add(terms, last=None, final=False)
    terms = []
    for s in range(1, sub):
        for array, e, x in parts:
            terms.append((swap(array, sub=s), 0, e, s * local + x, count))
    e = local_experts - 1
    joined = stack(crossed[e], [total]) if local > 1 else None
    terms += [(joined, (x - 1) * count, e, x, count) for x in range(1, local)]
    if terms:
        total = add(terms, last=total, final=False)
    terms = []
    for s in range(1, sub):
        got = swap(joined, sub=s)
        terms += [(got, (x - 1) * count, e, s * local + x, count) for x in range(1, local)]
    sent = add(terms, last=total, final=True)

    arrived = [sent[0]] + [swap(sent[z], node=z) for z in range(1, nodes)]
    order = list(range(nodes))[::-1]
    pieces = list(add_up([arrived[z] for z in order], rows, n_slices))
    for r in range(1, n_slices):
        s, x = divmod(r, local)
        by = {a: k for a, k in (("local", x), ("sub", s)) if k}
        pieces[r] = swap(pieces[r], **by)
    if width % LANES == 0:
        shape = jax.ShapeDtypeStruct((rows, features), bf16)
        return call(functools.partial(place_kernel, local, sub), shape, pieces)
    me = lax.axis_index("local") * sub + lax.axis_index("sub")
    out = jnp.zeros((rows, features), bf16)
    for r, piece in enumerate(pieces):
        s, x = divmod(r, local)
        out = lax.dynamic_update_slice(out, piece, (0, (me ^ (x * sub + s)) * width))
    return out


def solution(mesh):
    everything = P(("groups", "node", "local", "sub"), None)
    weights = P("node", None, ("local", "sub"))
    return jax.shard_map(
        per_device,
        mesh=mesh,
        in_specs=(everything,) * 3 + (weights,) * 3,
        out_specs=everything,
        check_vma=False,
    )
```

time: 54.8 us -> 44.1 us (0.80)
  local copies, waits for them, and re-layouts: 8.38 us -> 0.02 us
  waiting for transfers between devices: 24.9 us -> 20 us
  starting transfers between devices: 16.7 us -> 18.2 us
  Pallas kernels: 4.36 us -> 5.54 us
    unnamed x14 -> x8, local copies, waits for them, and re-layouts: 8.37 us -> 0.02 us
    ppermute x18 -> x19, waiting for transfers between devices: 24.9 us -> 20 us  [swap(): return lax.ppermute(x, axes if len(axes) > 1 else axes[0], pairs)]
    ppermute x18 -> x19, starting transfers between devices: 16.7 us -> 18.2 us  [swap(): return lax.ppermute(x, axes if len(axes) > 1 else axes[0], pairs)]
    pallas_call x6 -> x11, Pallas kernels: 4.36 us -> 5.54 us  [call(): pl.pallas_call(body, out_shape=out_shape, in_specs=[spec] * n + [HBM] * l...]
  transfers between devices with their start and end apart: 18 -> 19, of which waited for: 12 -> 11; matrix products, arithmetic and copies ran while one was open for 0% -> 0% of each run, Pallas kernels for 2% -> 6%
where the time goes in v3:
time: 44.1 us; the launch traced here: 43.9 us
  waiting for transfers between devices  20 us (45%)
  starting transfers between devices  18.2 us (41%)
  Pallas kernels  5.54 us (13%)
    ppermute x19, waiting for transfers between devices, swap(): return lax.ppermute(x, axes if len(axes) > 1 else axes[0], pairs)  20 us
    ppermute x19, starting transfers between devices, swap(): return lax.ppermute(x, axes if len(axes) > 1 else axes[0], pairs)  18.2 us
    pallas_call x11, Pallas kernels, call(): pl.pallas_call(body, out_shape=out_shape, in_specs=[spec] * n + [HBM] * l...  5.54 us
  transfers between devices with their start and end apart: 19, of which 11 were waited for; matrix products, arithmetic and copies ran while one was open for 0% of the time, Pallas kernels for 6%

profile of v3, /device:TPU:0, one launch (start us, length us, event | category | flops | bytes accessed | tf_op | source)
XLA Modules:
  0.0 43.9 jit_solution(3814140182575962808)
XLA Ops:
  0.0 0.9 %shard_map.64.refs_4_ = bf16[8,3712]{1,0:T(8,128)(2,1)S(1)} custom-call(bf16[8,3584]{1,0:T(8,128)(2,1)} %refs_0_.1, s32[8,8]{1,0:T(8,128)} %refs_1_.2, f32[8,8]{1,0:T(8,128)} %refs_2_.2), custom_call_target="tpu_custom_call" | custom-call | tf_op jit(solution)/shard_map/pallas_call | solution.py:41
  0.9 4.1 %collective-permute-start.3 = (bf16[8,3712]{1,0:T(8,128)(2,1)S(1)}, bf16[8,3712]{1,0:T(8,128)(2,1)S(1)}, u32[]{:S(2)}, u32[]{:S(2)}) collective-permute-start(bf16[8,3712]{1,0:T(8,128)(2,1)S(1)} %shard_map.64.refs_4_), channel_id=1, source_target_pairs={{0,8},{4,12},{8,0},{12,4},{1,9},{5,13},{9,1},{13,5},{2,10},{6,14},... | collective-permute-start | bytes 178184 | tf_op jit(solution)/shard_map/ppermute | solution.py:28
  5.0 1.3 %collective-permute-start.2 = (bf16[8,3712]{1,0:T(8,128)(2,1)S(1)}, bf16[8,3712]{1,0:T(8,128)(2,1)S(1)}, u32[]{:S(2)}, u32[]{:S(2)}) collective-permute-start(bf16[8,3712]{1,0:T(8,128)(2,1)S(1)} %shard_map.64.refs_4_), channel_id=1, source_target_pairs={{0,12},{4,8},{8,4},{12,0},{1,13},{5,9},{9,5},{13,1},{2,14},{6,10},... | collective-permute-start | bytes 178184 | tf_op jit(solution)/shard_map/ppermute | solution.py:28
  6.4 0.2 collective-permute-start.1
  6.6 1.5 %collective-permute-start = (bf16[8,3712]{1,0:T(8,128)(2,1)S(1)}, bf16[8,3712]{1,0:T(8,128)(2,1)S(1)}, u32[]{:S(2)}, u32[]{:S(2)}) collective-permute-start(bf16[8,3712]{1,0:T(8,128)(2,1)S(1)} %shard_map.64.refs_4_), channel_id=1, source_target_pairs={{0,2},{2,0},{1,3},{3,1},{4,6},{6,4},{5,7},{7,5},{8,10},{10,8},{9,1... | collective-permute-start | bytes 178184 | tf_op jit(solution)/shard_map/ppermute | solution.py:28
  8.1 0.0 collective-permute-done.3.refs_3_
  8.1 3.0 %collective-permute-done.2.refs_2_ = bf16[8,3712]{1,0:T(8,128)(2,1)S(1)} collective-permute-done((bf16[8,3712]{1,0:T(8,128)(2,1)S(1)}, bf16[8,3712]{1,0:T(8,128)(2,1)S(1)}, u32[]{:S(2)}, u32[]{:S(2)}) %collective-permute-start.2) | collective-permute-done | bytes 59424 | tf_op jit(solution)/shard_map/ppermute | solution.py:28
  11.2 0.1 collective-permute-done.1.refs_1_
  11.2 0.0 collective-permute-done.refs_0_
  11.2 0.0 copy-start.1
  11.3 0.0 copy-start
  11.3 1.6 %collective-permute-start.4 = (bf16[24,3712]{1,0:T(8,128)(2,1)S(1)}, bf16[24,3712]{1,0:T(8,128)(2,1)S(1)}, u32[]{:S(2)}, u32[]{:S(2)}) collective-permute-start(bf16[24,3712]{1,0:T(8,128)(2,1)S(1)} %get-tuple-element.16), channel_id=1, source_target_pairs={{0,2},{2,0},{1,3},{3,1},{4,6},{6,4},{5,7},{7,5},{8,10},{10,8},{9,1... | collective-permute-start | bytes 534536 | tf_op jit(solution)/shard_map/ppermute | solution.py:28
  12.8 0.0 collective-permute-start.5
  12.8 4.0 %collective-permute-done.4.refs_1_ = bf16[24,3712]{1,0:T(8,128)(2,1)S(1)} collective-permute-done((bf16[24,3712]{1,0:T(8,128)(2,1)S(1)}, bf16[24,3712]{1,0:T(8,128)(2,1)S(1)}, u32[]{:S(2)}, u32[]{:S(2)}) %collective-permute-start.4) | collective-permute-done | bytes 178208 | tf_op jit(solution)/shard_map/ppermute | solution.py:28
  16.8 0.1 collective-permute-start.6
  16.9 0.0 collective-permute-done.5.refs_2_
  16.9 1.5 %collective-permute-done.6.refs_3_ = bf16[32,3712]{1,0:T(8,128)(2,1)S(1)} collective-permute-done((bf16[32,3712]{1,0:T(8,128)(2,1)S(1)}, bf16[32,3712]{1,0:T(8,128)(2,1)S(1)}, u32[]{:S(2)}, u32[]{:S(2)}) %collective-permute-start.6) | collective-permute-done | bytes 237600 | tf_op jit(solution)/shard_map/ppermute | solution.py:28
  18.4 0.0 copy-done.1
  18.4 0.0 copy-done
  18.4 0.0 slice-start
  18.4 1.1 %shard_map.68.refs_0_ = bf16[128,512]{1,0:T(8,128)(2,1)S(1)} custom-call(bf16[32,3712]{1,0:T(8,128)(2,1)S(1)} %get-tuple-element.15.refs_0_, bf16[32,3712]{1,0:T(8,128)(2,1)S(1)} %shard_map.66.refs_1_, bf16[32,3712]{1,0:T(8,128)(2,1)S(1)} %collective-permute-done.5.refs_2_, bf16[32,3712]{1,0:T(8,128)(2,1)S(1)} %collective-permute-done.6.refs_3_, ...), custom_call_target="tpu_custom_call" | custom-call | flops 939524096 | bytes 7340032 | tf_op jit(solution)/shard_map/pallas_call | solution.py:41
  19.5 0.0 slice-start.1
  19.6 1.6 %collective-permute-start.8 = (bf16[128,512]{1,0:T(8,128)(2,1)S(1)}, bf16[128,512]{1,0:T(8,128)(2,1)S(1)}, u32[]{:S(2)}, u32[]{:S(2)}) collective-permute-start(bf16[128,512]{1,0:T(8,128)(2,1)S(1)} %shard_map.68.refs_0_), channel_id=1, source_target_pairs={{0,2},{2,0},{1,3},{3,1},{4,6},{6,4},{5,7},{7,5},{8,10},{10,8},{9,1... | collective-permute-start | bytes 393224 | tf_op jit(solution)/shard_map/ppermute | solution.py:28
  21.1 1.1 %shard_map.67.refs_1_ = bf16[128,512]{1,0:T(8,128)(2,1)S(1)} custom-call(bf16[32,3712]{1,0:T(8,128)(2,1)S(1)} %get-tuple-element.15.refs_0_, bf16[32,3712]{1,0:T(8,128)(2,1)S(1)} %shard_map.66.refs_1_, bf16[32,3712]{1,0:T(8,128)(2,1)S(1)} %collective-permute-done.5.refs_2_, bf16[32,3712]{1,0:T(8,128)(2,1)S(1)} %collective-permute-done.6.refs_3_, ...), custom_call_target="tpu_custom_call" | custom-call | flops 939524096 | bytes 7340032 | tf_op jit(solution)/shard_map/pallas_call | solution.py:41
  22.2 0.6 %collective-permute-start.7 = (bf16[128,512]{1,0:T(8,128)(2,1)S(1)}, bf16[128,512]{1,0:T(8,128)(2,1)S(1)}, u32[]{:S(2)}, u32[]{:S(2)}) collective-permute-start(bf16[128,512]{1,0:T(8,128)(2,1)S(1)} %shard_map.67.refs_1_), channel_id=1, source_target_pairs={{0,2},{2,0},{1,3},{3,1},{4,6},{6,4},{5,7},{7,5},{8,10},{10,8},{9,1... | collective-permute-start | bytes 393224 | tf_op jit(solution)/shard_map/ppermute | solution.py:28
  22.9 0.0 collective-permute-start.11
  22.9 0.5 %collective-permute-start.10 = (bf16[128,512]{1,0:T(8,128)(2,1)S(1)}, bf16[128,512]{1,0:T(8,128)(2,1)S(1)}, u32[]{:S(2)}, u32[]{:S(2)}) collective-permute-start(bf16[128,512]{1,0:T(8,128)(2,1)S(1)} %shard_map.68.refs_0_), channel_id=1, source_target_pairs={{0,1},{1,0},{2,3},{3,2},{4,5},{5,4},{6,7},{7,6},{8,9},{9,8},{10,11... | collective-permute-start | bytes 393224 | tf_op jit(solution)/shard_map/ppermute | solution.py:28
  23.4 2.1 %collective-permute-done.8.refs_2_ = bf16[128,512]{1,0:T(8,128)(2,1)S(1)} collective-permute-done((bf16[128,512]{1,0:T(8,128)(2,1)S(1)}, bf16[128,512]{1,0:T(8,128)(2,1)S(1)}, u32[]{:S(2)}, u32[]{:S(2)}) %collective-permute-start.8) | collective-permute-done | bytes 131104 | tf_op jit(solution)/shard_map/ppermute | solution.py:28
  25.5 0.0 collective-permute-start.12
  25.5 0.0 slice-done
  25.5 0.0 slice-done.1
  25.5 0.6 %shard_map.69.refs_1_.refs_5_ = f32[128,896]{1,0:T(8,128)S(1)} custom-call(bf16[128,512]{1,0:T(8,128)(2,1)S(1)} %shard_map.68.refs_0_, bf16[128,512]{1,0:T(8,128)(2,1)S(1)} %shard_map.67.refs_1_, bf16[128,512]{1,0:T(8,128)(2,1)S(1)} %collective-permute-done.8.refs_2_, bf16[2,2048,896]{2,1,0:T(8,128)(2,1)S(1)} %bitcast.1), custom_call_target="tpu_custom_call" | custom-call | flops 352321536 | bytes 2752512 | tf_op jit(solution)/shard_map/pallas_call | solution.py:41
  26.1 1.9 %collective-permute-done.7.refs_0_ = bf16[128,512]{1,0:T(8,128)(2,1)S(1)} collective-permute-done((bf16[128,512]{1,0:T(8,128)(2,1)S(1)}, bf16[128,512]{1,0:T(8,128)(2,1)S(1)}, u32[]{:S(2)}, u32[]{:S(2)}) %collective-permute-start.7) | collective-permute-done | bytes 131104 | tf_op jit(solution)/shard_map/ppermute | solution.py:28
  28.0 0.1 collective-permute-start.9
  28.1 0.0 collective-permute-done.11.refs_1_
  28.1 0.0 collective-permute-done.10.refs_0_
  28.1 0.0 collective-permute-done.12.refs_2_
  28.1 0.7 %shard_map.71.refs_2_ = f32[128,896]{1,0:T(8,128)S(1)} custom-call(bf16[128,512]{1,0:T(8,128)(2,1)S(1)} %collective-permute-done.10.refs_0_, bf16[128,512]{1,0:T(8,128)(2,1)S(1)} %collective-permute-done.11.refs_1_, bf16[128,512]{1,0:T(8,128)(2,1)S(1)} %collective-permute-done.12.refs_2_, bf16[128,512]{1,0:T(8,128)(2,1)S(1)} %shard_map.70.refs_3_, ...), custom_call_target="tpu_custom_call" | custom-call | flops 469762048 | bytes 3670016 | tf_op jit(solution)/shard_map/pallas_call | solution.py:41
  28.8 0.6 %collective-permute-done.9.refs_0_ = bf16[128,512]{1,0:T(8,128)(2,1)S(1)} collective-permute-done((bf16[128,512]{1,0:T(8,128)(2,1)S(1)}, bf16[128,512]{1,0:T(8,128)(2,1)S(1)}, u32[]{:S(2)}, u32[]{:S(2)}) %collective-permute-start.9) | collective-permute-done | bytes 131104 | tf_op jit(solution)/shard_map/ppermute | solution.py:28
  29.4 0.3 shard_map.72
  29.7 2.8 %collective-permute-start.13 = (bf16[32,896]{1,0:T(8,128)(2,1)S(1)}, bf16[32,896]{1,0:T(8,128)(2,1)S(1)}, u32[]{:S(2)}, u32[]{:S(2)}) collective-permute-start(bf16[32,896]{1,0:T(8,128)(2,1)S(1)} %get-tuple-element.17), channel_id=1, source_target_pairs={{0,12},{4,8},{8,4},{12,0},{1,13},{5,9},{9,5},{13,1},{2,14},{6,10},... | collective-permute-start | bytes 172040 | tf_op jit(solution)/shard_map/ppermute | solution.py:28
  32.5 0.1 collective-permute-start.14
  32.7 1.5 %collective-permute-start.15 = (bf16[32,896]{1,0:T(8,128)(2,1)S(1)}, bf16[32,896]{1,0:T(8,128)(2,1)S(1)}, u32[]{:S(2)}, u32[]{:S(2)}) collective-permute-start(bf16[32,896]{1,0:T(8,128)(2,1)S(1)} %get-tuple-element.19), channel_id=1, source_target_pairs={{0,4},{4,0},{8,12},{12,8},{1,5},{5,1},{9,13},{13,9},{2,6},{6,2},{1... | collective-permute-start | bytes 172040 | tf_op jit(solution)/shard_map/ppermute | solution.py:28
  34.2 1.7 %collective-permute-done.13.refs_0_ = bf16[32,896]{1,0:T(8,128)(2,1)S(1)} collective-permute-done((bf16[32,896]{1,0:T(8,128)(2,1)S(1)}, bf16[32,896]{1,0:T(8,128)(2,1)S(1)}, u32[]{:S(2)}, u32[]{:S(2)}) %collective-permute-start.13) | collective-permute-done | bytes 57376 | tf_op jit(solution)/shard_map/ppermute | solution.py:28
  35.8 2.7 %collective-permute-done.14.refs_1_ = bf16[32,896]{1,0:T(8,128)(2,1)S(1)} collective-permute-done((bf16[32,896]{1,0:T(8,128)(2,1)S(1)}, bf16[32,896]{1,0:T(8,128)(2,1)S(1)}, u32[]{:S(2)}, u32[]{:S(2)}) %collective-permute-start.14) | collective-permute-done | bytes 57376 | tf_op jit(solution)/shard_map/ppermute | solution.py:28
  38.5 0.0 collective-permute-done.15.refs_2_
  38.6 1.6 %collective-permute-start.16 = (bf16[8,896]{1,0:T(8,128)(2,1)S(1)}, bf16[8,896]{1,0:T(8,128)(2,1)S(1)}, u32[]{:S(2)}, u32[]{:S(2)}) collective-permute-start(bf16[8,896]{1,0:T(8,128)(2,1)S(1)} %get-tuple-element.22), channel_id=1, source_target_pairs={{0,2},{2,0},{1,3},{3,1},{4,6},{6,4},{5,7},{7,5},{8,10},{10,8},{9,1... | collective-permute-start | bytes 43016 | tf_op jit(solution)/shard_map/ppermute | solution.py:28
  40.1 0.0 collective-permute-start.17
  40.1 0.6 %collective-permute-start.18 = (bf16[8,896]{1,0:T(8,128)(2,1)S(1)}, bf16[8,896]{1,0:T(8,128)(2,1)S(1)}, u32[]{:S(2)}, u32[]{:S(2)}) collective-permute-start(bf16[8,896]{1,0:T(8,128)(2,1)S(1)} %get-tuple-element.24), channel_id=1, source_target_pairs={{0,3},{1,2},{2,1},{3,0},{4,7},{5,6},{6,5},{7,4},{8,11},{9,10},{10,... | collective-permute-start | bytes 43016 | tf_op jit(solution)/shard_map/ppermute | solution.py:28
  40.8 1.6 %collective-permute-done.16.refs_1_ = bf16[8,896]{1,0:T(8,128)(2,1)S(1)} collective-permute-done((bf16[8,896]{1,0:T(8,128)(2,1)S(1)}, bf16[8,896]{1,0:T(8,128)(2,1)S(1)}, u32[]{:S(2)}, u32[]{:S(2)}) %collective-permute-start.16) | collective-permute-done | bytes 14368 | tf_op jit(solution)/shard_map/ppermute | solution.py:28
  42.3 0.0 collective-permute-done.17.refs_2_
  42.3 0.9 %collective-permute-done.18.refs_3_ = bf16[8,896]{1,0:T(8,128)(2,1)S(1)} collective-permute-done((bf16[8,896]{1,0:T(8,128)(2,1)S(1)}, bf16[8,896]{1,0:T(8,128)(2,1)S(1)}, u32[]{:S(2)}, u32[]{:S(2)}) %collective-permute-start.18) | collective-permute-done | bytes 14368 | tf_op jit(solution)/shard_map/ppermute | solution.py:28
  43.3 0.6 %shard_map.74 = bf16[8,3584]{1,0:T(8,128)(2,1)} custom-call(bf16[8,896]{1,0:T(8,128)(2,1)S(1)} %get-tuple-element.21.refs_0_, bf16[8,896]{1,0:T(8,128)(2,1)S(1)} %collective-permute-done.16.refs_1_, bf16[8,896]{1,0:T(8,128)(2,1)S(1)} %collective-permute-done.17.refs_2_, bf16[8,896]{1,0:T(8,128)(2,1)S(1)} %collective-permute-done.18.refs_3_), custom_call_target="tpu_custom_call" | custom-call | tf_op jit(solution)/shard_map/pallas_call | solution.py:41
  (5 shorter events, 0.1 us)
Async XLA Ops:
  0.9 7.2 %collective-permute-start.3 = (bf16[8,3712]{1,0:T(8,128)(2,1)S(1)}, bf16[8,3712]{1,0:T(8,128)(2,1)S(1)}, u32[]{:S(2)}, u32[]{:S(2)}) collective-permute-start(bf16[8,3712]{1,0:T(8,128)(2,1)S(1)} %shard_map.64.refs_4_), channel_id=1, source_target_pairs={{0,8},{4,12},{8,0},{12,4},{1,9},{5,13},{9,1},{13,5},{2,10},{6,14},... | collective-permute-start | bytes 178184 | tf_op jit(solution)/shard_map/ppermute | solution.py:28
  5.0 6.1 %collective-permute-start.2 = (bf16[8,3712]{1,0:T(8,128)(2,1)S(1)}, bf16[8,3712]{1,0:T(8,128)(2,1)S(1)}, u32[]{:S(2)}, u32[]{:S(2)}) collective-permute-start(bf16[8,3712]{1,0:T(8,128)(2,1)S(1)} %shard_map.64.refs_4_), channel_id=1, source_target_pairs={{0,12},{4,8},{8,4},{12,0},{1,13},{5,9},{9,5},{13,1},{2,14},{6,10},... | collective-permute-start | bytes 178184 | tf_op jit(solution)/shard_map/ppermute | solution.py:28
  6.4 4.8 %collective-permute-start.1 = (bf16[8,3712]{1,0:T(8,128)(2,1)S(1)}, bf16[8,3712]{1,0:T(8,128)(2,1)S(1)}, u32[]{:S(2)}, u32[]{:S(2)}) collective-permute-start(bf16[8,3712]{1,0:T(8,128)(2,1)S(1)} %shard_map.64.refs_4_), channel_id=1, source_target_pairs={{0,4},{4,0},{8,12},{12,8},{1,5},{5,1},{9,13},{13,9},{2,6},{6,2},{1... | collective-permute-start | bytes 178184 | tf_op jit(solution)/shard_map/ppermute | solution.py:28
  6.6 4.6 %collective-permute-start = (bf16[8,3712]{1,0:T(8,128)(2,1)S(1)}, bf16[8,3712]{1,0:T(8,128)(2,1)S(1)}, u32[]{:S(2)}, u32[]{:S(2)}) collective-permute-start(bf16[8,3712]{1,0:T(8,128)(2,1)S(1)} %shard_map.64.refs_4_), channel_id=1, source_target_pairs={{0,2},{2,0},{1,3},{3,1},{4,6},{6,4},{5,7},{7,5},{8,10},{10,8},{9,1... | collective-permute-start | bytes 178184 | tf_op jit(solution)/shard_map/ppermute | solution.py:28
  11.2 7.2 %copy-start.1 = (bf16[2,3584,512]{2,1,0:T(8,128)(2,1)S(1)}, bf16[2,3584,512]{2,1,0:T(8,128)(2,1)}, u32[]{:S(2)}) copy-start(bf16[2,3584,512]{2,1,0:T(8,128)(2,1)} %refs_5_.5) | copy-start | bytes 22020100
  11.3 7.1 %copy-start = (bf16[2,3584,512]{2,1,0:T(8,128)(2,1)S(1)}, bf16[2,3584,512]{2,1,0:T(8,128)(2,1)}, u32[]{:S(2)}) copy-start(bf16[2,3584,512]{2,1,0:T(8,128)(2,1)} %refs_4_.4) | copy-start | bytes 22020100
  11.3 5.5 %collective-permute-start.4 = (bf16[24,3712]{1,0:T(8,128)(2,1)S(1)}, bf16[24,3712]{1,0:T(8,128)(2,1)S(1)}, u32[]{:S(2)}, u32[]{:S(2)}) collective-permute-start(bf16[24,3712]{1,0:T(8,128)(2,1)S(1)} %get-tuple-element.16), channel_id=1, source_target_pairs={{0,2},{2,0},{1,3},{3,1},{4,6},{6,4},{5,7},{7,5},{8,10},{10,8},{9,1... | collective-permute-start | bytes 534536 | tf_op jit(solution)/shard_map/ppermute | solution.py:28
  12.8 4.1 %collective-permute-start.5 = (bf16[32,3712]{1,0:T(8,128)(2,1)S(1)}, bf16[32,3712]{1,0:T(8,128)(2,1)S(1)}, u32[]{:S(2)}, u32[]{:S(2)}) collective-permute-start(bf16[32,3712]{1,0:T(8,128)(2,1)S(1)} %get-tuple-element.15.refs_0_), channel_id=1, source_target_pairs={{0,1},{1,0},{2,3},{3,2},{4,5},{5,4},{6,7},{7,6},{8,9},{9,8},{10,11... | collective-permute-start | bytes 712712 | tf_op jit(solution)/shard_map/ppermute | solution.py:28
  16.8 1.6 %collective-permute-start.6 = (bf16[32,3712]{1,0:T(8,128)(2,1)S(1)}, bf16[32,3712]{1,0:T(8,128)(2,1)S(1)}, u32[]{:S(2)}, u32[]{:S(2)}) collective-permute-start(bf16[32,3712]{1,0:T(8,128)(2,1)S(1)} %shard_map.66.refs_1_), channel_id=1, source_target_pairs={{0,1},{1,0},{2,3},{3,2},{4,5},{5,4},{6,7},{7,6},{8,9},{9,8},{10,11... | collective-permute-start | bytes 712712 | tf_op jit(solution)/shard_map/ppermute | solution.py:28
  18.4 7.1 %slice-start = ((s8[7340032]{0:T(1024)(128)(4,1)}), s8[4194304]{0:T(1024)(128)(4,1)S(1)}, s32[]{:S(2)}) async-start(s8[7340032]{0:T(1024)(128)(4,1)} %bitcast), calls=%async_computation | async-start | bytes 8388608
  19.5 6.0 %slice-start.1 = ((s8[7340032]{0:T(1024)(128)(4,1)}), s8[3145728]{0:T(1024)(128)(4,1)S(1)}, s32[]{:S(2)}) async-start(s8[7340032]{0:T(1024)(128)(4,1)} %bitcast), calls=%async_computation.1 | async-start | bytes 6291456
  19.6 5.9 %collective-permute-start.8 = (bf16[128,512]{1,0:T(8,128)(2,1)S(1)}, bf16[128,512]{1,0:T(8,128)(2,1)S(1)}, u32[]{:S(2)}, u32[]{:S(2)}) collective-permute-start(bf16[128,512]{1,0:T(8,128)(2,1)S(1)} %shard_map.68.refs_0_), channel_id=1, source_target_pairs={{0,2},{2,0},{1,3},{3,1},{4,6},{6,4},{5,7},{7,5},{8,10},{10,8},{9,1... | collective-permute-start | bytes 393224 | tf_op jit(solution)/shard_map/ppermute | solution.py:28
  22.2 5.7 %collective-permute-start.7 = (bf16[128,512]{1,0:T(8,128)(2,1)S(1)}, bf16[128,512]{1,0:T(8,128)(2,1)S(1)}, u32[]{:S(2)}, u32[]{:S(2)}) collective-permute-start(bf16[128,512]{1,0:T(8,128)(2,1)S(1)} %shard_map.67.refs_1_), channel_id=1, source_target_pairs={{0,2},{2,0},{1,3},{3,1},{4,6},{6,4},{5,7},{7,5},{8,10},{10,8},{9,1... | collective-permute-start | bytes 393224 | tf_op jit(solution)/shard_map/ppermute | solution.py:28
  22.9 5.2 %collective-permute-start.11 = (bf16[128,512]{1,0:T(8,128)(2,1)S(1)}, bf16[128,512]{1,0:T(8,128)(2,1)S(1)}, u32[]{:S(2)}, u32[]{:S(2)}) collective-permute-start(bf16[128,512]{1,0:T(8,128)(2,1)S(1)} %shard_map.67.refs_1_), channel_id=1, source_target_pairs={{0,1},{1,0},{2,3},{3,2},{4,5},{5,4},{6,7},{7,6},{8,9},{9,8},{10,11... | collective-permute-start | bytes 393224 | tf_op jit(solution)/shard_map/ppermute | solution.py:28
  22.9 5.2 %collective-permute-start.10 = (bf16[128,512]{1,0:T(8,128)(2,1)S(1)}, bf16[128,512]{1,0:T(8,128)(2,1)S(1)}, u32[]{:S(2)}, u32[]{:S(2)}) collective-permute-start(bf16[128,512]{1,0:T(8,128)(2,1)S(1)} %shard_map.68.refs_0_), channel_id=1, source_target_pairs={{0,1},{1,0},{2,3},{3,2},{4,5},{5,4},{6,7},{7,6},{8,9},{9,8},{10,11... | collective-permute-start | bytes 393224 | tf_op jit(solution)/shard_map/ppermute | solution.py:28
  25.5 2.6 %collective-permute-start.12 = (bf16[128,512]{1,0:T(8,128)(2,1)S(1)}, bf16[128,512]{1,0:T(8,128)(2,1)S(1)}, u32[]{:S(2)}, u32[]{:S(2)}) collective-permute-start(bf16[128,512]{1,0:T(8,128)(2,1)S(1)} %collective-permute-done.8.refs_2_), channel_id=1, source_target_pairs={{0,1},{1,0},{2,3},{3,2},{4,5},{5,4},{6,7},{7,6},{8,9},{9,8},{10,11... | collective-permute-start | bytes 393224 | tf_op jit(solution)/shard_map/ppermute | solution.py:28
  28.0 1.4 %collective-permute-start.9 = (bf16[128,512]{1,0:T(8,128)(2,1)S(1)}, bf16[128,512]{1,0:T(8,128)(2,1)S(1)}, u32[]{:S(2)}, u32[]{:S(2)}) collective-permute-start(bf16[128,512]{1,0:T(8,128)(2,1)S(1)} %shard_map.70.refs_3_), channel_id=1, source_target_pairs={{0,1},{1,0},{2,3},{3,2},{4,5},{5,4},{6,7},{7,6},{8,9},{9,8},{10,11... | collective-permute-start | bytes 393224 | tf_op jit(solution)/shard_map/ppermute | solution.py:28
  29.7 6.1 %collective-permute-start.13 = (bf16[32,896]{1,0:T(8,128)(2,1)S(1)}, bf16[32,896]{1,0:T(8,128)(2,1)S(1)}, u32[]{:S(2)}, u32[]{:S(2)}) collective-permute-start(bf16[32,896]{1,0:T(8,128)(2,1)S(1)} %get-tuple-element.17), channel_id=1, source_target_pairs={{0,12},{4,8},{8,4},{12,0},{1,13},{5,9},{9,5},{13,1},{2,14},{6,10},... | collective-permute-start | bytes 172040 | tf_op jit(solution)/shard_map/ppermute | solution.py:28
  32.5 6.0 %collective-permute-start.14 = (bf16[32,896]{1,0:T(8,128)(2,1)S(1)}, bf16[32,896]{1,0:T(8,128)(2,1)S(1)}, u32[]{:S(2)}, u32[]{:S(2)}) collective-permute-start(bf16[32,896]{1,0:T(8,128)(2,1)S(1)} %get-tuple-element.18), channel_id=1, source_target_pairs={{0,8},{4,12},{8,0},{12,4},{1,9},{5,13},{9,1},{13,5},{2,10},{6,14},... | collective-permute-start | bytes 172040 | tf_op jit(solution)/shard_map/ppermute | solution.py:28
  32.7 5.8 %collective-permute-start.15 = (bf16[32,896]{1,0:T(8,128)(2,1)S(1)}, bf16[32,896]{1,0:T(8,128)(2,1)S(1)}, u32[]{:S(2)}, u32[]{:S(2)}) collective-permute-start(bf16[32,896]{1,0:T(8,128)(2,1)S(1)} %get-tuple-element.19), channel_id=1, source_target_pairs={{0,4},{4,0},{8,12},{12,8},{1,5},{5,1},{9,13},{13,9},{2,6},{6,2},{1... | collective-permute-start | bytes 172040 | tf_op jit(solution)/shard_map/ppermute | solution.py:28
  38.6 3.8 %collective-permute-start.16 = (bf16[8,896]{1,0:T(8,128)(2,1)S(1)}, bf16[8,896]{1,0:T(8,128)(2,1)S(1)}, u32[]{:S(2)}, u32[]{:S(2)}) collective-permute-start(bf16[8,896]{1,0:T(8,128)(2,1)S(1)} %get-tuple-element.22), channel_id=1, source_target_pairs={{0,2},{2,0},{1,3},{3,1},{4,6},{6,4},{5,7},{7,5},{8,10},{10,8},{9,1... | collective-permute-start | bytes 43016 | tf_op jit(solution)/shard_map/ppermute | solution.py:28
  40.1 2.2 %collective-permute-start.17 = (bf16[8,896]{1,0:T(8,128)(2,1)S(1)}, bf16[8,896]{1,0:T(8,128)(2,1)S(1)}, u32[]{:S(2)}, u32[]{:S(2)}) collective-permute-start(bf16[8,896]{1,0:T(8,128)(2,1)S(1)} %get-tuple-element.23), channel_id=1, source_target_pairs={{0,1},{1,0},{2,3},{3,2},{4,5},{5,4},{6,7},{7,6},{8,9},{9,8},{10,11... | collective-permute-start | bytes 43016 | tf_op jit(solution)/shard_map/ppermute | solution.py:28
  40.1 3.1 %collective-permute-start.18 = (bf16[8,896]{1,0:T(8,128)(2,1)S(1)}, bf16[8,896]{1,0:T(8,128)(2,1)S(1)}, u32[]{:S(2)}, u32[]{:S(2)}) collective-permute-start(bf16[8,896]{1,0:T(8,128)(2,1)S(1)} %get-tuple-element.24), channel_id=1, source_target_pairs={{0,3},{1,2},{2,1},{3,0},{4,7},{5,6},{6,5},{7,4},{8,11},{9,10},{10,... | collective-permute-start | bytes 43016 | tf_op jit(solution)/shard_map/ppermute | solution.py:28

commit v4 on v3

--- a/solution.py
+++ b/solution.py
@@ -185,11 +185,11 @@
     return call(kernel, [shape] * n_slices, parts)
 
 
-def place_kernel(local, sub, *refs):
+def place_kernel(local, sub, order, *refs):
     *pieces, out_ref = refs
     me = lax.axis_index("local") * sub + lax.axis_index("sub")
     width = pieces[0].shape[1]
-    for r, piece in enumerate(pieces):
+    for r, piece in zip(order, pieces):
         s, x = divmod(r, local)
         at = pl.multiple_of((me ^ (x * sub + s)) * width, LANES)
         out_ref[:, pl.ds(at, width)] = piece[...]
@@ -222,7 +222,7 @@
         over.append([swap(packed, local=x)])
         over[x] += [swap(packed, node=z, local=x) for z in range(1, direct)]
     early = [b for x in range(1, local) for b in over[x]]
-    own, rest = stack(over[0], early, (gate_w, up_w), [4, 1, 3, 2, 0] if nodes == 4 else None, ((0, None), (direct, None)))
+    own, rest = stack(over[0], early, (gate_w, up_w), [4,1,3,2,0] if nodes == 4 else None, ((0, None), (direct, None)))
     far = [swap(rest, local=x) for x in range(1, local)]
 
     blocks = [own]
@@ -261,7 +261,7 @@
     sent = add(terms, last=total, final=True)
 
     arrived = [sent[0]] + [swap(sent[z], node=z) for z in range(1, nodes)]
-    order = list(range(nodes))[::-1]
+    order = [3,1,2,0] if nodes == 4 else list(range(nodes))
     pieces = list(add_up([arrived[z] for z in order], rows, n_slices))
     for r in range(1, n_slices):
         s, x = divmod(r, local)
@@ -269,7 +269,8 @@
         pieces[r] = swap(pieces[r], **by)
     if width % LANES == 0:
         shape = jax.ShapeDtypeStruct((rows, features), bf16)
-        return call(functools.partial(place_kernel, local, sub), shape, pieces)
+        order = [0, 3, 1, 2] if n_slices == 4 else list(range(n_slices))
+        return call(functools.partial(place_kernel, local, sub, order), shape, [pieces[r] for r in order])
     me = lax.axis_index("local") * sub + lax.axis_index("sub")
     out = jnp.zeros((rows, features), bf16)
     for r, piece in enumerate(pieces):

time: 44.1 us -> 43 us (0.975)
  waiting for transfers between devices: 20 us -> 19.2 us
    ppermute x19, waiting for transfers between devices: 20 us -> 19.2 us  [swap(): return lax.ppermute(x, axes if len(axes) > 1 else axes[0], pairs)]
  transfers between devices with their start and end apart: 19 -> 19, of which waited for: 11 -> 12; matrix products, arithmetic and copies ran while one was open for 0% -> 0% of each run, Pallas kernels for 6% -> 6%
where the time goes in v4:
time: 43 us; the launch traced here: 42.9 us
  waiting for transfers between devices  19.2 us (45%)
  starting transfers between devices  17.9 us (42%)
  Pallas kernels  5.54 us (13%)
    ppermute x19, waiting for transfers between devices, swap(): return lax.ppermute(x, axes if len(axes) > 1 else axes[0], pairs)  19.2 us
    ppermute x19, starting transfers between devices, swap(): return lax.ppermute(x, axes if len(axes) > 1 else axes[0], pairs)  17.9 us
    pallas_call x11, Pallas kernels, call(): pl.pallas_call(body, out_shape=out_shape, in_specs=[spec] * n + [HBM] * l...  5.54 us
  transfers between devices with their start and end apart: 19, of which 12 were waited for; matrix products, arithmetic and copies ran while one was open for 0% of the time, Pallas kernels for 6%

profile of v4, /device:TPU:0, one launch (start us, length us, event | category | flops | bytes accessed | tf_op | source)
XLA Modules:
  0.0 42.9 jit_solution(3868040440734374900)
XLA Ops:
  0.0 0.9 %shard_map.64.refs_4_ = bf16[8,3712]{1,0:T(8,128)(2,1)S(1)} custom-call(bf16[8,3584]{1,0:T(8,128)(2,1)} %refs_0_.1, s32[8,8]{1,0:T(8,128)} %refs_1_.2, f32[8,8]{1,0:T(8,128)} %refs_2_.2), custom_call_target="tpu_custom_call" | custom-call | tf_op jit(solution)/shard_map/pallas_call | solution.py:41
  0.9 4.1 %collective-permute-start.3 = (bf16[8,3712]{1,0:T(8,128)(2,1)S(1)}, bf16[8,3712]{1,0:T(8,128)(2,1)S(1)}, u32[]{:S(2)}, u32[]{:S(2)}) collective-permute-start(bf16[8,3712]{1,0:T(8,128)(2,1)S(1)} %shard_map.64.refs_4_), channel_id=1, source_target_pairs={{0,8},{4,12},{8,0},{12,4},{1,9},{5,13},{9,1},{13,5},{2,10},{6,14},... | collective-permute-start | bytes 178184 | tf_op jit(solution)/shard_map/ppermute | solution.py:28
  5.0 1.3 %collective-permute-start.2 = (bf16[8,3712]{1,0:T(8,128)(2,1)S(1)}, bf16[8,3712]{1,0:T(8,128)(2,1)S(1)}, u32[]{:S(2)}, u32[]{:S(2)}) collective-permute-start(bf16[8,3712]{1,0:T(8,128)(2,1)S(1)} %shard_map.64.refs_4_), channel_id=1, source_target_pairs={{0,12},{4,8},{8,4},{12,0},{1,13},{5,9},{9,5},{13,1},{2,14},{6,10},... | collective-permute-start | bytes 178184 | tf_op jit(solution)/shard_map/ppermute | solution.py:28
  6.4 0.2 collective-permute-start.1
  6.6 1.5 %collective-permute-start = (bf16[8,3712]{1,0:T(8,128)(2,1)S(1)}, bf16[8,3712]{1,0:T(8,128)(2,1)S(1)}, u32[]{:S(2)}, u32[]{:S(2)}) collective-permute-start(bf16[8,3712]{1,0:T(8,128)(2,1)S(1)} %shard_map.64.refs_4_), channel_id=1, source_target_pairs={{0,2},{2,0},{1,3},{3,1},{4,6},{6,4},{5,7},{7,5},{8,10},{10,8},{9,1... | collective-permute-start | bytes 178184 | tf_op jit(solution)/shard_map/ppermute | solution.py:28
  8.1 0.0 collective-permute-done.3.refs_3_
  8.1 3.0 %collective-permute-done.2.refs_2_ = bf16[8,3712]{1,0:T(8,128)(2,1)S(1)} collective-permute-done((bf16[8,3712]{1,0:T(8,128)(2,1)S(1)}, bf16[8,3712]{1,0:T(8,128)(2,1)S(1)}, u32[]{:S(2)}, u32[]{:S(2)}) %collective-permute-start.2) | collective-permute-done | bytes 59424 | tf_op jit(solution)/shard_map/ppermute | solution.py:28
  11.2 0.1 collective-permute-done.1.refs_1_
  11.2 0.0 collective-permute-done.refs_0_
  11.2 0.0 copy-start.1
  11.3 0.0 copy-start
  11.3 1.6 %collective-permute-start.4 = (bf16[24,3712]{1,0:T(8,128)(2,1)S(1)}, bf16[24,3712]{1,0:T(8,128)(2,1)S(1)}, u32[]{:S(2)}, u32[]{:S(2)}) collective-permute-start(bf16[24,3712]{1,0:T(8,128)(2,1)S(1)} %get-tuple-element.16), channel_id=1, source_target_pairs={{0,2},{2,0},{1,3},{3,1},{4,6},{6,4},{5,7},{7,5},{8,10},{10,8},{9,1... | collective-permute-start | bytes 534536 | tf_op jit(solution)/shard_map/ppermute | solution.py:28
  12.8 0.0 collective-permute-start.5
  12.8 4.0 %collective-permute-done.4.refs_1_ = bf16[24,3712]{1,0:T(8,128)(2,1)S(1)} collective-permute-done((bf16[24,3712]{1,0:T(8,128)(2,1)S(1)}, bf16[24,3712]{1,0:T(8,128)(2,1)S(1)}, u32[]{:S(2)}, u32[]{:S(2)}) %collective-permute-start.4) | collective-permute-done | bytes 178208 | tf_op jit(solution)/shard_map/ppermute | solution.py:28
  16.8 0.1 collective-permute-start.6
  16.9 0.0 collective-permute-done.5.refs_2_
  16.9 1.5 %collective-permute-done.6.refs_3_ = bf16[32,3712]{1,0:T(8,128)(2,1)S(1)} collective-permute-done((bf16[32,3712]{1,0:T(8,128)(2,1)S(1)}, bf16[32,3712]{1,0:T(8,128)(2,1)S(1)}, u32[]{:S(2)}, u32[]{:S(2)}) %collective-permute-start.6) | collective-permute-done | bytes 237600 | tf_op jit(solution)/shard_map/ppermute | solution.py:28
  18.4 0.0 copy-done.1
  18.4 0.0 copy-done
  18.4 0.0 slice-start
  18.4 1.1 %shard_map.68.refs_0_ = bf16[128,512]{1,0:T(8,128)(2,1)S(1)} custom-call(bf16[32,3712]{1,0:T(8,128)(2,1)S(1)} %get-tuple-element.15.refs_0_, bf16[32,3712]{1,0:T(8,128)(2,1)S(1)} %shard_map.66.refs_1_, bf16[32,3712]{1,0:T(8,128)(2,1)S(1)} %collective-permute-done.5.refs_2_, bf16[32,3712]{1,0:T(8,128)(2,1)S(1)} %collective-permute-done.6.refs_3_, ...), custom_call_target="tpu_custom_call" | custom-call | flops 939524096 | bytes 7340032 | tf_op jit(solution)/shard_map/pallas_call | solution.py:41
  19.5 0.0 slice-start.1
  19.6 1.6 %collective-permute-start.8 = (bf16[128,512]{1,0:T(8,128)(2,1)S(1)}, bf16[128,512]{1,0:T(8,128)(2,1)S(1)}, u32[]{:S(2)}, u32[]{:S(2)}) collective-permute-start(bf16[128,512]{1,0:T(8,128)(2,1)S(1)} %shard_map.68.refs_0_), channel_id=1, source_target_pairs={{0,2},{2,0},{1,3},{3,1},{4,6},{6,4},{5,7},{7,5},{8,10},{10,8},{9,1... | collective-permute-start | bytes 393224 | tf_op jit(solution)/shard_map/ppermute | solution.py:28
  21.1 1.1 %shard_map.67.refs_1_ = bf16[128,512]{1,0:T(8,128)(2,1)S(1)} custom-call(bf16[32,3712]{1,0:T(8,128)(2,1)S(1)} %get-tuple-element.15.refs_0_, bf16[32,3712]{1,0:T(8,128)(2,1)S(1)} %shard_map.66.refs_1_, bf16[32,3712]{1,0:T(8,128)(2,1)S(1)} %collective-permute-done.5.refs_2_, bf16[32,3712]{1,0:T(8,128)(2,1)S(1)} %collective-permute-done.6.refs_3_, ...), custom_call_target="tpu_custom_call" | custom-call | flops 939524096 | bytes 7340032 | tf_op jit(solution)/shard_map/pallas_call | solution.py:41
  22.2 0.6 %collective-permute-start.7 = (bf16[128,512]{1,0:T(8,128)(2,1)S(1)}, bf16[128,512]{1,0:T(8,128)(2,1)S(1)}, u32[]{:S(2)}, u32[]{:S(2)}) collective-permute-start(bf16[128,512]{1,0:T(8,128)(2,1)S(1)} %shard_map.67.refs_1_), channel_id=1, source_target_pairs={{0,2},{2,0},{1,3},{3,1},{4,6},{6,4},{5,7},{7,5},{8,10},{10,8},{9,1... | collective-permute-start | bytes 393224 | tf_op jit(solution)/shard_map/ppermute | solution.py:28
  22.9 0.0 collective-permute-start.11
  22.9 0.5 %collective-permute-start.10 = (bf16[128,512]{1,0:T(8,128)(2,1)S(1)}, bf16[128,512]{1,0:T(8,128)(2,1)S(1)}, u32[]{:S(2)}, u32[]{:S(2)}) collective-permute-start(bf16[128,512]{1,0:T(8,128)(2,1)S(1)} %shard_map.68.refs_0_), channel_id=1, source_target_pairs={{0,1},{1,0},{2,3},{3,2},{4,5},{5,4},{6,7},{7,6},{8,9},{9,8},{10,11... | collective-permute-start | bytes 393224 | tf_op jit(solution)/shard_map/ppermute | solution.py:28
  23.4 2.1 %collective-permute-done.8.refs_2_ = bf16[128,512]{1,0:T(8,128)(2,1)S(1)} collective-permute-done((bf16[128,512]{1,0:T(8,128)(2,1)S(1)}, bf16[128,512]{1,0:T(8,128)(2,1)S(1)}, u32[]{:S(2)}, u32[]{:S(2)}) %collective-permute-start.8) | collective-permute-done | bytes 131104 | tf_op jit(solution)/shard_map/ppermute | solution.py:28
  25.5 0.0 collective-permute-start.12
  25.5 0.0 slice-done
  25.5 0.0 slice-done.1
  25.5 0.6 %shard_map.69.refs_1_.refs_5_ = f32[128,896]{1,0:T(8,128)S(1)} custom-call(bf16[128,512]{1,0:T(8,128)(2,1)S(1)} %shard_map.68.refs_0_, bf16[128,512]{1,0:T(8,128)(2,1)S(1)} %shard_map.67.refs_1_, bf16[128,512]{1,0:T(8,128)(2,1)S(1)} %collective-permute-done.8.refs_2_, bf16[2,2048,896]{2,1,0:T(8,128)(2,1)S(1)} %bitcast.1), custom_call_target="tpu_custom_call" | custom-call | flops 352321536 | bytes 2752512 | tf_op jit(solution)/shard_map/pallas_call | solution.py:41
  26.1 1.9 %collective-permute-done.7.refs_0_ = bf16[128,512]{1,0:T(8,128)(2,1)S(1)} collective-permute-done((bf16[128,512]{1,0:T(8,128)(2,1)S(1)}, bf16[128,512]{1,0:T(8,128)(2,1)S(1)}, u32[]{:S(2)}, u32[]{:S(2)}) %collective-permute-start.7) | collective-permute-done | bytes 131104 | tf_op jit(solution)/shard_map/ppermute | solution.py:28
  28.0 0.1 collective-permute-start.9
  28.1 0.0 collective-permute-done.11.refs_1_
  28.1 0.0 collective-permute-done.10.refs_0_
  28.1 0.0 collective-permute-done.12.refs_2_
  28.1 0.7 %shard_map.71.refs_2_ = f32[128,896]{1,0:T(8,128)S(1)} custom-call(bf16[128,512]{1,0:T(8,128)(2,1)S(1)} %collective-permute-done.10.refs_0_, bf16[128,512]{1,0:T(8,128)(2,1)S(1)} %collective-permute-done.11.refs_1_, bf16[128,512]{1,0:T(8,128)(2,1)S(1)} %collective-permute-done.12.refs_2_, bf16[128,512]{1,0:T(8,128)(2,1)S(1)} %shard_map.70.refs_3_, ...), custom_call_target="tpu_custom_call" | custom-call | flops 469762048 | bytes 3670016 | tf_op jit(solution)/shard_map/pallas_call | solution.py:41
  28.8 0.6 %collective-permute-done.9.refs_0_ = bf16[128,512]{1,0:T(8,128)(2,1)S(1)} collective-permute-done((bf16[128,512]{1,0:T(8,128)(2,1)S(1)}, bf16[128,512]{1,0:T(8,128)(2,1)S(1)}, u32[]{:S(2)}, u32[]{:S(2)}) %collective-permute-start.9) | collective-permute-done | bytes 131104 | tf_op jit(solution)/shard_map/ppermute | solution.py:28
  29.4 0.3 shard_map.72
  29.7 2.8 %collective-permute-start.13 = (bf16[32,896]{1,0:T(8,128)(2,1)S(1)}, bf16[32,896]{1,0:T(8,128)(2,1)S(1)}, u32[]{:S(2)}, u32[]{:S(2)}) collective-permute-start(bf16[32,896]{1,0:T(8,128)(2,1)S(1)} %get-tuple-element.17), channel_id=1, source_target_pairs={{0,12},{4,8},{8,4},{12,0},{1,13},{5,9},{9,5},{13,1},{2,14},{6,10},... | collective-permute-start | bytes 172040 | tf_op jit(solution)/shard_map/ppermute | solution.py:28
  32.5 0.6 %collective-permute-start.14 = (bf16[32,896]{1,0:T(8,128)(2,1)S(1)}, bf16[32,896]{1,0:T(8,128)(2,1)S(1)}, u32[]{:S(2)}, u32[]{:S(2)}) collective-permute-start(bf16[32,896]{1,0:T(8,128)(2,1)S(1)} %get-tuple-element.18), channel_id=1, source_target_pairs={{0,4},{4,0},{8,12},{12,8},{1,5},{5,1},{9,13},{13,9},{2,6},{6,2},{1... | collective-permute-start | bytes 172040 | tf_op jit(solution)/shard_map/ppermute | solution.py:28
  33.2 1.0 %collective-permute-start.15 = (bf16[32,896]{1,0:T(8,128)(2,1)S(1)}, bf16[32,896]{1,0:T(8,128)(2,1)S(1)}, u32[]{:S(2)}, u32[]{:S(2)}) collective-permute-start(bf16[32,896]{1,0:T(8,128)(2,1)S(1)} %get-tuple-element.19), channel_id=1, source_target_pairs={{0,8},{4,12},{8,0},{12,4},{1,9},{5,13},{9,1},{13,5},{2,10},{6,14},... | collective-permute-start | bytes 172040 | tf_op jit(solution)/shard_map/ppermute | solution.py:28
  34.2 2.0 %collective-permute-done.13.refs_0_ = bf16[32,896]{1,0:T(8,128)(2,1)S(1)} collective-permute-done((bf16[32,896]{1,0:T(8,128)(2,1)S(1)}, bf16[32,896]{1,0:T(8,128)(2,1)S(1)}, u32[]{:S(2)}, u32[]{:S(2)}) %collective-permute-start.13) | collective-permute-done | bytes 57376 | tf_op jit(solution)/shard_map/ppermute | solution.py:28
  36.2 1.3 %collective-permute-done.14.refs_1_ = bf16[32,896]{1,0:T(8,128)(2,1)S(1)} collective-permute-done((bf16[32,896]{1,0:T(8,128)(2,1)S(1)}, bf16[32,896]{1,0:T(8,128)(2,1)S(1)}, u32[]{:S(2)}, u32[]{:S(2)}) %collective-permute-start.14) | collective-permute-done | bytes 57376 | tf_op jit(solution)/shard_map/ppermute | solution.py:28
  37.5 0.8 %collective-permute-done.15.refs_2_ = bf16[32,896]{1,0:T(8,128)(2,1)S(1)} collective-permute-done((bf16[32,896]{1,0:T(8,128)(2,1)S(1)}, bf16[32,896]{1,0:T(8,128)(2,1)S(1)}, u32[]{:S(2)}, u32[]{:S(2)}) %collective-permute-start.15) | collective-permute-done | bytes 57376 | tf_op jit(solution)/shard_map/ppermute | solution.py:28
  38.4 0.1 collective-permute-start.16
  38.4 1.6 %collective-permute-start.17 = (bf16[8,896]{1,0:T(8,128)(2,1)S(1)}, bf16[8,896]{1,0:T(8,128)(2,1)S(1)}, u32[]{:S(2)}, u32[]{:S(2)}) collective-permute-start(bf16[8,896]{1,0:T(8,128)(2,1)S(1)} %get-tuple-element.23), channel_id=1, source_target_pairs={{0,2},{2,0},{1,3},{3,1},{4,6},{6,4},{5,7},{7,5},{8,10},{10,8},{9,1... | collective-permute-start | bytes 43016 | tf_op jit(solution)/shard_map/ppermute | solution.py:28
  40.0 0.3 collective-permute-start.18
  40.3 1.4 %collective-permute-done.16.refs_1_ = bf16[8,896]{1,0:T(8,128)(2,1)S(1)} collective-permute-done((bf16[8,896]{1,0:T(8,128)(2,1)S(1)}, bf16[8,896]{1,0:T(8,128)(2,1)S(1)}, u32[]{:S(2)}, u32[]{:S(2)}) %collective-permute-start.16) | collective-permute-done | bytes 14368 | tf_op jit(solution)/shard_map/ppermute | solution.py:28
  41.7 0.5 %collective-permute-done.17.refs_2_ = bf16[8,896]{1,0:T(8,128)(2,1)S(1)} collective-permute-done((bf16[8,896]{1,0:T(8,128)(2,1)S(1)}, bf16[8,896]{1,0:T(8,128)(2,1)S(1)}, u32[]{:S(2)}, u32[]{:S(2)}) %collective-permute-start.17) | collective-permute-done | bytes 14368 | tf_op jit(solution)/shard_map/ppermute | solution.py:28
  42.2 0.0 collective-permute-done.18.refs_3_
  42.2 0.6 %shard_map.74 = bf16[8,3584]{1,0:T(8,128)(2,1)} custom-call(bf16[8,896]{1,0:T(8,128)(2,1)S(1)} %get-tuple-element.21.refs_0_, bf16[8,896]{1,0:T(8,128)(2,1)S(1)} %collective-permute-done.16.refs_1_, bf16[8,896]{1,0:T(8,128)(2,1)S(1)} %collective-permute-done.17.refs_2_, bf16[8,896]{1,0:T(8,128)(2,1)S(1)} %collective-permute-done.18.refs_3_), custom_call_target="tpu_custom_call" | custom-call | tf_op jit(solution)/shard_map/pallas_call | solution.py:41
  (5 shorter events, 0.1 us)
Async XLA Ops:
  0.9 7.2 %collective-permute-start.3 = (bf16[8,3712]{1,0:T(8,128)(2,1)S(1)}, bf16[8,3712]{1,0:T(8,128)(2,1)S(1)}, u32[]{:S(2)}, u32[]{:S(2)}) collective-permute-start(bf16[8,3712]{1,0:T(8,128)(2,1)S(1)} %shard_map.64.refs_4_), channel_id=1, source_target_pairs={{0,8},{4,12},{8,0},{12,4},{1,9},{5,13},{9,1},{13,5},{2,10},{6,14},... | collective-permute-start | bytes 178184 | tf_op jit(solution)/shard_map/ppermute | solution.py:28
  5.0 6.1 %collective-permute-start.2 = (bf16[8,3712]{1,0:T(8,128)(2,1)S(1)}, bf16[8,3712]{1,0:T(8,128)(2,1)S(1)}, u32[]{:S(2)}, u32[]{:S(2)}) collective-permute-start(bf16[8,3712]{1,0:T(8,128)(2,1)S(1)} %shard_map.64.refs_4_), channel_id=1, source_target_pairs={{0,12},{4,8},{8,4},{12,0},{1,13},{5,9},{9,5},{13,1},{2,14},{6,10},... | collective-permute-start | bytes 178184 | tf_op jit(solution)/shard_map/ppermute | solution.py:28
  6.4 4.8 %collective-permute-start.1 = (bf16[8,3712]{1,0:T(8,128)(2,1)S(1)}, bf16[8,3712]{1,0:T(8,128)(2,1)S(1)}, u32[]{:S(2)}, u32[]{:S(2)}) collective-permute-start(bf16[8,3712]{1,0:T(8,128)(2,1)S(1)} %shard_map.64.refs_4_), channel_id=1, source_target_pairs={{0,4},{4,0},{8,12},{12,8},{1,5},{5,1},{9,13},{13,9},{2,6},{6,2},{1... | collective-permute-start | bytes 178184 | tf_op jit(solution)/shard_map/ppermute | solution.py:28
  6.6 4.6 %collective-permute-start = (bf16[8,3712]{1,0:T(8,128)(2,1)S(1)}, bf16[8,3712]{1,0:T(8,128)(2,1)S(1)}, u32[]{:S(2)}, u32[]{:S(2)}) collective-permute-start(bf16[8,3712]{1,0:T(8,128)(2,1)S(1)} %shard_map.64.refs_4_), channel_id=1, source_target_pairs={{0,2},{2,0},{1,3},{3,1},{4,6},{6,4},{5,7},{7,5},{8,10},{10,8},{9,1... | collective-permute-start | bytes 178184 | tf_op jit(solution)/shard_map/ppermute | solution.py:28
  11.2 7.2 %copy-start.1 = (bf16[2,3584,512]{2,1,0:T(8,128)(2,1)S(1)}, bf16[2,3584,512]{2,1,0:T(8,128)(2,1)}, u32[]{:S(2)}) copy-start(bf16[2,3584,512]{2,1,0:T(8,128)(2,1)} %refs_5_.5) | copy-start | bytes 22020100
  11.3 7.1 %copy-start = (bf16[2,3584,512]{2,1,0:T(8,128)(2,1)S(1)}, bf16[2,3584,512]{2,1,0:T(8,128)(2,1)}, u32[]{:S(2)}) copy-start(bf16[2,3584,512]{2,1,0:T(8,128)(2,1)} %refs_4_.4) | copy-start | bytes 22020100
  11.3 5.5 %collective-permute-start.4 = (bf16[24,3712]{1,0:T(8,128)(2,1)S(1)}, bf16[24,3712]{1,0:T(8,128)(2,1)S(1)}, u32[]{:S(2)}, u32[]{:S(2)}) collective-permute-start(bf16[24,3712]{1,0:T(8,128)(2,1)S(1)} %get-tuple-element.16), channel_id=1, source_target_pairs={{0,2},{2,0},{1,3},{3,1},{4,6},{6,4},{5,7},{7,5},{8,10},{10,8},{9,1... | collective-permute-start | bytes 534536 | tf_op jit(solution)/shard_map/ppermute | solution.py:28
  12.8 4.1 %collective-permute-start.5 = (bf16[32,3712]{1,0:T(8,128)(2,1)S(1)}, bf16[32,3712]{1,0:T(8,128)(2,1)S(1)}, u32[]{:S(2)}, u32[]{:S(2)}) collective-permute-start(bf16[32,3712]{1,0:T(8,128)(2,1)S(1)} %get-tuple-element.15.refs_0_), channel_id=1, source_target_pairs={{0,1},{1,0},{2,3},{3,2},{4,5},{5,4},{6,7},{7,6},{8,9},{9,8},{10,11... | collective-permute-start | bytes 712712 | tf_op jit(solution)/shard_map/ppermute | solution.py:28
  16.8 1.6 %collective-permute-start.6 = (bf16[32,3712]{1,0:T(8,128)(2,1)S(1)}, bf16[32,3712]{1,0:T(8,128)(2,1)S(1)}, u32[]{:S(2)}, u32[]{:S(2)}) collective-permute-start(bf16[32,3712]{1,0:T(8,128)(2,1)S(1)} %shard_map.66.refs_1_), channel_id=1, source_target_pairs={{0,1},{1,0},{2,3},{3,2},{4,5},{5,4},{6,7},{7,6},{8,9},{9,8},{10,11... | collective-permute-start | bytes 712712 | tf_op jit(solution)/shard_map/ppermute | solution.py:28
  18.4 7.1 %slice-start = ((s8[7340032]{0:T(1024)(128)(4,1)}), s8[4194304]{0:T(1024)(128)(4,1)S(1)}, s32[]{:S(2)}) async-start(s8[7340032]{0:T(1024)(128)(4,1)} %bitcast), calls=%async_computation | async-start | bytes 8388608
  19.5 6.0 %slice-start.1 = ((s8[7340032]{0:T(1024)(128)(4,1)}), s8[3145728]{0:T(1024)(128)(4,1)S(1)}, s32[]{:S(2)}) async-start(s8[7340032]{0:T(1024)(128)(4,1)} %bitcast), calls=%async_computation.1 | async-start | bytes 6291456
  19.6 5.9 %collective-permute-start.8 = (bf16[128,512]{1,0:T(8,128)(2,1)S(1)}, bf16[128,512]{1,0:T(8,128)(2,1)S(1)}, u32[]{:S(2)}, u32[]{:S(2)}) collective-permute-start(bf16[128,512]{1,0:T(8,128)(2,1)S(1)} %shard_map.68.refs_0_), channel_id=1, source_target_pairs={{0,2},{2,0},{1,3},{3,1},{4,6},{6,4},{5,7},{7,5},{8,10},{10,8},{9,1... | collective-permute-start | bytes 393224 | tf_op jit(solution)/shard_map/ppermute | solution.py:28
  22.2 5.7 %collective-permute-start.7 = (bf16[128,512]{1,0:T(8,128)(2,1)S(1)}, bf16[128,512]{1,0:T(8,128)(2,1)S(1)}, u32[]{:S(2)}, u32[]{:S(2)}) collective-permute-start(bf16[128,512]{1,0:T(8,128)(2,1)S(1)} %shard_map.67.refs_1_), channel_id=1, source_target_pairs={{0,2},{2,0},{1,3},{3,1},{4,6},{6,4},{5,7},{7,5},{8,10},{10,8},{9,1... | collective-permute-start | bytes 393224 | tf_op jit(solution)/shard_map/ppermute | solution.py:28
  22.9 5.2 %collective-permute-start.11 = (bf16[128,512]{1,0:T(8,128)(2,1)S(1)}, bf16[128,512]{1,0:T(8,128)(2,1)S(1)}, u32[]{:S(2)}, u32[]{:S(2)}) collective-permute-start(bf16[128,512]{1,0:T(8,128)(2,1)S(1)} %shard_map.67.refs_1_), channel_id=1, source_target_pairs={{0,1},{1,0},{2,3},{3,2},{4,5},{5,4},{6,7},{7,6},{8,9},{9,8},{10,11... | collective-permute-start | bytes 393224 | tf_op jit(solution)/shard_map/ppermute | solution.py:28
  22.9 5.2 %collective-permute-start.10 = (bf16[128,512]{1,0:T(8,128)(2,1)S(1)}, bf16[128,512]{1,0:T(8,128)(2,1)S(1)}, u32[]{:S(2)}, u32[]{:S(2)}) collective-permute-start(bf16[128,512]{1,0:T(8,128)(2,1)S(1)} %shard_map.68.refs_0_), channel_id=1, source_target_pairs={{0,1},{1,0},{2,3},{3,2},{4,5},{5,4},{6,7},{7,6},{8,9},{9,8},{10,11... | collective-permute-start | bytes 393224 | tf_op jit(solution)/shard_map/ppermute | solution.py:28
  25.5 2.6 %collective-permute-start.12 = (bf16[128,512]{1,0:T(8,128)(2,1)S(1)}, bf16[128,512]{1,0:T(8,128)(2,1)S(1)}, u32[]{:S(2)}, u32[]{:S(2)}) collective-permute-start(bf16[128,512]{1,0:T(8,128)(2,1)S(1)} %collective-permute-done.8.refs_2_), channel_id=1, source_target_pairs={{0,1},{1,0},{2,3},{3,2},{4,5},{5,4},{6,7},{7,6},{8,9},{9,8},{10,11... | collective-permute-start | bytes 393224 | tf_op jit(solution)/shard_map/ppermute | solution.py:28
  28.0 1.4 %collective-permute-start.9 = (bf16[128,512]{1,0:T(8,128)(2,1)S(1)}, bf16[128,512]{1,0:T(8,128)(2,1)S(1)}, u32[]{:S(2)}, u32[]{:S(2)}) collective-permute-start(bf16[128,512]{1,0:T(8,128)(2,1)S(1)} %shard_map.70.refs_3_), channel_id=1, source_target_pairs={{0,1},{1,0},{2,3},{3,2},{4,5},{5,4},{6,7},{7,6},{8,9},{9,8},{10,11... | collective-permute-start | bytes 393224 | tf_op jit(solution)/shard_map/ppermute | solution.py:28
  29.7 6.5 %collective-permute-start.13 = (bf16[32,896]{1,0:T(8,128)(2,1)S(1)}, bf16[32,896]{1,0:T(8,128)(2,1)S(1)}, u32[]{:S(2)}, u32[]{:S(2)}) collective-permute-start(bf16[32,896]{1,0:T(8,128)(2,1)S(1)} %get-tuple-element.17), channel_id=1, source_target_pairs={{0,12},{4,8},{8,4},{12,0},{1,13},{5,9},{9,5},{13,1},{2,14},{6,10},... | collective-permute-start | bytes 172040 | tf_op jit(solution)/shard_map/ppermute | solution.py:28
  32.5 4.9 %collective-permute-start.14 = (bf16[32,896]{1,0:T(8,128)(2,1)S(1)}, bf16[32,896]{1,0:T(8,128)(2,1)S(1)}, u32[]{:S(2)}, u32[]{:S(2)}) collective-permute-start(bf16[32,896]{1,0:T(8,128)(2,1)S(1)} %get-tuple-element.18), channel_id=1, source_target_pairs={{0,4},{4,0},{8,12},{12,8},{1,5},{5,1},{9,13},{13,9},{2,6},{6,2},{1... | collective-permute-start | bytes 172040 | tf_op jit(solution)/shard_map/ppermute | solution.py:28
  33.2 5.2 %collective-permute-start.15 = (bf16[32,896]{1,0:T(8,128)(2,1)S(1)}, bf16[32,896]{1,0:T(8,128)(2,1)S(1)}, u32[]{:S(2)}, u32[]{:S(2)}) collective-permute-start(bf16[32,896]{1,0:T(8,128)(2,1)S(1)} %get-tuple-element.19), channel_id=1, source_target_pairs={{0,8},{4,12},{8,0},{12,4},{1,9},{5,13},{9,1},{13,5},{2,10},{6,14},... | collective-permute-start | bytes 172040 | tf_op jit(solution)/shard_map/ppermute | solution.py:28
  38.4 3.3 %collective-permute-start.16 = (bf16[8,896]{1,0:T(8,128)(2,1)S(1)}, bf16[8,896]{1,0:T(8,128)(2,1)S(1)}, u32[]{:S(2)}, u32[]{:S(2)}) collective-permute-start(bf16[8,896]{1,0:T(8,128)(2,1)S(1)} %get-tuple-element.22), channel_id=1, source_target_pairs={{0,3},{1,2},{2,1},{3,0},{4,7},{5,6},{6,5},{7,4},{8,11},{9,10},{10,... | collective-permute-start | bytes 43016 | tf_op jit(solution)/shard_map/ppermute | solution.py:28
  38.4 3.8 %collective-permute-start.17 = (bf16[8,896]{1,0:T(8,128)(2,1)S(1)}, bf16[8,896]{1,0:T(8,128)(2,1)S(1)}, u32[]{:S(2)}, u32[]{:S(2)}) collective-permute-start(bf16[8,896]{1,0:T(8,128)(2,1)S(1)} %get-tuple-element.23), channel_id=1, source_target_pairs={{0,2},{2,0},{1,3},{3,1},{4,6},{6,4},{5,7},{7,5},{8,10},{10,8},{9,1... | collective-permute-start | bytes 43016 | tf_op jit(solution)/shard_map/ppermute | solution.py:28
  40.0 2.2 %collective-permute-start.18 = (bf16[8,896]{1,0:T(8,128)(2,1)S(1)}, bf16[8,896]{1,0:T(8,128)(2,1)S(1)}, u32[]{:S(2)}, u32[]{:S(2)}) collective-permute-start(bf16[8,896]{1,0:T(8,128)(2,1)S(1)} %get-tuple-element.24), channel_id=1, source_target_pairs={{0,1},{1,0},{2,3},{3,2},{4,5},{5,4},{6,7},{7,6},{8,9},{9,8},{10,11... | collective-permute-start | bytes 43016 | tf_op jit(solution)/shard_map/ppermute | solution.py:28

commit v5 on v4

--- a/solution.py
+++ b/solution.py
@@ -123,7 +123,7 @@
     )
 
 
-def down(terms, weights, last, local, sub, nodes, final):
+def down(terms, weights, last, tokens, local, sub, nodes, final):
     n_slices = local * sub
     arrays = []
     for term in terms:
@@ -132,7 +132,6 @@
     index = [next(i for i, a in enumerate(arrays) if a is term[0]) for term in terms]
     depth = weights.shape[1] // n_slices
     width = weights.shape[2]
-    tokens = terms[0][4]
     block = tokens // n_slices
     rows = block // nodes
     before = [] if last is None else [last]
@@ -142,7 +141,7 @@
         outs = refs[len(arrays) + 1 + len(before) :]
         me = lax.axis_index("local") * sub + lax.axis_index("sub")
         total = refs[len(arrays) + 1][...] if before else None
-        for i, (_, at, e, r, _) in zip(index, terms):
+        for i, (_, at, e, r) in zip(index, terms):
             s, x = divmod(r, local)
             here = pl.ds(pl.multiple_of((me ^ (x * sub + s)) * depth, depth), depth)
             h = [ins[i][pl.ds(at + (b ^ r) * block, block), :] for b in range(n_slices)]
@@ -216,17 +215,13 @@
         ],
         spec=HBM,
     )
-    direct = min(1, nodes)
-    over = [[packed] + [swap(packed, node=z) for z in range(1, nodes)]]
-    for x in range(1, local):
-        over.append([swap(packed, local=x)])
-        over[x] += [swap(packed, node=z, local=x) for z in range(1, direct)]
-    early = [b for x in range(1, local) for b in over[x]]
-    own, rest = stack(over[0], early, (gate_w, up_w), [4,1,3,2,0] if nodes == 4 else None, ((0, None), (direct, None)))
+    early = [swap(packed, local=x) for x in range(1, local)]
+    column = [packed] + [swap(packed, node=z) for z in range(1, nodes)]
+    order = [4, 1, 3, 2, 0] if nodes == 4 and local == 2 else None
+    own, rest = stack(column, early, (gate_w, up_w), order, ((0, None), (1, None)))
     far = [swap(rest, local=x) for x in range(1, local)]
 
-    blocks = [own]
-    blocks += [stack(over[x] + [far[x - 1]], (), (gate_w,)) for x in range(1, local)]
+    blocks = [own] + [stack(pair, (), (gate_w,)) for pair in zip(early, far)]
     for s in range(1, sub):
         blocks += [swap(b, sub=s) for b in blocks[:local]]
 
@@ -235,33 +230,30 @@
         h = hidden(blocks, gate_w, up_w, e, features)
         units.append(h)
         crossed.append([swap(h, local=x) for x in range(1, local)])
-    e = local_experts - 1
-
-    def terms_of(array, at, e, r):
-        return [(array, at, e, r, count)]
-
-    add = functools.partial(down, weights=down_w, local=local, sub=sub, nodes=nodes)
-    parts = [(units[e], e, 0) for e in range(local_experts)]
-    parts += [(c, e, x + 1) for e in range(local_experts - 1) for x, c in enumerate(crossed[e])]
-    terms = [(array, 0, e, x, count) for array, e, x in parts]
-    total = add(terms, last=None, final=False)
-    terms = []
-    for s in range(1, sub):
-        for array, e, x in parts:
-            terms.append((swap(array, sub=s), 0, e, s * local + x, count))
-    e = local_experts - 1
-    joined = stack(crossed[e], [total]) if local > 1 else None
-    terms += [(joined, (x - 1) * count, e, x, count) for x in range(1, local)]
-    if terms:
-        total = add(terms, last=total, final=False)
-    terms = []
-    for s in range(1, sub):
-        got = swap(joined, sub=s)
-        terms += [(got, (x - 1) * count, e, s * local + x, count) for x in range(1, local)]
-    sent = add(terms, last=total, final=True)
+
+    add = functools.partial(
+        down, weights=down_w, tokens=count, local=local, sub=sub, nodes=nodes
+    )
+    last = local_experts - 1
+    parts = [(units[e], 0, e, 0) for e in range(local_experts)]
+    parts += [(c, 0, e, x + 1) for e in range(last) for x, c in enumerate(crossed[e])]
+    total = add(parts, last=None, final=False)
+    passed = [
+        (swap(array, sub=s), 0, e, s * local + x) for s in range(1, sub) for array, _, e, x in parts
+    ]
+    joined = stack(crossed[last], [total])
+    ends = [(joined, (x - 1) * count, last, x) for x in range(1, local)]
+    total = add(passed + ends, last=total, final=False)
+    ends = [
+        (got, at, e, s * local + x)
+        for s in range(1, sub)
+        for got in [swap(joined, sub=s)]
+        for _, at, e, x in ends
+    ]
+    sent = add(ends, last=total, final=True)
 
     arrived = [sent[0]] + [swap(sent[z], node=z) for z in range(1, nodes)]
-    order = [3,1,2,0] if nodes == 4 else list(range(nodes))
+    order = [3, 1, 2, 0] if nodes == 4 else range(nodes)
     pieces = list(add_up([arrived[z] for z in order], rows, n_slices))
     for r in range(1, n_slices):
         s, x = divmod(r, local)
@@ -269,8 +261,9 @@
         pieces[r] = swap(pieces[r], **by)
     if width % LANES == 0:
         shape = jax.ShapeDtypeStruct((rows, features), bf16)
-        order = [0, 3, 1, 2] if n_slices == 4 else list(range(n_slices))
-        return call(functools.partial(place_kernel, local, sub, order), shape, [pieces[r] for r in order])
+        order = [0, 3, 1, 2] if n_slices == 4 else range(n_slices)
+        kernel = functools.partial(place_kernel, local, sub, order)
+        return call(kernel, shape, [pieces[r] for r in order])
     me = lax.axis_index("local") * sub + lax.axis_index("sub")
     out = jnp.zeros((rows, features), bf16)
     for r, piece in enumerate(pieces):

time: 43 us -> 43 us (level)
  no operation moved by 1% of the time
where the time goes in v5:
time: 43 us; the launch traced here: 42.9 us
  waiting for transfers between devices  19.2 us (45%)
  starting transfers between devices  17.9 us (42%)
  Pallas kernels  5.54 us (13%)
    ppermute x19, waiting for transfers between devices, swap(): return lax.ppermute(x, axes if len(axes) > 1 else axes[0], pairs)  19.2 us
    ppermute x19, starting transfers between devices, swap(): return lax.ppermute(x, axes if len(axes) > 1 else axes[0], pairs)  17.9 us
    pallas_call x11, Pallas kernels, call(): pl.pallas_call(body, out_shape=out_shape, in_specs=[spec] * n + [HBM] * l...  5.54 us
  transfers between devices with their start and end apart: 19, of which 12 were waited for; matrix products, arithmetic and copies ran while one was open for 0% of the time, Pallas kernels for 6%

profile of v5, /device:TPU:0, one launch (start us, length us, event | category | flops | bytes accessed | tf_op | source)
XLA Modules:
  0.0 42.9 jit_solution(3868040440734374900)
XLA Ops:
  0.0 0.9 %shard_map.64.refs_4_ = bf16[8,3712]{1,0:T(8,128)(2,1)S(1)} custom-call(bf16[8,3584]{1,0:T(8,128)(2,1)} %refs_0_.1, s32[8,8]{1,0:T(8,128)} %refs_1_.2, f32[8,8]{1,0:T(8,128)} %refs_2_.2), custom_call_target="tpu_custom_call" | custom-call | tf_op jit(solution)/shard_map/pallas_call | solution.py:41
  0.9 4.1 %collective-permute-start.3 = (bf16[8,3712]{1,0:T(8,128)(2,1)S(1)}, bf16[8,3712]{1,0:T(8,128)(2,1)S(1)}, u32[]{:S(2)}, u32[]{:S(2)}) collective-permute-start(bf16[8,3712]{1,0:T(8,128)(2,1)S(1)} %shard_map.64.refs_4_), channel_id=1, source_target_pairs={{0,8},{4,12},{8,0},{12,4},{1,9},{5,13},{9,1},{13,5},{2,10},{6,14},... | collective-permute-start | bytes 178184 | tf_op jit(solution)/shard_map/ppermute | solution.py:28
  5.0 1.3 %collective-permute-start.2 = (bf16[8,3712]{1,0:T(8,128)(2,1)S(1)}, bf16[8,3712]{1,0:T(8,128)(2,1)S(1)}, u32[]{:S(2)}, u32[]{:S(2)}) collective-permute-start(bf16[8,3712]{1,0:T(8,128)(2,1)S(1)} %shard_map.64.refs_4_), channel_id=1, source_target_pairs={{0,12},{4,8},{8,4},{12,0},{1,13},{5,9},{9,5},{13,1},{2,14},{6,10},... | collective-permute-start | bytes 178184 | tf_op jit(solution)/shard_map/ppermute | solution.py:28
  6.4 0.2 collective-permute-start.1
  6.6 1.5 %collective-permute-start = (bf16[8,3712]{1,0:T(8,128)(2,1)S(1)}, bf16[8,3712]{1,0:T(8,128)(2,1)S(1)}, u32[]{:S(2)}, u32[]{:S(2)}) collective-permute-start(bf16[8,3712]{1,0:T(8,128)(2,1)S(1)} %shard_map.64.refs_4_), channel_id=1, source_target_pairs={{0,2},{2,0},{1,3},{3,1},{4,6},{6,4},{5,7},{7,5},{8,10},{10,8},{9,1... | collective-permute-start | bytes 178184 | tf_op jit(solution)/shard_map/ppermute | solution.py:28
  8.1 0.0 collective-permute-done.3.refs_3_
  8.1 3.0 %collective-permute-done.2.refs_2_ = bf16[8,3712]{1,0:T(8,128)(2,1)S(1)} collective-permute-done((bf16[8,3712]{1,0:T(8,128)(2,1)S(1)}, bf16[8,3712]{1,0:T(8,128)(2,1)S(1)}, u32[]{:S(2)}, u32[]{:S(2)}) %collective-permute-start.2) | collective-permute-done | bytes 59424 | tf_op jit(solution)/shard_map/ppermute | solution.py:28
  11.2 0.1 collective-permute-done.1.refs_1_
  11.2 0.0 collective-permute-done.refs_0_
  11.2 0.0 copy-start.1
  11.3 0.0 copy-start
  11.3 1.6 %collective-permute-start.4 = (bf16[24,3712]{1,0:T(8,128)(2,1)S(1)}, bf16[24,3712]{1,0:T(8,128)(2,1)S(1)}, u32[]{:S(2)}, u32[]{:S(2)}) collective-permute-start(bf16[24,3712]{1,0:T(8,128)(2,1)S(1)} %get-tuple-element.16), channel_id=1, source_target_pairs={{0,2},{2,0},{1,3},{3,1},{4,6},{6,4},{5,7},{7,5},{8,10},{10,8},{9,1... | collective-permute-start | bytes 534536 | tf_op jit(solution)/shard_map/ppermute | solution.py:28
  12.8 0.0 collective-permute-start.5
  12.8 4.0 %collective-permute-done.4.refs_1_ = bf16[24,3712]{1,0:T(8,128)(2,1)S(1)} collective-permute-done((bf16[24,3712]{1,0:T(8,128)(2,1)S(1)}, bf16[24,3712]{1,0:T(8,128)(2,1)S(1)}, u32[]{:S(2)}, u32[]{:S(2)}) %collective-permute-start.4) | collective-permute-done | bytes 178208 | tf_op jit(solution)/shard_map/ppermute | solution.py:28
  16.8 0.1 collective-permute-start.6
  16.9 0.0 collective-permute-done.5.refs_2_
  16.9 1.5 %collective-permute-done.6.refs_3_ = bf16[32,3712]{1,0:T(8,128)(2,1)S(1)} collective-permute-done((bf16[32,3712]{1,0:T(8,128)(2,1)S(1)}, bf16[32,3712]{1,0:T(8,128)(2,1)S(1)}, u32[]{:S(2)}, u32[]{:S(2)}) %collective-permute-start.6) | collective-permute-done | bytes 237600 | tf_op jit(solution)/shard_map/ppermute | solution.py:28
  18.4 0.0 copy-done.1
  18.4 0.0 copy-done
  18.4 0.0 slice-start
  18.4 1.1 %shard_map.68.refs_0_ = bf16[128,512]{1,0:T(8,128)(2,1)S(1)} custom-call(bf16[32,3712]{1,0:T(8,128)(2,1)S(1)} %get-tuple-element.15.refs_0_, bf16[32,3712]{1,0:T(8,128)(2,1)S(1)} %shard_map.66.refs_1_, bf16[32,3712]{1,0:T(8,128)(2,1)S(1)} %collective-permute-done.5.refs_2_, bf16[32,3712]{1,0:T(8,128)(2,1)S(1)} %collective-permute-done.6.refs_3_, ...), custom_call_target="tpu_custom_call" | custom-call | flops 939524096 | bytes 7340032 | tf_op jit(solution)/shard_map/pallas_call | solution.py:41
  19.5 0.0 slice-start.1
  19.6 1.6 %collective-permute-start.8 = (bf16[128,512]{1,0:T(8,128)(2,1)S(1)}, bf16[128,512]{1,0:T(8,128)(2,1)S(1)}, u32[]{:S(2)}, u32[]{:S(2)}) collective-permute-start(bf16[128,512]{1,0:T(8,128)(2,1)S(1)} %shard_map.68.refs_0_), channel_id=1, source_target_pairs={{0,2},{2,0},{1,3},{3,1},{4,6},{6,4},{5,7},{7,5},{8,10},{10,8},{9,1... | collective-permute-start | bytes 393224 | tf_op jit(solution)/shard_map/ppermute | solution.py:28
  21.1 1.1 %shard_map.67.refs_1_ = bf16[128,512]{1,0:T(8,128)(2,1)S(1)} custom-call(bf16[32,3712]{1,0:T(8,128)(2,1)S(1)} %get-tuple-element.15.refs_0_, bf16[32,3712]{1,0:T(8,128)(2,1)S(1)} %shard_map.66.refs_1_, bf16[32,3712]{1,0:T(8,128)(2,1)S(1)} %collective-permute-done.5.refs_2_, bf16[32,3712]{1,0:T(8,128)(2,1)S(1)} %collective-permute-done.6.refs_3_, ...), custom_call_target="tpu_custom_call" | custom-call | flops 939524096 | bytes 7340032 | tf_op jit(solution)/shard_map/pallas_call | solution.py:41
  22.2 0.6 %collective-permute-start.7 = (bf16[128,512]{1,0:T(8,128)(2,1)S(1)}, bf16[128,512]{1,0:T(8,128)(2,1)S(1)}, u32[]{:S(2)}, u32[]{:S(2)}) collective-permute-start(bf16[128,512]{1,0:T(8,128)(2,1)S(1)} %shard_map.67.refs_1_), channel_id=1, source_target_pairs={{0,2},{2,0},{1,3},{3,1},{4,6},{6,4},{5,7},{7,5},{8,10},{10,8},{9,1... | collective-permute-start | bytes 393224 | tf_op jit(solution)/shard_map/ppermute | solution.py:28
  22.9 0.0 collective-permute-start.11
  22.9 0.5 %collective-permute-start.10 = (bf16[128,512]{1,0:T(8,128)(2,1)S(1)}, bf16[128,512]{1,0:T(8,128)(2,1)S(1)}, u32[]{:S(2)}, u32[]{:S(2)}) collective-permute-start(bf16[128,512]{1,0:T(8,128)(2,1)S(1)} %shard_map.68.refs_0_), channel_id=1, source_target_pairs={{0,1},{1,0},{2,3},{3,2},{4,5},{5,4},{6,7},{7,6},{8,9},{9,8},{10,11... | collective-permute-start | bytes 393224 | tf_op jit(solution)/shard_map/ppermute | solution.py:28
  23.4 2.1 %collective-permute-done.8.refs_2_ = bf16[128,512]{1,0:T(8,128)(2,1)S(1)} collective-permute-done((bf16[128,512]{1,0:T(8,128)(2,1)S(1)}, bf16[128,512]{1,0:T(8,128)(2,1)S(1)}, u32[]{:S(2)}, u32[]{:S(2)}) %collective-permute-start.8) | collective-permute-done | bytes 131104 | tf_op jit(solution)/shard_map/ppermute | solution.py:28
  25.5 0.0 collective-permute-start.12
  25.5 0.0 slice-done
  25.5 0.0 slice-done.1
  25.5 0.6 %shard_map.69.refs_1_.refs_5_ = f32[128,896]{1,0:T(8,128)S(1)} custom-call(bf16[128,512]{1,0:T(8,128)(2,1)S(1)} %shard_map.68.refs_0_, bf16[128,512]{1,0:T(8,128)(2,1)S(1)} %shard_map.67.refs_1_, bf16[128,512]{1,0:T(8,128)(2,1)S(1)} %collective-permute-done.8.refs_2_, bf16[2,2048,896]{2,1,0:T(8,128)(2,1)S(1)} %bitcast.1), custom_call_target="tpu_custom_call" | custom-call | flops 352321536 | bytes 2752512 | tf_op jit(solution)/shard_map/pallas_call | solution.py:41
  26.1 1.9 %collective-permute-done.7.refs_0_ = bf16[128,512]{1,0:T(8,128)(2,1)S(1)} collective-permute-done((bf16[128,512]{1,0:T(8,128)(2,1)S(1)}, bf16[128,512]{1,0:T(8,128)(2,1)S(1)}, u32[]{:S(2)}, u32[]{:S(2)}) %collective-permute-start.7) | collective-permute-done | bytes 131104 | tf_op jit(solution)/shard_map/ppermute | solution.py:28
  28.0 0.1 collective-permute-start.9
  28.1 0.0 collective-permute-done.11.refs_1_
  28.1 0.0 collective-permute-done.10.refs_0_
  28.1 0.0 collective-permute-done.12.refs_2_
  28.1 0.7 %shard_map.71.refs_2_ = f32[128,896]{1,0:T(8,128)S(1)} custom-call(bf16[128,512]{1,0:T(8,128)(2,1)S(1)} %collective-permute-done.10.refs_0_, bf16[128,512]{1,0:T(8,128)(2,1)S(1)} %collective-permute-done.11.refs_1_, bf16[128,512]{1,0:T(8,128)(2,1)S(1)} %collective-permute-done.12.refs_2_, bf16[128,512]{1,0:T(8,128)(2,1)S(1)} %shard_map.70.refs_3_, ...), custom_call_target="tpu_custom_call" | custom-call | flops 469762048 | bytes 3670016 | tf_op jit(solution)/shard_map/pallas_call | solution.py:41
  28.8 0.6 %collective-permute-done.9.refs_0_ = bf16[128,512]{1,0:T(8,128)(2,1)S(1)} collective-permute-done((bf16[128,512]{1,0:T(8,128)(2,1)S(1)}, bf16[128,512]{1,0:T(8,128)(2,1)S(1)}, u32[]{:S(2)}, u32[]{:S(2)}) %collective-permute-start.9) | collective-permute-done | bytes 131104 | tf_op jit(solution)/shard_map/ppermute | solution.py:28
  29.4 0.3 shard_map.72
  29.7 2.8 %collective-permute-start.13 = (bf16[32,896]{1,0:T(8,128)(2,1)S(1)}, bf16[32,896]{1,0:T(8,128)(2,1)S(1)}, u32[]{:S(2)}, u32[]{:S(2)}) collective-permute-start(bf16[32,896]{1,0:T(8,128)(2,1)S(1)} %get-tuple-element.17), channel_id=1, source_target_pairs={{0,12},{4,8},{8,4},{12,0},{1,13},{5,9},{9,5},{13,1},{2,14},{6,10},... | collective-permute-start | bytes 172040 | tf_op jit(solution)/shard_map/ppermute | solution.py:28
  32.5 0.6 %collective-permute-start.14 = (bf16[32,896]{1,0:T(8,128)(2,1)S(1)}, bf16[32,896]{1,0:T(8,128)(2,1)S(1)}, u32[]{:S(2)}, u32[]{:S(2)}) collective-permute-start(bf16[32,896]{1,0:T(8,128)(2,1)S(1)} %get-tuple-element.18), channel_id=1, source_target_pairs={{0,4},{4,0},{8,12},{12,8},{1,5},{5,1},{9,13},{13,9},{2,6},{6,2},{1... | collective-permute-start | bytes 172040 | tf_op jit(solution)/shard_map/ppermute | solution.py:28
  33.2 1.0 %collective-permute-start.15 = (bf16[32,896]{1,0:T(8,128)(2,1)S(1)}, bf16[32,896]{1,0:T(8,128)(2,1)S(1)}, u32[]{:S(2)}, u32[]{:S(2)}) collective-permute-start(bf16[32,896]{1,0:T(8,128)(2,1)S(1)} %get-tuple-element.19), channel_id=1, source_target_pairs={{0,8},{4,12},{8,0},{12,4},{1,9},{5,13},{9,1},{13,5},{2,10},{6,14},... | collective-permute-start | bytes 172040 | tf_op jit(solution)/shard_map/ppermute | solution.py:28
  34.2 2.0 %collective-permute-done.13.refs_0_ = bf16[32,896]{1,0:T(8,128)(2,1)S(1)} collective-permute-done((bf16[32,896]{1,0:T(8,128)(2,1)S(1)}, bf16[32,896]{1,0:T(8,128)(2,1)S(1)}, u32[]{:S(2)}, u32[]{:S(2)}) %collective-permute-start.13) | collective-permute-done | bytes 57376 | tf_op jit(solution)/shard_map/ppermute | solution.py:28
  36.2 1.3 %collective-permute-done.14.refs_1_ = bf16[32,896]{1,0:T(8,128)(2,1)S(1)} collective-permute-done((bf16[32,896]{1,0:T(8,128)(2,1)S(1)}, bf16[32,896]{1,0:T(8,128)(2,1)S(1)}, u32[]{:S(2)}, u32[]{:S(2)}) %collective-permute-start.14) | collective-permute-done | bytes 57376 | tf_op jit(solution)/shard_map/ppermute | solution.py:28
  37.5 0.8 %collective-permute-done.15.refs_2_ = bf16[32,896]{1,0:T(8,128)(2,1)S(1)} collective-permute-done((bf16[32,896]{1,0:T(8,128)(2,1)S(1)}, bf16[32,896]{1,0:T(8,128)(2,1)S(1)}, u32[]{:S(2)}, u32[]{:S(2)}) %collective-permute-start.15) | collective-permute-done | bytes 57376 | tf_op jit(solution)/shard_map/ppermute | solution.py:28
  38.4 0.1 collective-permute-start.16
  38.4 1.6 %collective-permute-start.17 = (bf16[8,896]{1,0:T(8,128)(2,1)S(1)}, bf16[8,896]{1,0:T(8,128)(2,1)S(1)}, u32[]{:S(2)}, u32[]{:S(2)}) collective-permute-start(bf16[8,896]{1,0:T(8,128)(2,1)S(1)} %get-tuple-element.23), channel_id=1, source_target_pairs={{0,2},{2,0},{1,3},{3,1},{4,6},{6,4},{5,7},{7,5},{8,10},{10,8},{9,1... | collective-permute-start | bytes 43016 | tf_op jit(solution)/shard_map/ppermute | solution.py:28
  40.0 0.3 collective-permute-start.18
  40.3 1.4 %collective-permute-done.16.refs_1_ = bf16[8,896]{1,0:T(8,128)(2,1)S(1)} collective-permute-done((bf16[8,896]{1,0:T(8,128)(2,1)S(1)}, bf16[8,896]{1,0:T(8,128)(2,1)S(1)}, u32[]{:S(2)}, u32[]{:S(2)}) %collective-permute-start.16) | collective-permute-done | bytes 14368 | tf_op jit(solution)/shard_map/ppermute | solution.py:28
  41.7 0.5 %collective-permute-done.17.refs_2_ = bf16[8,896]{1,0:T(8,128)(2,1)S(1)} collective-permute-done((bf16[8,896]{1,0:T(8,128)(2,1)S(1)}, bf16[8,896]{1,0:T(8,128)(2,1)S(1)}, u32[]{:S(2)}, u32[]{:S(2)}) %collective-permute-start.17) | collective-permute-done | bytes 14368 | tf_op jit(solution)/shard_map/ppermute | solution.py:28
  42.2 0.0 collective-permute-done.18.refs_3_
  42.2 0.6 %shard_map.74 = bf16[8,3584]{1,0:T(8,128)(2,1)} custom-call(bf16[8,896]{1,0:T(8,128)(2,1)S(1)} %get-tuple-element.21.refs_0_, bf16[8,896]{1,0:T(8,128)(2,1)S(1)} %collective-permute-done.16.refs_1_, bf16[8,896]{1,0:T(8,128)(2,1)S(1)} %collective-permute-done.17.refs_2_, bf16[8,896]{1,0:T(8,128)(2,1)S(1)} %collective-permute-done.18.refs_3_), custom_call_target="tpu_custom_call" | custom-call | tf_op jit(solution)/shard_map/pallas_call | solution.py:41
  (5 shorter events, 0.1 us)
Async XLA Ops:
  0.9 7.2 %collective-permute-start.3 = (bf16[8,3712]{1,0:T(8,128)(2,1)S(1)}, bf16[8,3712]{1,0:T(8,128)(2,1)S(1)}, u32[]{:S(2)}, u32[]{:S(2)}) collective-permute-start(bf16[8,3712]{1,0:T(8,128)(2,1)S(1)} %shard_map.64.refs_4_), channel_id=1, source_target_pairs={{0,8},{4,12},{8,0},{12,4},{1,9},{5,13},{9,1},{13,5},{2,10},{6,14},... | collective-permute-start | bytes 178184 | tf_op jit(solution)/shard_map/ppermute | solution.py:28
  5.0 6.1 %collective-permute-start.2 = (bf16[8,3712]{1,0:T(8,128)(2,1)S(1)}, bf16[8,3712]{1,0:T(8,128)(2,1)S(1)}, u32[]{:S(2)}, u32[]{:S(2)}) collective-permute-start(bf16[8,3712]{1,0:T(8,128)(2,1)S(1)} %shard_map.64.refs_4_), channel_id=1, source_target_pairs={{0,12},{4,8},{8,4},{12,0},{1,13},{5,9},{9,5},{13,1},{2,14},{6,10},... | collective-permute-start | bytes 178184 | tf_op jit(solution)/shard_map/ppermute | solution.py:28
  6.4 4.8 %collective-permute-start.1 = (bf16[8,3712]{1,0:T(8,128)(2,1)S(1)}, bf16[8,3712]{1,0:T(8,128)(2,1)S(1)}, u32[]{:S(2)}, u32[]{:S(2)}) collective-permute-start(bf16[8,3712]{1,0:T(8,128)(2,1)S(1)} %shard_map.64.refs_4_), channel_id=1, source_target_pairs={{0,4},{4,0},{8,12},{12,8},{1,5},{5,1},{9,13},{13,9},{2,6},{6,2},{1... | collective-permute-start | bytes 178184 | tf_op jit(solution)/shard_map/ppermute | solution.py:28
  6.6 4.6 %collective-permute-start = (bf16[8,3712]{1,0:T(8,128)(2,1)S(1)}, bf16[8,3712]{1,0:T(8,128)(2,1)S(1)}, u32[]{:S(2)}, u32[]{:S(2)}) collective-permute-start(bf16[8,3712]{1,0:T(8,128)(2,1)S(1)} %shard_map.64.refs_4_), channel_id=1, source_target_pairs={{0,2},{2,0},{1,3},{3,1},{4,6},{6,4},{5,7},{7,5},{8,10},{10,8},{9,1... | collective-permute-start | bytes 178184 | tf_op jit(solution)/shard_map/ppermute | solution.py:28
  11.2 7.2 %copy-start.1 = (bf16[2,3584,512]{2,1,0:T(8,128)(2,1)S(1)}, bf16[2,3584,512]{2,1,0:T(8,128)(2,1)}, u32[]{:S(2)}) copy-start(bf16[2,3584,512]{2,1,0:T(8,128)(2,1)} %refs_5_.5) | copy-start | bytes 22020100
  11.3 7.1 %copy-start = (bf16[2,3584,512]{2,1,0:T(8,128)(2,1)S(1)}, bf16[2,3584,512]{2,1,0:T(8,128)(2,1)}, u32[]{:S(2)}) copy-start(bf16[2,3584,512]{2,1,0:T(8,128)(2,1)} %refs_4_.4) | copy-start | bytes 22020100
  11.3 5.5 %collective-permute-start.4 = (bf16[24,3712]{1,0:T(8,128)(2,1)S(1)}, bf16[24,3712]{1,0:T(8,128)(2,1)S(1)}, u32[]{:S(2)}, u32[]{:S(2)}) collective-permute-start(bf16[24,3712]{1,0:T(8,128)(2,1)S(1)} %get-tuple-element.16), channel_id=1, source_target_pairs={{0,2},{2,0},{1,3},{3,1},{4,6},{6,4},{5,7},{7,5},{8,10},{10,8},{9,1... | collective-permute-start | bytes 534536 | tf_op jit(solution)/shard_map/ppermute | solution.py:28
  12.8 4.1 %collective-permute-start.5 = (bf16[32,3712]{1,0:T(8,128)(2,1)S(1)}, bf16[32,3712]{1,0:T(8,128)(2,1)S(1)}, u32[]{:S(2)}, u32[]{:S(2)}) collective-permute-start(bf16[32,3712]{1,0:T(8,128)(2,1)S(1)} %get-tuple-element.15.refs_0_), channel_id=1, source_target_pairs={{0,1},{1,0},{2,3},{3,2},{4,5},{5,4},{6,7},{7,6},{8,9},{9,8},{10,11... | collective-permute-start | bytes 712712 | tf_op jit(solution)/shard_map/ppermute | solution.py:28
  16.8 1.6 %collective-permute-start.6 = (bf16[32,3712]{1,0:T(8,128)(2,1)S(1)}, bf16[32,3712]{1,0:T(8,128)(2,1)S(1)}, u32[]{:S(2)}, u32[]{:S(2)}) collective-permute-start(bf16[32,3712]{1,0:T(8,128)(2,1)S(1)} %shard_map.66.refs_1_), channel_id=1, source_target_pairs={{0,1},{1,0},{2,3},{3,2},{4,5},{5,4},{6,7},{7,6},{8,9},{9,8},{10,11... | collective-permute-start | bytes 712712 | tf_op jit(solution)/shard_map/ppermute | solution.py:28
  18.4 7.1 %slice-start = ((s8[7340032]{0:T(1024)(128)(4,1)}), s8[4194304]{0:T(1024)(128)(4,1)S(1)}, s32[]{:S(2)}) async-start(s8[7340032]{0:T(1024)(128)(4,1)} %bitcast), calls=%async_computation | async-start | bytes 8388608
  19.5 6.0 %slice-start.1 = ((s8[7340032]{0:T(1024)(128)(4,1)}), s8[3145728]{0:T(1024)(128)(4,1)S(1)}, s32[]{:S(2)}) async-start(s8[7340032]{0:T(1024)(128)(4,1)} %bitcast), calls=%async_computation.1 | async-start | bytes 6291456
  19.6 5.9 %collective-permute-start.8 = (bf16[128,512]{1,0:T(8,128)(2,1)S(1)}, bf16[128,512]{1,0:T(8,128)(2,1)S(1)}, u32[]{:S(2)}, u32[]{:S(2)}) collective-permute-start(bf16[128,512]{1,0:T(8,128)(2,1)S(1)} %shard_map.68.refs_0_), channel_id=1, source_target_pairs={{0,2},{2,0},{1,3},{3,1},{4,6},{6,4},{5,7},{7,5},{8,10},{10,8},{9,1... | collective-permute-start | bytes 393224 | tf_op jit(solution)/shard_map/ppermute | solution.py:28
  22.2 5.7 %collective-permute-start.7 = (bf16[128,512]{1,0:T(8,128)(2,1)S(1)}, bf16[128,512]{1,0:T(8,128)(2,1)S(1)}, u32[]{:S(2)}, u32[]{:S(2)}) collective-permute-start(bf16[128,512]{1,0:T(8,128)(2,1)S(1)} %shard_map.67.refs_1_), channel_id=1, source_target_pairs={{0,2},{2,0},{1,3},{3,1},{4,6},{6,4},{5,7},{7,5},{8,10},{10,8},{9,1... | collective-permute-start | bytes 393224 | tf_op jit(solution)/shard_map/ppermute | solution.py:28
  22.9 5.2 %collective-permute-start.11 = (bf16[128,512]{1,0:T(8,128)(2,1)S(1)}, bf16[128,512]{1,0:T(8,128)(2,1)S(1)}, u32[]{:S(2)}, u32[]{:S(2)}) collective-permute-start(bf16[128,512]{1,0:T(8,128)(2,1)S(1)} %shard_map.67.refs_1_), channel_id=1, source_target_pairs={{0,1},{1,0},{2,3},{3,2},{4,5},{5,4},{6,7},{7,6},{8,9},{9,8},{10,11... | collective-permute-start | bytes 393224 | tf_op jit(solution)/shard_map/ppermute | solution.py:28
  22.9 5.2 %collective-permute-start.10 = (bf16[128,512]{1,0:T(8,128)(2,1)S(1)}, bf16[128,512]{1,0:T(8,128)(2,1)S(1)}, u32[]{:S(2)}, u32[]{:S(2)}) collective-permute-start(bf16[128,512]{1,0:T(8,128)(2,1)S(1)} %shard_map.68.refs_0_), channel_id=1, source_target_pairs={{0,1},{1,0},{2,3},{3,2},{4,5},{5,4},{6,7},{7,6},{8,9},{9,8},{10,11... | collective-permute-start | bytes 393224 | tf_op jit(solution)/shard_map/ppermute | solution.py:28
  25.5 2.6 %collective-permute-start.12 = (bf16[128,512]{1,0:T(8,128)(2,1)S(1)}, bf16[128,512]{1,0:T(8,128)(2,1)S(1)}, u32[]{:S(2)}, u32[]{:S(2)}) collective-permute-start(bf16[128,512]{1,0:T(8,128)(2,1)S(1)} %collective-permute-done.8.refs_2_), channel_id=1, source_target_pairs={{0,1},{1,0},{2,3},{3,2},{4,5},{5,4},{6,7},{7,6},{8,9},{9,8},{10,11... | collective-permute-start | bytes 393224 | tf_op jit(solution)/shard_map/ppermute | solution.py:28
  28.0 1.4 %collective-permute-start.9 = (bf16[128,512]{1,0:T(8,128)(2,1)S(1)}, bf16[128,512]{1,0:T(8,128)(2,1)S(1)}, u32[]{:S(2)}, u32[]{:S(2)}) collective-permute-start(bf16[128,512]{1,0:T(8,128)(2,1)S(1)} %shard_map.70.refs_3_), channel_id=1, source_target_pairs={{0,1},{1,0},{2,3},{3,2},{4,5},{5,4},{6,7},{7,6},{8,9},{9,8},{10,11... | collective-permute-start | bytes 393224 | tf_op jit(solution)/shard_map/ppermute | solution.py:28
  29.7 6.5 %collective-permute-start.13 = (bf16[32,896]{1,0:T(8,128)(2,1)S(1)}, bf16[32,896]{1,0:T(8,128)(2,1)S(1)}, u32[]{:S(2)}, u32[]{:S(2)}) collective-permute-start(bf16[32,896]{1,0:T(8,128)(2,1)S(1)} %get-tuple-element.17), channel_id=1, source_target_pairs={{0,12},{4,8},{8,4},{12,0},{1,13},{5,9},{9,5},{13,1},{2,14},{6,10},... | collective-permute-start | bytes 172040 | tf_op jit(solution)/shard_map/ppermute | solution.py:28
  32.5 4.9 %collective-permute-start.14 = (bf16[32,896]{1,0:T(8,128)(2,1)S(1)}, bf16[32,896]{1,0:T(8,128)(2,1)S(1)}, u32[]{:S(2)}, u32[]{:S(2)}) collective-permute-start(bf16[32,896]{1,0:T(8,128)(2,1)S(1)} %get-tuple-element.18), channel_id=1, source_target_pairs={{0,4},{4,0},{8,12},{12,8},{1,5},{5,1},{9,13},{13,9},{2,6},{6,2},{1... | collective-permute-start | bytes 172040 | tf_op jit(solution)/shard_map/ppermute | solution.py:28
  33.2 5.2 %collective-permute-start.15 = (bf16[32,896]{1,0:T(8,128)(2,1)S(1)}, bf16[32,896]{1,0:T(8,128)(2,1)S(1)}, u32[]{:S(2)}, u32[]{:S(2)}) collective-permute-start(bf16[32,896]{1,0:T(8,128)(2,1)S(1)} %get-tuple-element.19), channel_id=1, source_target_pairs={{0,8},{4,12},{8,0},{12,4},{1,9},{5,13},{9,1},{13,5},{2,10},{6,14},... | collective-permute-start | bytes 172040 | tf_op jit(solution)/shard_map/ppermute | solution.py:28
  38.4 3.3 %collective-permute-start.16 = (bf16[8,896]{1,0:T(8,128)(2,1)S(1)}, bf16[8,896]{1,0:T(8,128)(2,1)S(1)}, u32[]{:S(2)}, u32[]{:S(2)}) collective-permute-start(bf16[8,896]{1,0:T(8,128)(2,1)S(1)} %get-tuple-element.22), channel_id=1, source_target_pairs={{0,3},{1,2},{2,1},{3,0},{4,7},{5,6},{6,5},{7,4},{8,11},{9,10},{10,... | collective-permute-start | bytes 43016 | tf_op jit(solution)/shard_map/ppermute | solution.py:28
  38.4 3.8 %collective-permute-start.17 = (bf16[8,896]{1,0:T(8,128)(2,1)S(1)}, bf16[8,896]{1,0:T(8,128)(2,1)S(1)}, u32[]{:S(2)}, u32[]{:S(2)}) collective-permute-start(bf16[8,896]{1,0:T(8,128)(2,1)S(1)} %get-tuple-element.23), channel_id=1, source_target_pairs={{0,2},{2,0},{1,3},{3,1},{4,6},{6,4},{5,7},{7,5},{8,10},{10,8},{9,1... | collective-permute-start | bytes 43016 | tf_op jit(solution)/shard_map/ppermute | solution.py:28
  40.0 2.2 %collective-permute-start.18 = (bf16[8,896]{1,0:T(8,128)(2,1)S(1)}, bf16[8,896]{1,0:T(8,128)(2,1)S(1)}, u32[]{:S(2)}, u32[]{:S(2)}) collective-permute-start(bf16[8,896]{1,0:T(8,128)(2,1)S(1)} %get-tuple-element.24), channel_id=1, source_target_pairs={{0,1},{1,0},{2,3},{3,2},{4,5},{5,4},{6,7},{7,6},{8,9},{9,8},{10,11... | collective-permute-start | bytes 43016 | tf_op jit(solution)/shard_map/ppermute | solution.py:28

commit v6 on v5

--- a/solution.py
+++ b/solution.py
@@ -215,6 +215,7 @@
         ],
         spec=HBM,
     )
+    CROSS = 1 if sub > 1 else 0
     early = [swap(packed, local=x) for x in range(1, local)]
     column = [packed] + [swap(packed, node=z) for z in range(1, nodes)]
     order = [4, 1, 3, 2, 0] if nodes == 4 and local == 2 else None
@@ -229,26 +230,34 @@
     for e in range(local_experts):
         h = hidden(blocks, gate_w, up_w, e, features)
         units.append(h)
-        crossed.append([swap(h, local=x) for x in range(1, local)])
+        crossed.append([swap(h, local=x, sub=CROSS) for x in range(1, local)])
 
     add = functools.partial(
         down, weights=down_w, tokens=count, local=local, sub=sub, nodes=nodes
     )
     last = local_experts - 1
+    def via(x):
+        return CROSS * local + x if x else 0
+
+    def term(array, at, e, r):
+        return (array, at, e, r)
+
     parts = [(units[e], 0, e, 0) for e in range(local_experts)]
-    parts += [(c, 0, e, x + 1) for e in range(last) for x, c in enumerate(crossed[e])]
+    parts += [(c, 0, e, via(x + 1)) for e in range(last) for x, c in enumerate(crossed[e])]
     total = add(parts, last=None, final=False)
     passed = [
-        (swap(array, sub=s), 0, e, s * local + x) for s in range(1, sub) for array, _, e, x in parts
+        (swap(array if r else stack([array], [total]), sub=s), 0, e, r ^ (s * local))
+        for s in range(1, sub)
+        for array, _, e, r in parts
     ]
     joined = stack(crossed[last], [total])
-    ends = [(joined, (x - 1) * count, last, x) for x in range(1, local)]
+    ends = [(joined, (x - 1) * count, last, via(x)) for x in range(1, local)]
     total = add(passed + ends, last=total, final=False)
     ends = [
-        (got, at, e, s * local + x)
+        (got, at, e, r ^ (s * local))
         for s in range(1, sub)
         for got in [swap(joined, sub=s)]
-        for _, at, e, x in ends
+        for _, at, e, r in ends
     ]
     sent = add(ends, last=total, final=True)
 

time: 43 us -> 43 us (level)
  starting transfers between devices: 17.9 us -> 18.6 us
  waiting for transfers between devices: 19.2 us -> 18.5 us
    ppermute x19, waiting for transfers between devices: 19.2 us -> 18.5 us  [swap(): return lax.ppermute(x, axes if len(axes) > 1 else axes[0], pairs)]
    ppermute x19, starting transfers between devices: 17.9 us -> 18.6 us  [swap(): return lax.ppermute(x, axes if len(axes) > 1 else axes[0], pairs)]
    pallas_call x11 -> x13, Pallas kernels: 5.54 us -> 5.58 us  [call(): pl.pallas_call(body, out_shape=out_shape, in_specs=[spec] * n + [HBM] * l...]
where the time goes in v6:
time: 43 us; the launch traced here: 42.8 us
  starting transfers between devices  18.6 us (43%)
  waiting for transfers between devices  18.5 us (43%)
  Pallas kernels  5.58 us (13%)
    ppermute x19, starting transfers between devices, swap(): return lax.ppermute(x, axes if len(axes) > 1 else axes[0], pairs)  18.6 us
    ppermute x19, waiting for transfers between devices, swap(): return lax.ppermute(x, axes if len(axes) > 1 else axes[0], pairs)  18.5 us
    pallas_call x13, Pallas kernels, call(): pl.pallas_call(body, out_shape=out_shape, in_specs=[spec] * n + [HBM] * l...  5.58 us
  transfers between devices with their start and end apart: 19, of which 12 were waited for; matrix products, arithmetic and copies ran while one was open for 0% of the time, Pallas kernels for 6%

profile of v6, /device:TPU:0, one launch (start us, length us, event | category | flops | bytes accessed | tf_op | source)
XLA Modules:
  0.0 42.8 jit_solution(12540851477125631574)
XLA Ops:
  0.0 0.9 %shard_map.64.refs_4_ = bf16[8,3712]{1,0:T(8,128)(2,1)S(1)} custom-call(bf16[8,3584]{1,0:T(8,128)(2,1)} %refs_0_.1, s32[8,8]{1,0:T(8,128)} %refs_1_.2, f32[8,8]{1,0:T(8,128)} %refs_2_.2), custom_call_target="tpu_custom_call" | custom-call | tf_op jit(solution)/shard_map/pallas_call | solution.py:41
  0.9 4.1 %collective-permute-start.3 = (bf16[8,3712]{1,0:T(8,128)(2,1)S(1)}, bf16[8,3712]{1,0:T(8,128)(2,1)S(1)}, u32[]{:S(2)}, u32[]{:S(2)}) collective-permute-start(bf16[8,3712]{1,0:T(8,128)(2,1)S(1)} %shard_map.64.refs_4_), channel_id=1, source_target_pairs={{0,8},{4,12},{8,0},{12,4},{1,9},{5,13},{9,1},{13,5},{2,10},{6,14},... | collective-permute-start | bytes 178184 | tf_op jit(solution)/shard_map/ppermute | solution.py:28
  5.0 1.3 %collective-permute-start.2 = (bf16[8,3712]{1,0:T(8,128)(2,1)S(1)}, bf16[8,3712]{1,0:T(8,128)(2,1)S(1)}, u32[]{:S(2)}, u32[]{:S(2)}) collective-permute-start(bf16[8,3712]{1,0:T(8,128)(2,1)S(1)} %shard_map.64.refs_4_), channel_id=1, source_target_pairs={{0,12},{4,8},{8,4},{12,0},{1,13},{5,9},{9,5},{13,1},{2,14},{6,10},... | collective-permute-start | bytes 178184 | tf_op jit(solution)/shard_map/ppermute | solution.py:28
  6.4 0.2 collective-permute-start.1
  6.6 1.5 %collective-permute-start = (bf16[8,3712]{1,0:T(8,128)(2,1)S(1)}, bf16[8,3712]{1,0:T(8,128)(2,1)S(1)}, u32[]{:S(2)}, u32[]{:S(2)}) collective-permute-start(bf16[8,3712]{1,0:T(8,128)(2,1)S(1)} %shard_map.64.refs_4_), channel_id=1, source_target_pairs={{0,2},{2,0},{1,3},{3,1},{4,6},{6,4},{5,7},{7,5},{8,10},{10,8},{9,1... | collective-permute-start | bytes 178184 | tf_op jit(solution)/shard_map/ppermute | solution.py:28
  8.1 0.0 collective-permute-done.3.refs_3_
  8.1 3.0 %collective-permute-done.2.refs_2_ = bf16[8,3712]{1,0:T(8,128)(2,1)S(1)} collective-permute-done((bf16[8,3712]{1,0:T(8,128)(2,1)S(1)}, bf16[8,3712]{1,0:T(8,128)(2,1)S(1)}, u32[]{:S(2)}, u32[]{:S(2)}) %collective-permute-start.2) | collective-permute-done | bytes 59424 | tf_op jit(solution)/shard_map/ppermute | solution.py:28
  11.2 0.1 collective-permute-done.1.refs_1_
  11.2 0.0 collective-permute-done.refs_0_
  11.2 0.0 copy-start.1
  11.3 0.0 copy-start
  11.3 1.6 %collective-permute-start.4 = (bf16[24,3712]{1,0:T(8,128)(2,1)S(1)}, bf16[24,3712]{1,0:T(8,128)(2,1)S(1)}, u32[]{:S(2)}, u32[]{:S(2)}) collective-permute-start(bf16[24,3712]{1,0:T(8,128)(2,1)S(1)} %get-tuple-element.16), channel_id=1, source_target_pairs={{0,2},{2,0},{1,3},{3,1},{4,6},{6,4},{5,7},{7,5},{8,10},{10,8},{9,1... | collective-permute-start | bytes 534536 | tf_op jit(solution)/shard_map/ppermute | solution.py:28
  12.8 0.0 collective-permute-start.5
  12.8 4.0 %collective-permute-done.4.refs_1_ = bf16[24,3712]{1,0:T(8,128)(2,1)S(1)} collective-permute-done((bf16[24,3712]{1,0:T(8,128)(2,1)S(1)}, bf16[24,3712]{1,0:T(8,128)(2,1)S(1)}, u32[]{:S(2)}, u32[]{:S(2)}) %collective-permute-start.4) | collective-permute-done | bytes 178208 | tf_op jit(solution)/shard_map/ppermute | solution.py:28
  16.8 0.1 collective-permute-start.6
  16.9 0.0 collective-permute-done.5.refs_2_
  16.9 1.5 %collective-permute-done.6.refs_3_ = bf16[32,3712]{1,0:T(8,128)(2,1)S(1)} collective-permute-done((bf16[32,3712]{1,0:T(8,128)(2,1)S(1)}, bf16[32,3712]{1,0:T(8,128)(2,1)S(1)}, u32[]{:S(2)}, u32[]{:S(2)}) %collective-permute-start.6) | collective-permute-done | bytes 237600 | tf_op jit(solution)/shard_map/ppermute | solution.py:28
  18.4 0.0 copy-done.1
  18.4 0.0 copy-done
  18.4 0.0 slice-start
  18.4 1.1 %shard_map.68.refs_0_ = bf16[128,512]{1,0:T(8,128)(2,1)S(1)} custom-call(bf16[32,3712]{1,0:T(8,128)(2,1)S(1)} %get-tuple-element.15.refs_0_, bf16[32,3712]{1,0:T(8,128)(2,1)S(1)} %shard_map.66.refs_1_, bf16[32,3712]{1,0:T(8,128)(2,1)S(1)} %collective-permute-done.5.refs_2_, bf16[32,3712]{1,0:T(8,128)(2,1)S(1)} %collective-permute-done.6.refs_3_, ...), custom_call_target="tpu_custom_call" | custom-call | flops 939524096 | bytes 7340032 | tf_op jit(solution)/shard_map/pallas_call | solution.py:41
  19.6 0.0 slice-start.1
  19.6 1.3 %collective-permute-start.8 = (bf16[128,512]{1,0:T(8,128)(2,1)S(1)}, bf16[128,512]{1,0:T(8,128)(2,1)S(1)}, u32[]{:S(2)}, u32[]{:S(2)}) collective-permute-start(bf16[128,512]{1,0:T(8,128)(2,1)S(1)} %shard_map.68.refs_0_), channel_id=1, source_target_pairs={{0,3},{1,2},{2,1},{3,0},{4,7},{5,6},{6,5},{7,4},{8,11},{9,10},{10,... | collective-permute-start | bytes 393224 | tf_op jit(solution)/shard_map/ppermute | solution.py:28
  20.9 1.1 %shard_map.67.refs_1_.refs_0_ = bf16[128,512]{1,0:T(8,128)(2,1)S(1)} custom-call(bf16[32,3712]{1,0:T(8,128)(2,1)S(1)} %get-tuple-element.15.refs_0_, bf16[32,3712]{1,0:T(8,128)(2,1)S(1)} %shard_map.66.refs_1_, bf16[32,3712]{1,0:T(8,128)(2,1)S(1)} %collective-permute-done.5.refs_2_, bf16[32,3712]{1,0:T(8,128)(2,1)S(1)} %collective-permute-done.6.refs_3_, ...), custom_call_target="tpu_custom_call" | custom-call | flops 939524096 | bytes 7340032 | tf_op jit(solution)/shard_map/pallas_call | solution.py:41
  22.0 0.6 %collective-permute-start.7 = (bf16[128,512]{1,0:T(8,128)(2,1)S(1)}, bf16[128,512]{1,0:T(8,128)(2,1)S(1)}, u32[]{:S(2)}, u32[]{:S(2)}) collective-permute-start(bf16[128,512]{1,0:T(8,128)(2,1)S(1)} %shard_map.67.refs_1_.refs_0_), channel_id=1, source_target_pairs={{0,3},{1,2},{2,1},{3,0},{4,7},{5,6},{6,5},{7,4},{8,11},{9,10},{10,... | collective-permute-start | bytes 393224 | tf_op jit(solution)/shard_map/ppermute | solution.py:28
  22.6 2.5 %collective-permute-done.8.refs_2_ = bf16[128,512]{1,0:T(8,128)(2,1)S(1)} collective-permute-done((bf16[128,512]{1,0:T(8,128)(2,1)S(1)}, bf16[128,512]{1,0:T(8,128)(2,1)S(1)}, u32[]{:S(2)}, u32[]{:S(2)}) %collective-permute-start.8) | collective-permute-done | bytes 131104 | tf_op jit(solution)/shard_map/ppermute | solution.py:28
  25.1 0.0 slice-done
  25.1 0.0 slice-done.1
  25.1 0.6 %shard_map.69.refs_1_.refs_5_ = f32[128,896]{1,0:T(8,128)S(1)} custom-call(bf16[128,512]{1,0:T(8,128)(2,1)S(1)} %shard_map.68.refs_0_, bf16[128,512]{1,0:T(8,128)(2,1)S(1)} %shard_map.67.refs_1_.refs_0_, bf16[128,512]{1,0:T(8,128)(2,1)S(1)} %collective-permute-done.8.refs_2_, bf16[2,2048,896]{2,1,0:T(8,128)(2,1)S(1)} %bitcast.1), custom_call_target="tpu_custom_call" | custom-call | flops 352321536 | bytes 2752512 | tf_op jit(solution)/shard_map/pallas_call | solution.py:41
  25.8 0.8 %collective-permute-start.12 = (bf16[128,512]{1,0:T(8,128)(2,1)S(1)}, bf16[128,512]{1,0:T(8,128)(2,1)S(1)}, u32[]{:S(2)}, u32[]{:S(2)}) collective-permute-start(bf16[128,512]{1,0:T(8,128)(2,1)S(1)} %collective-permute-done.8.refs_2_), channel_id=1, source_target_pairs={{0,1},{1,0},{2,3},{3,2},{4,5},{5,4},{6,7},{7,6},{8,9},{9,8},{10,11... | collective-permute-start | bytes 393224 | tf_op jit(solution)/shard_map/ppermute | solution.py:28
  26.6 0.1 collective-permute-start.10
  26.6 0.4 %collective-permute-start.11 = (bf16[128,512]{1,0:T(8,128)(2,1)S(1)}, bf16[128,512]{1,0:T(8,128)(2,1)S(1)}, u32[]{:S(2)}, u32[]{:S(2)}) collective-permute-start(bf16[128,512]{1,0:T(8,128)(2,1)S(1)} %shard_map.72), channel_id=1, source_target_pairs={{0,1},{1,0},{2,3},{3,2},{4,5},{5,4},{6,7},{7,6},{8,9},{9,8},{10,11... | collective-permute-start | bytes 393224 | tf_op jit(solution)/shard_map/ppermute | solution.py:28
  27.1 0.8 %collective-permute-done.7.refs_0_ = bf16[128,512]{1,0:T(8,128)(2,1)S(1)} collective-permute-done((bf16[128,512]{1,0:T(8,128)(2,1)S(1)}, bf16[128,512]{1,0:T(8,128)(2,1)S(1)}, u32[]{:S(2)}, u32[]{:S(2)}) %collective-permute-start.7) | collective-permute-done | bytes 131104 | tf_op jit(solution)/shard_map/ppermute | solution.py:28
  27.9 0.2 collective-permute-start.9
  28.1 0.0 collective-permute-done.12.refs_2_
  28.1 0.0 collective-permute-done.10.refs_0_
  28.1 0.0 collective-permute-done.11.refs_1_
  28.1 0.7 %shard_map.73.refs_2_ = f32[128,896]{1,0:T(8,128)S(1)} custom-call(bf16[128,512]{1,0:T(8,128)(2,1)S(1)} %collective-permute-done.10.refs_0_, bf16[128,512]{1,0:T(8,128)(2,1)S(1)} %collective-permute-done.11.refs_1_, bf16[128,512]{1,0:T(8,128)(2,1)S(1)} %collective-permute-done.12.refs_2_, bf16[128,512]{1,0:T(8,128)(2,1)S(1)} %shard_map.70.refs_3_, ...), custom_call_target="tpu_custom_call" | custom-call | flops 469762048 | bytes 3670016 | tf_op jit(solution)/shard_map/pallas_call | solution.py:41
  28.9 0.5 %collective-permute-done.9.refs_0_ = bf16[128,512]{1,0:T(8,128)(2,1)S(1)} collective-permute-done((bf16[128,512]{1,0:T(8,128)(2,1)S(1)}, bf16[128,512]{1,0:T(8,128)(2,1)S(1)}, u32[]{:S(2)}, u32[]{:S(2)}) %collective-permute-start.9) | collective-permute-done | bytes 131104 | tf_op jit(solution)/shard_map/ppermute | solution.py:28
  29.3 0.3 shard_map.74
  29.7 2.8 %collective-permute-start.13 = (bf16[32,896]{1,0:T(8,128)(2,1)S(1)}, bf16[32,896]{1,0:T(8,128)(2,1)S(1)}, u32[]{:S(2)}, u32[]{:S(2)}) collective-permute-start(bf16[32,896]{1,0:T(8,128)(2,1)S(1)} %get-tuple-element.17), channel_id=1, source_target_pairs={{0,12},{4,8},{8,4},{12,0},{1,13},{5,9},{9,5},{13,1},{2,14},{6,10},... | collective-permute-start | bytes 172040 | tf_op jit(solution)/shard_map/ppermute | solution.py:28
  32.5 0.6 %collective-permute-start.14 = (bf16[32,896]{1,0:T(8,128)(2,1)S(1)}, bf16[32,896]{1,0:T(8,128)(2,1)S(1)}, u32[]{:S(2)}, u32[]{:S(2)}) collective-permute-start(bf16[32,896]{1,0:T(8,128)(2,1)S(1)} %get-tuple-element.18), channel_id=1, source_target_pairs={{0,4},{4,0},{8,12},{12,8},{1,5},{5,1},{9,13},{13,9},{2,6},{6,2},{1... | collective-permute-start | bytes 172040 | tf_op jit(solution)/shard_map/ppermute | solution.py:28
  33.1 1.0 %collective-permute-start.15 = (bf16[32,896]{1,0:T(8,128)(2,1)S(1)}, bf16[32,896]{1,0:T(8,128)(2,1)S(1)}, u32[]{:S(2)}, u32[]{:S(2)}) collective-permute-start(bf16[32,896]{1,0:T(8,128)(2,1)S(1)} %get-tuple-element.19), channel_id=1, source_target_pairs={{0,8},{4,12},{8,0},{12,4},{1,9},{5,13},{9,1},{13,5},{2,10},{6,14},... | collective-permute-start | bytes 172040 | tf_op jit(solution)/shard_map/ppermute | solution.py:28
  34.1 2.0 %collective-permute-done.13.refs_0_ = bf16[32,896]{1,0:T(8,128)(2,1)S(1)} collective-permute-done((bf16[32,896]{1,0:T(8,128)(2,1)S(1)}, bf16[32,896]{1,0:T(8,128)(2,1)S(1)}, u32[]{:S(2)}, u32[]{:S(2)}) %collective-permute-start.13) | collective-permute-done | bytes 57376 | tf_op jit(solution)/shard_map/ppermute | solution.py:28
  36.1 1.3 %collective-permute-done.14.refs_1_ = bf16[32,896]{1,0:T(8,128)(2,1)S(1)} collective-permute-done((bf16[32,896]{1,0:T(8,128)(2,1)S(1)}, bf16[32,896]{1,0:T(8,128)(2,1)S(1)}, u32[]{:S(2)}, u32[]{:S(2)}) %collective-permute-start.14) | collective-permute-done | bytes 57376 | tf_op jit(solution)/shard_map/ppermute | solution.py:28
  37.4 0.8 %collective-permute-done.15.refs_2_ = bf16[32,896]{1,0:T(8,128)(2,1)S(1)} collective-permute-done((bf16[32,896]{1,0:T(8,128)(2,1)S(1)}, bf16[32,896]{1,0:T(8,128)(2,1)S(1)}, u32[]{:S(2)}, u32[]{:S(2)}) %collective-permute-start.15) | collective-permute-done | bytes 57376 | tf_op jit(solution)/shard_map/ppermute | solution.py:28
  38.3 0.1 collective-permute-start.16
  38.4 1.6 %collective-permute-start.17 = (bf16[8,896]{1,0:T(8,128)(2,1)S(1)}, bf16[8,896]{1,0:T(8,128)(2,1)S(1)}, u32[]{:S(2)}, u32[]{:S(2)}) collective-permute-start(bf16[8,896]{1,0:T(8,128)(2,1)S(1)} %get-tuple-element.23), channel_id=1, source_target_pairs={{0,2},{2,0},{1,3},{3,1},{4,6},{6,4},{5,7},{7,5},{8,10},{10,8},{9,1... | collective-permute-start | bytes 43016 | tf_op jit(solution)/shard_map/ppermute | solution.py:28
  39.9 0.3 collective-permute-start.18
  40.2 1.4 %collective-permute-done.16.refs_1_ = bf16[8,896]{1,0:T(8,128)(2,1)S(1)} collective-permute-done((bf16[8,896]{1,0:T(8,128)(2,1)S(1)}, bf16[8,896]{1,0:T(8,128)(2,1)S(1)}, u32[]{:S(2)}, u32[]{:S(2)}) %collective-permute-start.16) | collective-permute-done | bytes 14368 | tf_op jit(solution)/shard_map/ppermute | solution.py:28
  41.6 0.5 %collective-permute-done.17.refs_2_ = bf16[8,896]{1,0:T(8,128)(2,1)S(1)} collective-permute-done((bf16[8,896]{1,0:T(8,128)(2,1)S(1)}, bf16[8,896]{1,0:T(8,128)(2,1)S(1)}, u32[]{:S(2)}, u32[]{:S(2)}) %collective-permute-start.17) | collective-permute-done | bytes 14368 | tf_op jit(solution)/shard_map/ppermute | solution.py:28
  42.2 0.0 collective-permute-done.18.refs_3_
  42.2 0.6 %shard_map.76 = bf16[8,3584]{1,0:T(8,128)(2,1)} custom-call(bf16[8,896]{1,0:T(8,128)(2,1)S(1)} %get-tuple-element.21.refs_0_, bf16[8,896]{1,0:T(8,128)(2,1)S(1)} %collective-permute-done.16.refs_1_, bf16[8,896]{1,0:T(8,128)(2,1)S(1)} %collective-permute-done.17.refs_2_, bf16[8,896]{1,0:T(8,128)(2,1)S(1)} %collective-permute-done.18.refs_3_), custom_call_target="tpu_custom_call" | custom-call | tf_op jit(solution)/shard_map/pallas_call | solution.py:41
  (7 shorter events, 0.1 us)
Async XLA Ops:
  0.9 7.2 %collective-permute-start.3 = (bf16[8,3712]{1,0:T(8,128)(2,1)S(1)}, bf16[8,3712]{1,0:T(8,128)(2,1)S(1)}, u32[]{:S(2)}, u32[]{:S(2)}) collective-permute-start(bf16[8,3712]{1,0:T(8,128)(2,1)S(1)} %shard_map.64.refs_4_), channel_id=1, source_target_pairs={{0,8},{4,12},{8,0},{12,4},{1,9},{5,13},{9,1},{13,5},{2,10},{6,14},... | collective-permute-start | bytes 178184 | tf_op jit(solution)/shard_map/ppermute | solution.py:28
  5.0 6.1 %collective-permute-start.2 = (bf16[8,3712]{1,0:T(8,128)(2,1)S(1)}, bf16[8,3712]{1,0:T(8,128)(2,1)S(1)}, u32[]{:S(2)}, u32[]{:S(2)}) collective-permute-start(bf16[8,3712]{1,0:T(8,128)(2,1)S(1)} %shard_map.64.refs_4_), channel_id=1, source_target_pairs={{0,12},{4,8},{8,4},{12,0},{1,13},{5,9},{9,5},{13,1},{2,14},{6,10},... | collective-permute-start | bytes 178184 | tf_op jit(solution)/shard_map/ppermute | solution.py:28
  6.4 4.8 %collective-permute-start.1 = (bf16[8,3712]{1,0:T(8,128)(2,1)S(1)}, bf16[8,3712]{1,0:T(8,128)(2,1)S(1)}, u32[]{:S(2)}, u32[]{:S(2)}) collective-permute-start(bf16[8,3712]{1,0:T(8,128)(2,1)S(1)} %shard_map.64.refs_4_), channel_id=1, source_target_pairs={{0,4},{4,0},{8,12},{12,8},{1,5},{5,1},{9,13},{13,9},{2,6},{6,2},{1... | collective-permute-start | bytes 178184 | tf_op jit(solution)/shard_map/ppermute | solution.py:28
  6.6 4.6 %collective-permute-start = (bf16[8,3712]{1,0:T(8,128)(2,1)S(1)}, bf16[8,3712]{1,0:T(8,128)(2,1)S(1)}, u32[]{:S(2)}, u32[]{:S(2)}) collective-permute-start(bf16[8,3712]{1,0:T(8,128)(2,1)S(1)} %shard_map.64.refs_4_), channel_id=1, source_target_pairs={{0,2},{2,0},{1,3},{3,1},{4,6},{6,4},{5,7},{7,5},{8,10},{10,8},{9,1... | collective-permute-start | bytes 178184 | tf_op jit(solution)/shard_map/ppermute | solution.py:28
  11.2 7.2 %copy-start.1 = (bf16[2,3584,512]{2,1,0:T(8,128)(2,1)S(1)}, bf16[2,3584,512]{2,1,0:T(8,128)(2,1)}, u32[]{:S(2)}) copy-start(bf16[2,3584,512]{2,1,0:T(8,128)(2,1)} %refs_5_.5) | copy-start | bytes 22020100
  11.3 7.1 %copy-start = (bf16[2,3584,512]{2,1,0:T(8,128)(2,1)S(1)}, bf16[2,3584,512]{2,1,0:T(8,128)(2,1)}, u32[]{:S(2)}) copy-start(bf16[2,3584,512]{2,1,0:T(8,128)(2,1)} %refs_4_.4) | copy-start | bytes 22020100
  11.3 5.5 %collective-permute-start.4 = (bf16[24,3712]{1,0:T(8,128)(2,1)S(1)}, bf16[24,3712]{1,0:T(8,128)(2,1)S(1)}, u32[]{:S(2)}, u32[]{:S(2)}) collective-permute-start(bf16[24,3712]{1,0:T(8,128)(2,1)S(1)} %get-tuple-element.16), channel_id=1, source_target_pairs={{0,2},{2,0},{1,3},{3,1},{4,6},{6,4},{5,7},{7,5},{8,10},{10,8},{9,1... | collective-permute-start | bytes 534536 | tf_op jit(solution)/shard_map/ppermute | solution.py:28
  12.8 4.1 %collective-permute-start.5 = (bf16[32,3712]{1,0:T(8,128)(2,1)S(1)}, bf16[32,3712]{1,0:T(8,128)(2,1)S(1)}, u32[]{:S(2)}, u32[]{:S(2)}) collective-permute-start(bf16[32,3712]{1,0:T(8,128)(2,1)S(1)} %get-tuple-element.15.refs_0_), channel_id=1, source_target_pairs={{0,1},{1,0},{2,3},{3,2},{4,5},{5,4},{6,7},{7,6},{8,9},{9,8},{10,11... | collective-permute-start | bytes 712712 | tf_op jit(solution)/shard_map/ppermute | solution.py:28
  16.8 1.6 %collective-permute-start.6 = (bf16[32,3712]{1,0:T(8,128)(2,1)S(1)}, bf16[32,3712]{1,0:T(8,128)(2,1)S(1)}, u32[]{:S(2)}, u32[]{:S(2)}) collective-permute-start(bf16[32,3712]{1,0:T(8,128)(2,1)S(1)} %shard_map.66.refs_1_), channel_id=1, source_target_pairs={{0,1},{1,0},{2,3},{3,2},{4,5},{5,4},{6,7},{7,6},{8,9},{9,8},{10,11... | collective-permute-start | bytes 712712 | tf_op jit(solution)/shard_map/ppermute | solution.py:28
  18.4 6.7 %slice-start = ((s8[7340032]{0:T(1024)(128)(4,1)}), s8[4194304]{0:T(1024)(128)(4,1)S(1)}, s32[]{:S(2)}) async-start(s8[7340032]{0:T(1024)(128)(4,1)} %bitcast), calls=%async_computation | async-start | bytes 8388608
  19.6 5.6 %slice-start.1 = ((s8[7340032]{0:T(1024)(128)(4,1)}), s8[3145728]{0:T(1024)(128)(4,1)S(1)}, s32[]{:S(2)}) async-start(s8[7340032]{0:T(1024)(128)(4,1)} %bitcast), calls=%async_computation.1 | async-start | bytes 6291456
  19.6 5.5 %collective-permute-start.8 = (bf16[128,512]{1,0:T(8,128)(2,1)S(1)}, bf16[128,512]{1,0:T(8,128)(2,1)S(1)}, u32[]{:S(2)}, u32[]{:S(2)}) collective-permute-start(bf16[128,512]{1,0:T(8,128)(2,1)S(1)} %shard_map.68.refs_0_), channel_id=1, source_target_pairs={{0,3},{1,2},{2,1},{3,0},{4,7},{5,6},{6,5},{7,4},{8,11},{9,10},{10,... | collective-permute-start | bytes 393224 | tf_op jit(solution)/shard_map/ppermute | solution.py:28
  22.0 5.9 %collective-permute-start.7 = (bf16[128,512]{1,0:T(8,128)(2,1)S(1)}, bf16[128,512]{1,0:T(8,128)(2,1)S(1)}, u32[]{:S(2)}, u32[]{:S(2)}) collective-permute-start(bf16[128,512]{1,0:T(8,128)(2,1)S(1)} %shard_map.67.refs_1_.refs_0_), channel_id=1, source_target_pairs={{0,3},{1,2},{2,1},{3,0},{4,7},{5,6},{6,5},{7,4},{8,11},{9,10},{10,... | collective-permute-start | bytes 393224 | tf_op jit(solution)/shard_map/ppermute | solution.py:28
  25.8 2.4 %collective-permute-start.12 = (bf16[128,512]{1,0:T(8,128)(2,1)S(1)}, bf16[128,512]{1,0:T(8,128)(2,1)S(1)}, u32[]{:S(2)}, u32[]{:S(2)}) collective-permute-start(bf16[128,512]{1,0:T(8,128)(2,1)S(1)} %collective-permute-done.8.refs_2_), channel_id=1, source_target_pairs={{0,1},{1,0},{2,3},{3,2},{4,5},{5,4},{6,7},{7,6},{8,9},{9,8},{10,11... | collective-permute-start | bytes 393224 | tf_op jit(solution)/shard_map/ppermute | solution.py:28
  26.6 1.6 %collective-permute-start.10 = (bf16[128,512]{1,0:T(8,128)(2,1)S(1)}, bf16[128,512]{1,0:T(8,128)(2,1)S(1)}, u32[]{:S(2)}, u32[]{:S(2)}) collective-permute-start(bf16[128,512]{1,0:T(8,128)(2,1)S(1)} %shard_map.71), channel_id=1, source_target_pairs={{0,1},{1,0},{2,3},{3,2},{4,5},{5,4},{6,7},{7,6},{8,9},{9,8},{10,11... | collective-permute-start | bytes 393224 | tf_op jit(solution)/shard_map/ppermute | solution.py:28
  26.6 1.5 %collective-permute-start.11 = (bf16[128,512]{1,0:T(8,128)(2,1)S(1)}, bf16[128,512]{1,0:T(8,128)(2,1)S(1)}, u32[]{:S(2)}, u32[]{:S(2)}) collective-permute-start(bf16[128,512]{1,0:T(8,128)(2,1)S(1)} %shard_map.72), channel_id=1, source_target_pairs={{0,1},{1,0},{2,3},{3,2},{4,5},{5,4},{6,7},{7,6},{8,9},{9,8},{10,11... | collective-permute-start | bytes 393224 | tf_op jit(solution)/shard_map/ppermute | solution.py:28
  27.9 1.4 %collective-permute-start.9 = (bf16[128,512]{1,0:T(8,128)(2,1)S(1)}, bf16[128,512]{1,0:T(8,128)(2,1)S(1)}, u32[]{:S(2)}, u32[]{:S(2)}) collective-permute-start(bf16[128,512]{1,0:T(8,128)(2,1)S(1)} %shard_map.70.refs_3_), channel_id=1, source_target_pairs={{0,1},{1,0},{2,3},{3,2},{4,5},{5,4},{6,7},{7,6},{8,9},{9,8},{10,11... | collective-permute-start | bytes 393224 | tf_op jit(solution)/shard_map/ppermute | solution.py:28
  29.7 6.5 %collective-permute-start.13 = (bf16[32,896]{1,0:T(8,128)(2,1)S(1)}, bf16[32,896]{1,0:T(8,128)(2,1)S(1)}, u32[]{:S(2)}, u32[]{:S(2)}) collective-permute-start(bf16[32,896]{1,0:T(8,128)(2,1)S(1)} %get-tuple-element.17), channel_id=1, source_target_pairs={{0,12},{4,8},{8,4},{12,0},{1,13},{5,9},{9,5},{13,1},{2,14},{6,10},... | collective-permute-start | bytes 172040 | tf_op jit(solution)/shard_map/ppermute | solution.py:28
  32.5 4.9 %collective-permute-start.14 = (bf16[32,896]{1,0:T(8,128)(2,1)S(1)}, bf16[32,896]{1,0:T(8,128)(2,1)S(1)}, u32[]{:S(2)}, u32[]{:S(2)}) collective-permute-start(bf16[32,896]{1,0:T(8,128)(2,1)S(1)} %get-tuple-element.18), channel_id=1, source_target_pairs={{0,4},{4,0},{8,12},{12,8},{1,5},{5,1},{9,13},{13,9},{2,6},{6,2},{1... | collective-permute-start | bytes 172040 | tf_op jit(solution)/shard_map/ppermute | solution.py:28
  33.1 5.1 %collective-permute-start.15 = (bf16[32,896]{1,0:T(8,128)(2,1)S(1)}, bf16[32,896]{1,0:T(8,128)(2,1)S(1)}, u32[]{:S(2)}, u32[]{:S(2)}) collective-permute-start(bf16[32,896]{1,0:T(8,128)(2,1)S(1)} %get-tuple-element.19), channel_id=1, source_target_pairs={{0,8},{4,12},{8,0},{12,4},{1,9},{5,13},{9,1},{13,5},{2,10},{6,14},... | collective-permute-start | bytes 172040 | tf_op jit(solution)/shard_map/ppermute | solution.py:28
  38.3 3.3 %collective-permute-start.16 = (bf16[8,896]{1,0:T(8,128)(2,1)S(1)}, bf16[8,896]{1,0:T(8,128)(2,1)S(1)}, u32[]{:S(2)}, u32[]{:S(2)}) collective-permute-start(bf16[8,896]{1,0:T(8,128)(2,1)S(1)} %get-tuple-element.22), channel_id=1, source_target_pairs={{0,3},{1,2},{2,1},{3,0},{4,7},{5,6},{6,5},{7,4},{8,11},{9,10},{10,... | collective-permute-start | bytes 43016 | tf_op jit(solution)/shard_map/ppermute | solution.py:28
  38.4 3.8 %collective-permute-start.17 = (bf16[8,896]{1,0:T(8,128)(2,1)S(1)}, bf16[8,896]{1,0:T(8,128)(2,1)S(1)}, u32[]{:S(2)}, u32[]{:S(2)}) collective-permute-start(bf16[8,896]{1,0:T(8,128)(2,1)S(1)} %get-tuple-element.23), channel_id=1, source_target_pairs={{0,2},{2,0},{1,3},{3,1},{4,6},{6,4},{5,7},{7,5},{8,10},{10,8},{9,1... | collective-permute-start | bytes 43016 | tf_op jit(solution)/shard_map/ppermute | solution.py:28
  39.9 2.2 %collective-permute-start.18 = (bf16[8,896]{1,0:T(8,128)(2,1)S(1)}, bf16[8,896]{1,0:T(8,128)(2,1)S(1)}, u32[]{:S(2)}, u32[]{:S(2)}) collective-permute-start(bf16[8,896]{1,0:T(8,128)(2,1)S(1)} %get-tuple-element.24), channel_id=1, source_target_pairs={{0,1},{1,0},{2,3},{3,2},{4,5},{5,4},{6,7},{7,6},{8,9},{9,8},{10,11... | collective-permute-start | bytes 43016 | tf_op jit(solution)/shard_map/ppermute | solution.py:28
